TPU v7x, 32 devices: a whole 2x2x4 slice. The times are simulated.
32 devices in a mesh: rep: 2 (over core), src: 8 (over z, x), tgt: 2 (over y).
Axes of the slice: x: 2, y: 2, z: 4, core: 2. Of those that a mesh axis runs over, the one named last changes fastest.
Arguments:
- src_feats: float32 [2, 256, 3200], P('rep', ('src', 'tgt')), may hold values from -6 to 6
- tgt_cotangent: float32 [2, 256, 3200], P('rep', ('tgt', 'src')), may hold values from -0.6 to 0.6
- rotation: float32 [2, 8, 2, 115, 384], P('rep', 'src', 'tgt'), may hold values from -3 to 3
- edge_src: int32 [2, 8, 2, 384], P('rep', 'src', 'tgt'), may hold values from 0 to 31
- edge_tgt: int32 [2, 8, 2, 384], P('rep', 'src', 'tgt'), may hold values from 0 to 127
- edge_count: int32 [2, 8, 2], P('rep', 'src', 'tgt'), may hold values from 192 to 384, as said below
- w_zero: float32 [640, 640], replicated, may hold values from -0.25 to 0.25
- w_one_re: float32 [512, 512], replicated, may hold values from -0.1875 to 0.1875
- w_one_im: float32 [512, 512], replicated, may hold values from -0.1875 to 0.1875
- w_two_re: float32 [384, 384], replicated, may hold values from -0.21875 to 0.21875
- w_two_im: float32 [384, 384], replicated, may hold values from -0.21875 to 0.21875
Outputs:
- grad_feats: float32 [2, 256, 3200], P('rep', ('src', 'tgt'))
- grad_w_zero: float32 [640, 640], P('src')
- grad_w_one_re: float32 [512, 512], P('src')
- grad_w_one_im: float32 [512, 512], P('src')
- grad_w_two_re: float32 [384, 384], P('src')
- grad_w_two_im: float32 [384, 384], P('src')
Inputs may be any that keep to these rules, and one draw needn't show every extreme that they name: `edge_count`: some tile of each structure is full.
All inputs are finite; a program needn't handle non-finite values.
Results may differ from a plain program's by a relative error of at most 0.0003.
Values sent between devices are 32-bit elements; how exact they have to be, the bound alone decides.
No kernel may reach another device: no remote copies, remote signals or barrier semaphores. Data moves between devices by JAX's collectives and lax.ppermute only.
A program may use at most 128 MiB of HBM per device.

v0:
```python
import jax
import jax.numpy as jnp
from jax import lax
from jax.sharding import PartitionSpec as P

OFFSETS = (0, 1, 10, 35, 70)
HIGH = lax.Precision.HIGHEST


def rotations(wig):
    mats = []
    for level in range(5):
        order = min(level, 2)
        rows = 2 * order + 1
        cols = 2 * level + 1
        piece = wig[OFFSETS[level] : OFFSETS[level] + rows * cols]
        mats.append(piece.reshape(rows, cols, piece.shape[-1]))
    return mats


def group(rotated, count):
    zero = jnp.stack([rotated[v][:, min(v, 2)] for v in range(5)], 1)
    plus_one = jnp.stack([rotated[v][:, min(v, 2) + 1] for v in range(1, 5)], 1)
    minus_one = jnp.stack([rotated[v][:, min(v, 2) - 1] for v in range(1, 5)], 1)
    plus_two = jnp.stack([rotated[v][:, 4] for v in range(2, 5)], 1)
    minus_two = jnp.stack([rotated[v][:, 0] for v in range(2, 5)], 1)
    return tuple((a.reshape(count, -1) for a in (zero, plus_one, minus_one, plus_two, minus_two)))


def ungroup(groups, count, chans):
    zero, plus_one, minus_one, plus_two, minus_two = [a.reshape(count, -1, chans) for a in groups]
    result = []
    for level in range(5):
        rows = []
        if level >= 2:
            rows.append(minus_two[:, level - 2])
        if level >= 1:
            rows.append(minus_one[:, level - 1])
        rows.append(zero[:, level])
        if level >= 1:
            rows.append(plus_one[:, level - 1])
        if level >= 2:
            rows.append(plus_two[:, level - 2])
        result.append(jnp.stack(rows, 1))
    return result


def tdot(left, right):
    return lax.dot_general(
        left, right, (((0,), (0,)), ((), ())), precision=HIGH, preferred_element_type=jnp.float32
    )


def ntdot(left, right):
    return lax.dot_general(
        left, right, (((1,), (1,)), ((), ())), precision=HIGH, preferred_element_type=jnp.float32
    )


def block_grads(xrows, grows, wig, weights):
    w_zero, w_one_re, w_one_im, w_two_re, w_two_im = weights
    count, coefs, chans = xrows.shape
    mats = rotations(wig)
    xrot = [
        jnp.einsum("rcb,bcf->brf", mats[v], xrows[:, v * v : (v + 1) * (v + 1)], precision=HIGH)
        for v in range(5)
    ]
    grot = [
        jnp.einsum("rcb,bcf->brf", mats[v], grows[:, v * v : (v + 1) * (v + 1)], precision=HIGH)
        for v in range(5)
    ]
    z0, zp1, zm1, zp2, zm2 = group(xrot, count)
    u0, up1, um1, up2, um2 = group(grot, count)
    grads = (
        tdot(z0, u0),
        tdot(zp1, up1) + tdot(zm1, um1),
        tdot(zp1, um1) - tdot(zm1, up1),
        tdot(zp2, up2) + tdot(zm2, um2),
        tdot(zp2, um2) - tdot(zm2, up2),
    )
    d0 = ntdot(u0, w_zero)
    dp1 = ntdot(up1, w_one_re) + ntdot(um1, w_one_im)
    dm1 = ntdot(um1, w_one_re) - ntdot(up1, w_one_im)
    dp2 = ntdot(up2, w_two_re) + ntdot(um2, w_two_im)
    dm2 = ntdot(um2, w_two_re) - ntdot(up2, w_two_im)
    back = ungroup((d0, dp1, dm1, dp2, dm2), count, chans)
    pieces = [jnp.einsum("rcb,brf->bcf", mats[v], back[v], precision=HIGH) for v in range(5)]
    return (jnp.concatenate(pieces, 1), grads)


def local(
    src_feats,
    tgt_cotangent,
    rotation,
    edge_src,
    edge_tgt,
    edge_count,
    w_zero,
    w_one_re,
    w_one_im,
    w_two_re,
    w_two_im,
):
    weights = (w_zero, w_one_re, w_one_im, w_two_re, w_two_im)
    chans = w_zero.shape[0] // 5
    feat = src_feats.shape[2]
    source_block = lax.all_gather(src_feats, "tgt", axis=1, tiled=True)[0]
    target_block = lax.all_gather(tgt_cotangent, "src", axis=1, tiled=True)[0]
    src_blk = source_block.shape[0]
    source_block = source_block.reshape(src_blk, 25, chans)
    target_block = target_block.reshape(target_block.shape[0], 25, chans)
    sources = edge_src[0, 0, 0]
    targets = edge_tgt[0, 0, 0]
    wig = rotation[0, 0, 0]
    live_count = edge_count[0, 0, 0]
    cap = sources.shape[0]
    width = 128
    atom_ids = jnp.arange(src_blk, dtype=jnp.int32)

    def step(index, carry):
        total, sums = carry
        start = index * width
        src_ids = lax.dynamic_slice_in_dim(sources, start, width)
        tgt_ids = lax.dynamic_slice_in_dim(targets, start, width)
        wig_block = lax.dynamic_slice_in_dim(wig, start, width, 1)
        live = (start + jnp.arange(width, dtype=jnp.int32) < live_count).astype(jnp.float32)
        xrows = jnp.take(source_block, src_ids, axis=0) * live[:, None, None]
        grows = jnp.take(target_block, tgt_ids, axis=0) * live[:, None, None]
        term, parts = block_grads(xrows, grows, wig_block, weights)
        onehot = (src_ids[:, None] == atom_ids[None, :]).astype(jnp.float32)
        added = tdot(onehot, term.reshape(width, feat))
        return (total + added, tuple((a + b for a, b in zip(sums, parts))))

    stop = cap // width
    init = (
        jnp.zeros((src_blk, feat), jnp.float32),
        tuple((jnp.zeros(w.shape, jnp.float32) for w in weights)),
    )
    total, sums = lax.fori_loop(0, stop, step, init)
    grad_feats = lax.psum_scatter(total[None], "tgt", scatter_dimension=1, tiled=True)
    summed = lax.psum((sums[0], sums[1], sums[2], sums[3], sums[4]), ("rep", "src", "tgt"))
    owner = lax.axis_index("src")
    parts_count = lax.axis_size("src")
    final = tuple(
        (
            lax.dynamic_slice_in_dim(
                a, owner * (a.shape[0] // parts_count), a.shape[0] // parts_count, 0
            )
            for a in summed
        )
    )
    return (grad_feats, final[0], final[1], final[2], final[3], final[4])


def solution(mesh):
    placed = (
        P("rep", ("src", "tgt"), None),
        P("rep", ("tgt", "src"), None),
        P("rep", "src", "tgt", None, None),
        P("rep", "src", "tgt", None),
        P("rep", "src", "tgt", None),
        P("rep", "src", "tgt"),
        P(),
        P(),
        P(),
        P(),
        P(),
    )
    return jax.shard_map(
        local,
        mesh=mesh,
        in_specs=placed,
        out_specs=(
            P("rep", ("src", "tgt"), None),
            P("src", None),
            P("src", None),
            P("src", None),
            P("src", None),
            P("src", None),
        ),
        check_vma=False,
    )
```

profile of v0, /device:TPU:0, one launch (start us, length us, event | category | flops | bytes accessed | tf_op | source)
XLA Modules:
  0.0 542.8 jit_solution(16878376208703558799)
XLA Ops:
  9.2 9.0 %all_gather.7 = f32[1,32,3200]{2,1,0:T(8,128)S(1)} all-gather(f32[1,16,3200]{2,1,0:T(8,128)} %param.13), channel_id=1, replica_groups=mesh['rep'=2,'src'=8,'tgt'=2] {'tgt'}, dimensions={1}, use_global_device_ids=true | all-gather | bytes 614400 | tf_op jit(solution)/shard_map/all_gather | solution.py:107
  19.0 39.0 %all-gather.2.cloned.1.call-done = f32[1,128,3200]{2,0,1:T(1,128)} async-done(((f32[1,16,3200]{2,0,1:T(1,128)}), f32[1,128,3200]{2,0,1:T(1,128)}) %all-gather.2.cloned.1.call-update) | async-done | bytes 1638416 | tf_op jit(solution)/shard_map/all_gather | solution.py:108
  58.1 3.4 copy.143
  63.6 310.7 %while.24 = (s32[]{:T(128)}, f32[32,3200]{1,0:T(8,128)}, f32[640,640]{1,0:T(8,128)}, f32[512,512]{1,0:T(8,128)}, f32[512,512]{1,0:T(8,128)}, /*index=5*/f32[384,...) while((s32[]{:T(128)}, f32[32,3200]{1,0:T(8,128)}, ...), condition=%wide.region_1.0_spmd.clone, body=%wide.region_0.1_spmd.clone.sunk | while | flops 6522671104 | bytes 163724032 | solution.py:139
  99.7 2.8 fusion.308
  119.8 2.7 select_add_fusion.2
  125.8 3.7 fusion.286
  144.6 3.0 fusion.292
  152.9 6.7 %concatenate.9 = f32[128,25,128]{2,1,0:T(8,128)S(1)} concatenate(f32[128,1,128]{2,1,0:T(1,128)S(1)} %bitcast.325, f32[128,3,128]{2,1,0:T(4,128)S(1)} %fusion.288, f32[128,5,128]{2,1,0:T(8,128)} %fusion.290, f32[128,7,128]{2,1,0:T(8,128)S(1)} %fusion.291, f32[128,9,128]{2,1,0:T(8,128)} %fusion.292), dimensions={1} | concatenate | bytes 3276800 | tf_op jit(solution)/shard_map/while/body/eval_jaxpr/concatenate | solution.py:88
  161.4 2.5 convolution_add_fusion.10
  200.7 2.9 fusion.308
  213.9 3.5 fusion.304
  222.4 4.2 select_add_fusion.2
  229.9 3.7 fusion.286
  248.7 3.2 fusion.292
  257.2 6.7 %concatenate.9 = f32[128,25,128]{2,1,0:T(8,128)S(1)} concatenate(f32[128,1,128]{2,1,0:T(1,128)S(1)} %bitcast.325, f32[128,3,128]{2,1,0:T(4,128)S(1)} %fusion.288, f32[128,5,128]{2,1,0:T(8,128)} %fusion.290, f32[128,7,128]{2,1,0:T(8,128)S(1)} %fusion.291, f32[128,9,128]{2,1,0:T(8,128)} %fusion.292), dimensions={1} | concatenate | bytes 3276800 | tf_op jit(solution)/shard_map/while/body/eval_jaxpr/concatenate | solution.py:88
  304.8 2.9 fusion.308
  318.0 3.5 fusion.304
  326.8 4.2 select_add_fusion.2
  334.3 3.7 fusion.286
  353.1 3.0 fusion.292
  361.4 6.7 %concatenate.9 = f32[128,25,128]{2,1,0:T(8,128)S(1)} concatenate(f32[128,1,128]{2,1,0:T(1,128)S(1)} %bitcast.325, f32[128,3,128]{2,1,0:T(4,128)S(1)} %fusion.288, f32[128,5,128]{2,1,0:T(8,128)} %fusion.290, f32[128,7,128]{2,1,0:T(8,128)S(1)} %fusion.291, f32[128,9,128]{2,1,0:T(8,128)} %fusion.292), dimensions={1} | concatenate | bytes 3276800 | tf_op jit(solution)/shard_map/while/body/eval_jaxpr/concatenate | solution.py:88
  375.1 146.0 %all-reduce.3.cloned.1.call-done = (f32[640,640]{1,0:T(8,128)}, f32[512,512]{1,0:T(8,128)}, f32[512,512]{1,0:T(8,128)}, f32[384,384]{1,0:T(8,128)}, f32[384,384]{1,0:T(8,128)}) async-done(((f32[640,640]{1,0:T(8,128)}, f32[512,512]{1,0:T(8,128)}, f32[512,512]{1,0:T(8,128)}, f32[384,384]{1,0:T(8,128)}, f32[384,384]{1,0:T(8,128)}), (f32[640,640]{1,0:T(8,128)}, f32[512,512]{1,0:T(8,128)}, f32[512,512]{1,0:T(8,128)}, ...) | async-done | bytes 4915216 | tf_op jit(solution)/shard_map/psum | solution.py:141
  526.0 10.1 %reduce-scatter.2.cloned.1.call-done = f32[1,16,3200]{2,1,0:T(8,128)} async-done(((f32[1,32,3200]{2,1,0:T(8,128)}), f32[1,16,3200]{2,1,0:T(8,128)}) %reduce-scatter.2.cloned.1.call-update) | async-done | bytes 204816 | tf_op jit(solution)/shard_map/reduce_scatter | solution.py:140
  (723 shorter events, 246.4 us)
Async XLA Ops:
  7.2 11.1 %copy-start.56 = (f32[1,1,1,115,384]{4,2,3,1,0:T(1,128)S(1)}, f32[1,1,1,115,384]{4,2,3,1,0:T(1,128)}, u32[]{:S(2)}) copy-start(f32[1,1,1,115,384]{4,2,3,1,0:T(1,128)} %param.15) | copy-start | bytes 529924
  7.2 11.8 %copy-start.63 = (s32[1,1,1,384]{3,2,1,0:T(1,128)S(1)}, s32[1,1,1,384]{3,2,1,0:T(1,128)}, u32[]{:S(2)}) copy-start(s32[1,1,1,384]{3,2,1,0:T(1,128)} %param.16) | copy-start | bytes 4612
  7.2 11.8 %copy-start.64 = (s32[1,1,1,384]{3,2,1,0:T(1,128)S(1)}, s32[1,1,1,384]{3,2,1,0:T(1,128)}, u32[]{:S(2)}) copy-start(s32[1,1,1,384]{3,2,1,0:T(1,128)} %param.17) | copy-start | bytes 4612
  7.2 50.9 %all-gather.2.cloned.1.call-start = ((), (), s32[]{:S(2)}) async-start(), calls=%async_computation.1 | async-start | bytes 1843200 | tf_op jit(solution)/shard_map/all_gather | solution.py:108
  9.1 511.9 %all-reduce.3.cloned.1.call-start = ((), (), s32[]{:S(2)}) async-start(), calls=%async_computation.3 | async-start | bytes 9830400 | tf_op jit(solution)/shard_map/psum | solution.py:141
  63.6 15.3 %copy-start.61 = (s32[384]{0:T(512)}, s32[384]{0:T(512)S(1)}, u32[]{:S(2)}) copy-start(s32[384]{0:T(512)S(1)} %get-tuple-element.817) | copy-start | bytes 4612 | tf_op jit(solution)/shard_map/while
  78.9 12.8 %copy-start.19 = (f32[128,3,128]{0,2,1:T(8,128)}, f32[128,3,128]{0,2,1:T(8,128)S(1)}, u32[]{:S(2)}) copy-start(f32[128,3,128]{0,2,1:T(8,128)S(1)} %copy.306) | copy-start | bytes 589828 | tf_op jit(solution)/shard_map/while
  91.7 11.4 %copy-start.4 = (f32[128,3,128]{0,2,1:T(8,128)}, f32[128,3,128]{0,2,1:T(8,128)S(1)}, u32[]{:S(2)}) copy-start(f32[128,3,128]{0,2,1:T(8,128)S(1)} %copy.288) | copy-start | bytes 589828 | tf_op jit(solution)/shard_map/while
  130.7 5.6 %copy-start.7 = (f32[128,3,128]{0,2,1:T(8,128)S(1)}, f32[128,3,128]{0,2,1:T(8,128)}, u32[]{:S(2)}) copy-start(f32[128,3,128]{0,2,1:T(8,128)} %copy-done.6) | copy-start | bytes 589828 | tf_op jit(solution)/shard_map/while
  130.7 5.6 %copy-start.15 = (f32[384,384]{1,0:T(8,128)S(1)}, f32[384,384]{1,0:T(8,128)}, u32[]{:S(2)}) copy-start(f32[384,384]{1,0:T(8,128)} %get-tuple-element.824) | copy-start | bytes 1769476 | tf_op jit(solution)/shard_map/while
  134.4 5.5 %copy-start.23 = (f32[128,5,128]{0,2,1:T(8,128)S(1)}, f32[128,5,128]{0,2,1:T(8,128)}, u32[]{:S(2)}) copy-start(f32[128,5,128]{0,2,1:T(8,128)} %fusion.286) | copy-start | bytes 983044 | tf_op jit(solution)/shard_map/while
  165.1 15.3 %copy-start.61 = (s32[384]{0:T(512)}, s32[384]{0:T(512)S(1)}, u32[]{:S(2)}) copy-start(s32[384]{0:T(512)S(1)} %get-tuple-element.817) | copy-start | bytes 4612 | tf_op jit(solution)/shard_map/while
  180.4 12.4 %copy-start.19 = (f32[128,3,128]{0,2,1:T(8,128)}, f32[128,3,128]{0,2,1:T(8,128)S(1)}, u32[]{:S(2)}) copy-start(f32[128,3,128]{0,2,1:T(8,128)S(1)} %copy.306) | copy-start | bytes 589828 | tf_op jit(solution)/shard_map/while
  192.8 11.6 %copy-start.4 = (f32[128,3,128]{0,2,1:T(8,128)}, f32[128,3,128]{0,2,1:T(8,128)S(1)}, u32[]{:S(2)}) copy-start(f32[128,3,128]{0,2,1:T(8,128)S(1)} %copy.288) | copy-start | bytes 589828 | tf_op jit(solution)/shard_map/while
  234.8 5.6 %copy-start.7 = (f32[128,3,128]{0,2,1:T(8,128)S(1)}, f32[128,3,128]{0,2,1:T(8,128)}, u32[]{:S(2)}) copy-start(f32[128,3,128]{0,2,1:T(8,128)} %copy-done.6) | copy-start | bytes 589828 | tf_op jit(solution)/shard_map/while
  234.8 5.6 %copy-start.15 = (f32[384,384]{1,0:T(8,128)S(1)}, f32[384,384]{1,0:T(8,128)}, u32[]{:S(2)}) copy-start(f32[384,384]{1,0:T(8,128)} %get-tuple-element.824) | copy-start | bytes 1769476 | tf_op jit(solution)/shard_map/while
  238.5 5.5 %copy-start.23 = (f32[128,5,128]{0,2,1:T(8,128)S(1)}, f32[128,5,128]{0,2,1:T(8,128)}, u32[]{:S(2)}) copy-start(f32[128,5,128]{0,2,1:T(8,128)} %fusion.286) | copy-start | bytes 983044 | tf_op jit(solution)/shard_map/while
  269.1 15.3 %copy-start.61 = (s32[384]{0:T(512)}, s32[384]{0:T(512)S(1)}, u32[]{:S(2)}) copy-start(s32[384]{0:T(512)S(1)} %get-tuple-element.817) | copy-start | bytes 4612 | tf_op jit(solution)/shard_map/while
  284.5 12.4 %copy-start.19 = (f32[128,3,128]{0,2,1:T(8,128)}, f32[128,3,128]{0,2,1:T(8,128)S(1)}, u32[]{:S(2)}) copy-start(f32[128,3,128]{0,2,1:T(8,128)S(1)} %copy.306) | copy-start | bytes 589828 | tf_op jit(solution)/shard_map/while
  296.9 11.6 %copy-start.4 = (f32[128,3,128]{0,2,1:T(8,128)}, f32[128,3,128]{0,2,1:T(8,128)S(1)}, u32[]{:S(2)}) copy-start(f32[128,3,128]{0,2,1:T(8,128)S(1)} %copy.288) | copy-start | bytes 589828 | tf_op jit(solution)/shard_map/while
  339.1 5.6 %copy-start.7 = (f32[128,3,128]{0,2,1:T(8,128)S(1)}, f32[128,3,128]{0,2,1:T(8,128)}, u32[]{:S(2)}) copy-start(f32[128,3,128]{0,2,1:T(8,128)} %copy-done.6) | copy-start | bytes 589828 | tf_op jit(solution)/shard_map/while
  339.2 5.6 %copy-start.15 = (f32[384,384]{1,0:T(8,128)S(1)}, f32[384,384]{1,0:T(8,128)}, u32[]{:S(2)}) copy-start(f32[384,384]{1,0:T(8,128)} %get-tuple-element.824) | copy-start | bytes 1769476 | tf_op jit(solution)/shard_map/while
  342.9 5.5 %copy-start.23 = (f32[128,5,128]{0,2,1:T(8,128)S(1)}, f32[128,5,128]{0,2,1:T(8,128)}, u32[]{:S(2)}) copy-start(f32[128,5,128]{0,2,1:T(8,128)} %fusion.286) | copy-start | bytes 983044 | tf_op jit(solution)/shard_map/while
  374.3 161.7 %reduce-scatter.2.cloned.1.call-start = ((), (), s32[]{:S(2)}) async-start(), calls=%async_computation.2 | async-start | bytes 614400 | tf_op jit(solution)/shard_map/reduce_scatter | solution.py:140
  (177 other events, 462.4 us)
Sparse Core Ops, SparseCore 0:
  10.8 47.2 all-gather.1
  374.4 146.5 all-reduce.2
  523.9 12.0 reduce-scatter.1
where the time goes:
time: 548 us; the launch traced here: 543 us
  waiting for transfers between devices  196 us (36%)
  matrix products  145 us (26%)
  local copies, waits for them, and re-layouts  144 us (26%)
  other arithmetic  29.3 us (5%)
  between operations  14.1 us (3%)
  blocking collectives  8.97 us (2%)
    psum x1, waiting for transfers between devices, local(): lax.psum((sums[0], sums[1], sums[2], sums[3], sums[4]), ('rep', 'src', 't...  146 us
    dot_general x30, matrix products, tdot(): lax.dot_general(left, right, (((0,), (0,)), ((), ())), precision=HIGH, pr...  55.5 us
    dot_general x27, matrix products, ntdot(): lax.dot_general(left, right, (((1,), (1,)), ((), ())), precision=HIGH, pr...  40.4 us
    all_gather x1, waiting for transfers between devices, local(): target_block = lax.all_gather(tgt_cotangent, 'src', axis=1, tiled=True)[0]  39 us
    while x405, local copies, waits for them, and re-layouts  26.4 us
    concatenate x6, local copies, waits for them, and re-layouts, block_grads(): return (jnp.concatenate(pieces, 1), grads)  25.2 us
    dot_general x12, matrix products, block_grads(): jnp.einsum('rcb,brf->bcf', mats[v], back[v], precision=HIGH)  20.3 us
    dot_general x12, matrix products, block_grads(): jnp.einsum('rcb,bcf->brf', mats[v], xrows[:, v * v:(v + 1) * (v + 1)], pr...  17 us
  transfers between devices with their start and end apart: 3, of which 3 were waited for; matrix products, arithmetic and copies ran while one was open for 1% of the time, Pallas kernels for 0%

commit v1 on v0

v1 whole, which is shorter than its diff:
```python
import functools

import jax
import jax.numpy as jnp
from jax import lax
from jax.experimental import pallas as pl
from jax.experimental.pallas import tpu as pltpu
from jax.sharding import PartitionSpec as P

OFFSETS = (0, 1, 10, 35, 70)
ROT = 115
LANES = 128
AXES = ("rep", "src", "tgt")
F32 = jnp.float32
BF16 = jnp.bfloat16

GROUPS = (5, 4, 4, 3, 3)
STARTS = (0, 5, 9, 13, 16)


def place(level, order):
    group = {0: 0, 1: 1, -1: 2, 2: 3, -2: 4}[order]
    return STARTS[group] + level - abs(order)


def split(value):
    high = value.astype(BF16)
    return high, (value - high.astype(F32)).astype(BF16)


def nt(left, right):
    return lax.dot_general(left, right, (((1,), (1,)), ((), ())), preferred_element_type=F32)


def tn(left, right):
    return lax.dot_general(left, right, (((0,), (0,)), ((), ())), preferred_element_type=F32)


def nn(left, right):
    return lax.dot_general(left, right, (((1,), (0,)), ((), ())), preferred_element_type=F32)


def onehot(row, atoms, shard, mine, flip, twice=True):
    ids = row.astype(jnp.int32)
    bits = shard.bit_length() - 1
    rel = lax.shift_right_arithmetic(ids, bits) ^ mine
    if flip is not None:
        pair = rel & 3
        swapped = lax.shift_right_logical(pair, 1) | lax.shift_left(pair & 1, 1)
        rel = jnp.where(flip != 0, (rel & ~3) | swapped, rel)
    where = jnp.where(ids < 0, -1, lax.shift_left(rel, bits) | (ids & (shard - 1)))
    hit = lax.broadcasted_iota(jnp.int32, (atoms, row.shape[1]), 0) == where
    one = jnp.where(hit, 1.0, 0.0).astype(BF16)
    return jnp.concatenate([one, one], 0) if twice else one


def gather(shards, select, out, chans):
    for level in range(5):
        first, last = level * level * chans, (level + 1) * (level + 1) * chans
        rows = jnp.concatenate([s[:, first:last] for s in shards], 0)
        high, low = split(rows)
        out[first:last, :] = tn(jnp.concatenate([high, low], 0), select)


def spread(pack, out):
    for k in range(ROT):
        out[k] = jnp.broadcast_to(pack[k : k + 1, :], (8, pack.shape[1]))


def rotate(rot, feats, base, store, chans):
    edges = rot.shape[2]
    tiles = edges // LANES

    def body(step, carry):
        tile = step % tiles
        strip = step // tiles
        lanes = pl.ds(pl.multiple_of(tile * LANES, LANES), LANES)
        wide = pl.ds(pl.multiple_of(base + tile * LANES, LANES), LANES)
        for level in range(5):
            order = min(level, 2)
            cols = 2 * level + 1
            acc = [[None, None] for _ in range(2 * order + 1)]
            for c in range(cols):
                row = pl.multiple_of((level * level + c) * chans + strip * 16, 16)
                x = feats[pl.ds(row, 16), wide]
                for r in range(2 * order + 1):
                    factor = rot[OFFSETS[level] + r * cols + c, :, lanes]
                    for half in range(2):
                        term = factor * x[half * 8 : half * 8 + 8]
                        acc[r][half] = term if c == 0 else acc[r][half] + term
            for r in range(2 * order + 1):
                store(place(level, r - order), strip, wide, jnp.concatenate(acc[r], 0))
        return carry

    lax.fori_loop(0, (chans // 16) * tiles, body, 0)


def source_kernel(count, shard, own_slots, chans, me, *refs):
    shards = (refs[:count], refs[count : 2 * count])
    packs = refs[2 * count : 2 * count + 2]
    high_out, low_out, feats, rot, full, picked = refs[2 * count + 2 :]
    edges = packs[0].shape[1]
    mine, owner = me[1], me[0]
    rows = tuple(g * chans // (2 * own_slots) for g in GROUPS)
    for tile in range(2):
        select = onehot(packs[tile][ROT : ROT + 1, :], count * shard, shard, mine, None)
        gather(shards[tile], select, feats, chans)
        spread(packs[tile], rot)

        def store(where, strip, lanes, value):
            full[pl.ds(pl.multiple_of(where * chans + strip * 16, 16), 16), lanes] = value

        rotate(rot, feats, 0, store, chans)
        at = 0
        for group in range(5):
            for slot in range(own_slots):
                owned = owner ^ (2 * slot)
                source = pl.multiple_of(STARTS[group] * chans + owned * rows[group], 8)
                picked[at : at + rows[group], :] = full[pl.ds(source, rows[group]), :]
                at += rows[group]
        high, low = split(picked[...])
        high_out[:, tile * edges : (tile + 1) * edges] = high
        low_out[:, tile * edges : (tile + 1) * edges] = low


def weight_kernel(count, shard, own_slots, parts, chans, me, *refs):
    shards = refs[:count]
    packs = refs[count : count + 2]
    zh_any, zl_any = refs[count + 2 : count + 4]
    keep_any, send_any, uh_any, ul_any = refs[count + 4 : count + 8]
    feats, rot, zh, zl, uh, ul, full, load_sem, u_sem, out_sem = refs[count + 8 :]
    edges = packs[0].shape[1]
    owner, core, tgt = me[0], me[2], me[1]
    loads = [
        pltpu.make_async_copy(zh_any, zh, load_sem.at[0]),
        pltpu.make_async_copy(zl_any, zl, load_sem.at[1]),
    ]
    for load in loads:
        load.start()
    select = jnp.concatenate(
        [onehot(p[ROT + 1 : ROT + 2, :], count * shard, shard, owner, core) for p in packs], 1
    )
    gather(shards, select, feats, chans)

    def store(where, strip, lanes, value):
        high, low = split(value)
        rows = pl.ds(pl.multiple_of(where * chans + strip * 16, 16), 16)
        uh[rows, lanes] = high
        ul[rows, lanes] = low

    for tile in range(2):
        spread(packs[tile], rot)
        rotate(rot, feats, tile * edges, store, chans)
        if tile == 0:
            saves = [
                pltpu.make_async_copy(uh.at[:, 0:edges], uh_any, u_sem.at[0]),
                pltpu.make_async_copy(ul.at[:, 0:edges], ul_any, u_sem.at[1]),
            ]
            for save in saves:
                save.start()
    for load in loads:
        load.wait()

    def product(left, right):
        lo = sum(GROUPS[:left]) * chans // 2, sum(GROUPS[: left + 1]) * chans // 2
        ro = STARTS[right] * chans, (STARTS[right] + GROUPS[right]) * chans
        a, b = zh[lo[0] : lo[1], :], uh[ro[0] : ro[1], :]
        c, d = zl[lo[0] : lo[1], :], ul[ro[0] : ro[1], :]
        return nt(a, b) + nt(a, d) + nt(c, b)

    def put(at, value):
        wide = value.shape[1] // LANES
        high = value.shape[0] // own_slots // 8
        for col in range(wide):
            block = value[:, col * LANES : (col + 1) * LANES]
            full[:, at + col * high : at + (col + 1) * high] = block.reshape(own_slots, high, 8, LANES)
        return at + wide * high

    at = put(0, product(0, 0))
    at = put(at, product(1, 1) + product(2, 2))
    at = put(at, product(1, 2) - product(2, 1))
    at = put(at, product(3, 3) + product(4, 4))
    at = put(at, product(3, 4) - product(4, 3))
    total = full.shape[1]
    if at < total:
        full[:, at:total] = jnp.zeros((own_slots, total - at, 8, LANES), F32)
    piece = total // (2 * parts)
    rest = parts * own_slots // 4
    copies = []
    for side, target in ((0, keep_any), (1, send_any)):
        for part in range(parts):
            for slot in range(own_slots):
                first, second = part & 1, slot & 1
                lower = (part >> 1) * (own_slots // 2) + (slot >> 1)
                pos = jnp.where(core == side, first * 2 + second, second * 2 + first) * rest + lower
                begin = ((core ^ side) * parts + (tgt ^ part)) * piece
                copy = pltpu.make_async_copy(
                    full.at[slot, pl.ds(begin, piece)], target.at[pos], out_sem.at[len(copies)]
                )
                copy.start()
                copies.append(copy)
    for copy in copies + saves:
        copy.wait()


def dual(wh, wl, uh, ul):
    return nn(wh, uh) + nn(wh, ul) + nn(wl, uh)


def back_zero_kernel(chans, w, uh, ul, out):
    wh, wl = split(w[...])
    out[...] = dual(wh, wl, uh[0 : 5 * chans, :], ul[0 : 5 * chans, :])


def back_pair_kernel(first, groups, chans, re, im, uh, ul, out):
    size = groups * chans
    rh, rl = split(re[...])
    ih, il = split(im[...])
    p = slice(first * chans, first * chans + size)
    m = slice(first * chans + size, first * chans + 2 * size)
    out[0:size, :] = dual(rh, rl, uh[p, :], ul[p, :]) + dual(ih, il, uh[m, :], ul[m, :])
    out[size : 2 * size, :] = dual(rh, rl, uh[m, :], ul[m, :]) - dual(ih, il, uh[p, :], ul[p, :])


def scatter_kernel(count, shard, chans, me, pack, d0, d1, d2, out, rot, back):
    select = onehot(pack[ROT : ROT + 1, :], count * shard, shard, me[1], None, False)
    spread(pack, rot)
    edges = pack.shape[1]
    tiles = edges // LANES
    pieces = (d0, d1, d2)
    firsts = (0, 5, 13)

    def load(where, strip, lanes):
        which = 0 if where < 5 else 1 if where < 13 else 2
        row = pl.multiple_of((where - firsts[which]) * chans + strip * 16, 16)
        return pieces[which][pl.ds(row, 16), lanes]

    def body(step, carry):
        tile = step % tiles
        strip = step // tiles
        lanes = pl.ds(pl.multiple_of(tile * LANES, LANES), LANES)
        for level in range(5):
            order = min(level, 2)
            cols = 2 * level + 1
            d = [load(place(level, r - order), strip, lanes) for r in range(2 * order + 1)]
            for c in range(cols):
                acc = [None, None]
                for r in range(2 * order + 1):
                    factor = rot[OFFSETS[level] + r * cols + c, :, lanes]
                    for half in range(2):
                        term = factor * d[r][half * 8 : half * 8 + 8]
                        acc[half] = term if r == 0 else acc[half] + term
                row = pl.multiple_of((level * level + c) * chans + strip * 16, 16)
                back[pl.ds(row, 16), lanes] = jnp.concatenate(acc, 0)
        return carry

    lax.fori_loop(0, (chans // 16) * tiles, body, 0)
    for level in range(5):
        first, last = level * level * chans, (level + 1) * (level + 1) * chans
        high, low = split(back[first:last, :])
        total = nt(select, high) + nt(select, low)
        for part in range(count):
            out[part, :, first:last] = total[part * shard : (part + 1) * shard]


def unpack_kernel(parts, chans, me, *refs):
    mine = refs[:parts]
    other = refs[parts : 2 * parts]
    outs = refs[2 * parts : 2 * parts + 5]
    tiles = refs[2 * parts + 5]
    piece = mine[0].shape[0]
    tgt, core = me[1], me[2]
    for side, group in ((0, mine), (1, other)):
        for part in range(parts):
            begin = ((core ^ side) * parts + (tgt ^ part)) * piece
            tiles[pl.ds(begin, piece)] = group[part][...]
    at = 0
    for out in outs:
        high, wide = out.shape[0] // 8, out.shape[1] // LANES
        for col in range(wide):
            block = tiles[at : at + high].reshape(high * 8, LANES)
            out[:, col * LANES : (col + 1) * LANES] = block
            at += high


def vmem(count):
    return [pl.BlockSpec(memory_space=pltpu.VMEM)] * count


def anywhere(count):
    return [pl.BlockSpec(memory_space=pl.ANY)] * count


SMEM = [pl.BlockSpec(memory_space=pltpu.SMEM)]


def call(kernel, name, ins, outs, shapes, scratch, flops, moved):
    return pl.pallas_call(
        kernel,
        name=name,
        in_specs=ins,
        out_specs=outs,
        out_shape=shapes,
        scratch_shapes=scratch,
        compiler_params=pltpu.CompilerParams(vmem_limit_bytes=56 * 1024 * 1024),
        cost_estimate=pl.CostEstimate(flops=flops, bytes_accessed=moved, transcendentals=0),
    )


def shape(*dims, dtype=F32):
    return jax.ShapeDtypeStruct(dims, dtype)


def local(
    sizes,
    src_feats,
    tgt_cotangent,
    rotation,
    edge_src,
    edge_tgt,
    edge_count,
    w_zero,
    w_one_re,
    w_one_im,
    w_two_re,
    w_two_im,
):
    reps, nsrc, ntgt = sizes
    chans = w_zero.shape[0] // 5
    shard, feat = src_feats.shape[1], src_feats.shape[2]
    edges = edge_src.shape[-1]
    slots = nsrc // 2
    src_bits = nsrc.bit_length() - 1
    tgt_bits = ntgt.bit_length() - 1
    me_src, me_tgt, me_rep = (lax.axis_index(a).astype(jnp.int32) for a in ("src", "tgt", "rep"))
    me = jnp.stack([me_src, me_tgt, me_rep])

    def hop(value, axes, *routes):
        pairs = []
        for rep in range(reps):
            s_mask, t_mask = routes[rep % len(routes)]
            for s in range(nsrc):
                for t in range(ntgt):
                    base = rep * nsrc * ntgt
                    pairs.append((base + s * ntgt + t, base + (s ^ s_mask) * ntgt + (t ^ t_mask)))
        return lax.ppermute(value, AXES, pairs)

    def cross(value):
        half = nsrc * ntgt
        return lax.ppermute(value, AXES, [(i, (i + half) % (2 * half)) for i in range(2 * half)])

    live = jnp.arange(edges, dtype=jnp.int32) < edge_count[0, 0, 0]
    ends = jnp.stack([jnp.where(live, e[0, 0, 0], -1) for e in (edge_src, edge_tgt)]).astype(F32)
    pack = jnp.concatenate([rotation[0, 0, 0], ends, jnp.zeros((3, edges), F32)], 0)
    x_own = src_feats[0]
    g_own = tgt_cotangent[0]

    g_parts = {0: g_own}
    for bit in range(src_bits - 1, 1, -1):
        for k, part in list(g_parts.items()):
            g_parts[k | (1 << bit)] = hop(part, None, (1 << bit, 0))
    pack_other = hop(pack, None, (1, 0))
    x_other = hop(x_own, None, (1, 0))
    for k, part in list(g_parts.items()):
        g_parts[k | 1] = hop(part, None, (1, 0), (2, 0))
    x_parts = [x_own] + [hop(x_own, None, (0, t)) for t in range(1, ntgt)]
    y_parts = [x_other] + [hop(x_other, None, (0, t)) for t in range(1, ntgt)]
    for k, part in list(g_parts.items()):
        g_parts[k | 2] = hop(part, None, (2, 0), (1, 0))
    g_list = [g_parts[k] for k in range(nsrc)]

    groups = sum(GROUPS) * chans
    z_rows = groups // 2
    zh, zl = call(
        functools.partial(source_kernel, ntgt, shard, slots, chans),
        "source_rows",
        SMEM + vmem(2 * ntgt + 2),
        vmem(2),
        [shape(z_rows, 2 * edges, dtype=BF16)] * 2,
        [
            pltpu.VMEM((feat, edges), F32),
            pltpu.VMEM((ROT, 8, edges), F32),
            pltpu.VMEM((groups, edges), F32),
            pltpu.VMEM((z_rows, edges), F32),
        ],
        3_000_000_000,
        8_000_000,
    )(me, *x_parts, *y_parts, pack, pack_other)

    per_slot = sum(
        (w.shape[0] // nsrc // 8) * (w.shape[1] // LANES)
        for w in (w_zero, w_one_re, w_one_im, w_two_re, w_two_im)
    )
    piece = -(-per_slot // (reps * ntgt))
    subs = ntgt * slots
    keep, send, uh, ul = call(
        functools.partial(weight_kernel, nsrc, shard, slots, ntgt, chans),
        "weight_terms",
        SMEM + vmem(nsrc + 2) + anywhere(2),
        anywhere(4),
        [shape(subs, piece, 8, LANES)] * 2 + [shape(groups, edges, dtype=BF16)] * 2,
        [
            pltpu.VMEM((feat, 2 * edges), F32),
            pltpu.VMEM((ROT, 8, edges), F32),
            pltpu.VMEM((z_rows, 2 * edges), BF16),
            pltpu.VMEM((z_rows, 2 * edges), BF16),
            pltpu.VMEM((groups, 2 * edges), BF16),
            pltpu.VMEM((groups, 2 * edges), BF16),
            pltpu.VMEM((slots, piece * reps * ntgt, 8, LANES), F32),
            pltpu.SemaphoreType.DMA((2,)),
            pltpu.SemaphoreType.DMA((2,)),
            pltpu.SemaphoreType.DMA((2 * subs,)),
        ],
        8_000_000_000,
        12_000_000,
    )(me, *g_list, pack, pack_other, zh, zl)

    routes = [((0, 1), (2, 0)), ((2, 0), (0, 1))]
    routes += [((0, 1 << b),) * 2 for b in range(tgt_bits - 1, 0, -1)]
    routes += [((1 << b, 0),) * 2 for b in range(src_bits - 1, 1, -1)]
    held, came = keep, cross(send)
    for route in routes:
        half = held.shape[0] // 2
        sent = held[half:] + came[half:]
        held = held[:half] + came[:half]
        came = hop(sent, None, *route)
    final = held[0] + came[0]

    d0 = call(
        functools.partial(back_zero_kernel, chans),
        "back_zero", vmem(3), vmem(1)[0], shape(5 * chans, edges), [], 1_900_000_000, 4_000_000,
    )(w_zero, uh, ul)
    d1 = call(
        functools.partial(back_pair_kernel, 5, 4, chans),
        "back_one", vmem(4), vmem(1)[0], shape(8 * chans, edges), [], 3_000_000_000, 5_000_000,
    )(w_one_re, w_one_im, uh, ul)
    d2 = call(
        functools.partial(back_pair_kernel, 13, 3, chans),
        "back_two", vmem(4), vmem(1)[0], shape(6 * chans, edges), [], 1_800_000_000, 4_000_000,
    )(w_two_re, w_two_im, uh, ul)
    atoms = call(
        functools.partial(scatter_kernel, ntgt, shard, chans),
        "source_sums",
        SMEM + vmem(4),
        vmem(1)[0],
        shape(ntgt, shard, feat),
        [pltpu.VMEM((ROT, 8, edges), F32), pltpu.VMEM((feat, edges), F32)],
        3_000_000_000,
        4_000_000,
    )(me, pack, d0, d1, d2)
    for b in range(tgt_bits - 1, -1, -1):
        half = atoms.shape[0] // 2
        atoms = atoms[:half] + hop(atoms[half:], None, (0, 1 << b))
    grad_feats = atoms

    mine = [final] + [hop(final, None, (0, t)) for t in range(1, ntgt)]
    other = [cross(m) for m in mine]
    outs = call(
        functools.partial(unpack_kernel, ntgt, chans),
        "unpack",
        SMEM + vmem(2 * ntgt),
        vmem(5),
        [
            shape(w.shape[0] // nsrc, w.shape[1])
            for w in (w_zero, w_one_re, w_one_im, w_two_re, w_two_im)
        ],
        [pltpu.VMEM((piece * reps * ntgt, 8, LANES), F32)],
        1_000_000,
        1_500_000,
    )(me, *mine, *other)
    return (grad_feats, *outs)


def solution(mesh):
    placed = (
        P("rep", ("src", "tgt"), None),
        P("rep", ("tgt", "src"), None),
        P("rep", "src", "tgt", None, None),
        P("rep", "src", "tgt", None),
        P("rep", "src", "tgt", None),
        P("rep", "src", "tgt"),
        P(),
        P(),
        P(),
        P(),
        P(),
    )
    sizes = tuple(mesh.shape[a] for a in AXES)
    return jax.shard_map(
        functools.partial(local, sizes),
        mesh=mesh,
        in_specs=placed,
        out_specs=(
            P("rep", ("src", "tgt"), None),
            P("src", None),
            P("src", None),
            P("src", None),
            P("src", None),
            P("src", None),
        ),
        check_vma=False,
    )
```

time: 548 us -> 111 us (0.20)
  waiting for transfers between devices: 196 us -> 25.7 us
  matrix products: 145 us -> 0 us
  local copies, waits for them, and re-layouts: 144 us -> 4.79 us
  Pallas kernels: 0 us -> 53.2 us
  other arithmetic: 29.3 us -> 4.71 us
  starting transfers between devices: 0.12 us -> 20.8 us
  between operations: 14.1 us -> 1.51 us
  blocking collectives: 8.97 us -> 0 us
    psum x1 -> x0, waiting for transfers between devices: 146 us -> none  [local(): lax.psum((sums[0], sums[1], sums[2], sums[3], sums[4]), ('rep', 'src', 't...]
    dot_general x93 -> x0, matrix products: 145 us -> none  [the longest x30 55.5 us: tdot(): lax.dot_general(left, right, (((0,), (0,)), ((), ())), precision=HIGH, pr...]
    pallas_call x0 -> x7, Pallas kernels: none -> 53.2 us  [the longest x1 16.6 us: local(): call(functools.partial(weight_kernel, nsrc, shard, slots, ntgt, chans), '...]
    all_gather x1 -> x0, waiting for transfers between devices: 39 us -> none  [local(): target_block = lax.all_gather(tgt_cotangent, 'src', axis=1, tiled=True)[0]]
    slice x60 -> x1, local copies, waits for them, and re-layouts: 29.3 us -> 0.94 us  [local(): atoms = atoms[:half] + hop(atoms[half:], None, (0, 1 << b))]
    while x405 -> x0, local copies, waits for them, and re-layouts: 26.4 us -> none
    ppermute x0 -> x19, waiting for transfers between devices: none -> 25.7 us  [the longest x16 22.6 us: hop(): return lax.ppermute(value, AXES, pairs)]
    concatenate x6 -> x1, local copies, waits for them, and re-layouts: 25.2 us -> 0.07 us  [local(): jnp.concatenate([rotation[0, 0, 0], ends, jnp.zeros((3, edges), F32)], 0)]
  transfers between devices with their start and end apart: 3 -> 19, of which waited for: 3 -> 5; matrix products, arithmetic and copies ran while one was open for 1% -> 5% of each run, Pallas kernels for 0% -> 31%
where the time goes in v1:
time: 111 us
  Pallas kernels  53.2 us (48%)
  waiting for transfers between devices  25.7 us (23%)
  starting transfers between devices  20.8 us (19%)
  local copies, waits for them, and re-layouts  4.79 us (4%)
  other arithmetic  4.71 us (4%)
  between operations  1.51 us (1%)
    ppermute x16, waiting for transfers between devices, hop(): return lax.ppermute(value, AXES, pairs)  22.6 us
    ppermute x16, starting transfers between devices, hop(): return lax.ppermute(value, AXES, pairs)  20.8 us
    pallas_call x1, Pallas kernels, local(): call(functools.partial(weight_kernel, nsrc, shard, slots, ntgt, chans), '...  16.6 us
    pallas_call x1, Pallas kernels, local(): call(functools.partial(source_kernel, ntgt, shard, slots, chans), 'source...  9.67 us
    pallas_call x1, Pallas kernels, local(): call(functools.partial(back_pair_kernel, 5, 4, chans), 'back_one', vmem(4...  7.29 us
    pallas_call x1, Pallas kernels, local(): call(functools.partial(scatter_kernel, ntgt, shard, chans), 'source_sums'...  6.78 us
    pallas_call x1, Pallas kernels, local(): call(functools.partial(back_pair_kernel, 13, 3, chans), 'back_two', vmem(...  5.76 us
    pallas_call x1, Pallas kernels, local(): call(functools.partial(back_zero_kernel, chans), 'back_zero', vmem(3), vm...  5.08 us
  transfers between devices with their start and end apart: 19, of which 5 were waited for; matrix products, arithmetic and copies ran while one was open for 5% of the time, Pallas kernels for 31%

profile of v1, /device:TPU:0, one launch (start us, length us, event | category | flops | bytes accessed | tf_op | source)
XLA Modules:
  0.0 110.8 jit_solution(9594983773629958082)
XLA Ops:
  0.6 3.0 %collective-permute-start.9 = (f32[16,3200]{1,0:T(8,128)}, f32[16,3200]{1,0:T(8,128)S(1)}, u32[]{:S(2)}, u32[]{:S(2)}) collective-permute-start(f32[16,3200]{1,0:T(8,128)} %bitcast.17), channel_id=1, source_target_pairs={{0,2},{1,3},{2,0},{3,1},{4,6},{5,7},{6,4},{7,5},{8,10},{9,11},{10,... | collective-permute-start | bytes 614408 | tf_op jit(solution)/shard_map/ppermute | solution.py:346
  3.6 1.5 %collective-permute-start.8 = (f32[16,3200]{1,0:T(8,128)}, f32[16,3200]{1,0:T(8,128)S(1)}, u32[]{:S(2)}, u32[]{:S(2)}) collective-permute-start(f32[16,3200]{1,0:T(8,128)} %bitcast.18), channel_id=1, source_target_pairs={{0,1},{1,0},{2,3},{3,2},{4,5},{5,4},{6,7},{7,6},{8,9},{9,8},{10,11... | collective-permute-start | bytes 614408 | tf_op jit(solution)/shard_map/ppermute | solution.py:346
  5.2 2.6 %collective-permute-start.3 = (f32[16,3200]{1,0:T(8,128)}, f32[16,3200]{1,0:T(8,128)S(1)}, u32[]{:S(2)}, u32[]{:S(2)}) collective-permute-start(f32[16,3200]{1,0:T(8,128)} %bitcast.20), channel_id=1, source_target_pairs={{0,8},{1,9},{2,10},{3,11},{4,12},{5,13},{6,14},{7,15},{8,0},{9,1},... | collective-permute-start | bytes 614408 | tf_op jit(solution)/shard_map/ppermute | solution.py:346
  9.6 0.9 copy.19
  11.3 5.7 %collective-permute-done.3.refs_4_ = f32[16,3200]{1,0:T(8,128)S(1)} collective-permute-done((f32[16,3200]{1,0:T(8,128)}, f32[16,3200]{1,0:T(8,128)S(1)}, u32[]{:S(2)}, u32[]{:S(2)}) %collective-permute-start.3) | collective-permute-done | bytes 204832 | tf_op jit(solution)/shard_map/ppermute | solution.py:346
  17.5 1.6 %collective-permute-start.7 = (f32[120,384]{1,0:T(8,128)S(1)}, f32[120,384]{1,0:T(8,128)S(1)}, u32[]{:S(2)}, u32[]{:S(2)}) collective-permute-start(f32[120,384]{1,0:T(8,128)S(1)} %maximum_maximum_fusion.refs_4_.refs_8_.pack), channel_id=1, source_target_pairs={{0,2},{1,3},{2,0},{3,1},{4,6},{5,7},{6,4},{7,5},{8,10},{9,11},{10,... | collective-permute-start | bytes 552968 | tf_op jit(solution)/shard_map/ppermute | solution.py:346
  19.8 6.6 %collective-permute-done.7.refs_5_.refs_9_ = f32[120,384]{1,0:T(8,128)S(1)} collective-permute-done((f32[120,384]{1,0:T(8,128)S(1)}, f32[120,384]{1,0:T(8,128)S(1)}, u32[]{:S(2)}, u32[]{:S(2)}) %collective-permute-start.7) | collective-permute-done | bytes 184352 | tf_op jit(solution)/shard_map/ppermute | solution.py:346
  26.6 1.7 %collective-permute-start.5 = (f32[16,3200]{1,0:T(8,128)S(1)}, f32[16,3200]{1,0:T(8,128)S(1)}, u32[]{:S(2)}, u32[]{:S(2)}) collective-permute-start(f32[16,3200]{1,0:T(8,128)S(1)} %collective-permute-done.3.refs_4_), channel_id=1, source_target_pairs={{0,4},{1,5},{2,6},{3,7},{4,0},{5,1},{6,2},{7,3},{8,12},{9,13},{10,... | collective-permute-start | bytes 614408 | tf_op jit(solution)/shard_map/ppermute | solution.py:346
  28.7 1.7 %collective-permute-start.6 = (f32[16,3200]{1,0:T(8,128)S(1)}, f32[16,3200]{1,0:T(8,128)S(1)}, u32[]{:S(2)}, u32[]{:S(2)}) collective-permute-start(f32[16,3200]{1,0:T(8,128)S(1)} %collective-permute-done.4.refs_5_), channel_id=1, source_target_pairs={{0,4},{1,5},{2,6},{3,7},{4,0},{5,1},{6,2},{7,3},{8,12},{9,13},{10,... | collective-permute-start | bytes 614408 | tf_op jit(solution)/shard_map/ppermute | solution.py:346
  31.1 9.7 %source_rows.1 = (bf16[1216,768]{1,0:T(8,128)(2,1)}, bf16[1216,768]{1,0:T(8,128)(2,1)}) custom-call(s32[3]{0:T(128)} %pad_add_fusion.me, f32[16,3200]{1,0:T(8,128)} %bitcast.19, f32[16,3200]{1,0:T(8,128)} %copy-done.8, f32[16,3200]{1,0:T(8,128)} %copy-done.7, f32[16,3200]{1,0:T(8,128)} %copy-done.10, f32[120,384]{1,0:T(8,128)} %copy-done.1, ...), custom_call_target="tpu_custom_call" | custom-call | flops 3000000000 | bytes 8000000 | tf_op jit(solution)/shard_map/source_rows/pallas_call | solution.py:374
  41.7 16.6 %weight_terms.1 = (f32[8,38,8,128]{3,2,1,0:T(8,128)}, f32[8,38,8,128]{3,2,1,0:T(8,128)}, bf16[2432,384]{1,0:T(8,128)(2,1)}, bf16[2432,384]{1,0:T(8,128)(2,1)}) custom-call(s32[3]{0:T(128)} %pad_add_fusion.me, f32[16,3200]{1,0:T(8,128)} %bitcast.23, f32[16,3200]{1,0:T(8,128)} %copy-done.6, f32[16,3200]{1,0:T(8,128)} %copy-done.11, f32[16,3200]{1,0:T(8,128)} %copy-done.13, ...), custom_call_target="tpu_custom_call" | custom-call | flops 8000000000 | bytes 12000000 | tf_op jit(solution)/shard_map/weight_terms/pallas_call | solution.py:396
  58.4 3.1 %collective-permute-done.12 = f32[8,38,8,128]{3,2,1,0:T(8,128)S(1)} collective-permute-done((f32[8,38,8,128]{3,2,1,0:T(8,128)}, f32[8,38,8,128]{3,2,1,0:T(8,128)S(1)}, u32[]{:S(2)}, u32[]{:S(2)}) %collective-permute-start.12) | collective-permute-done | bytes 1245216 | tf_op jit(solution)/shard_map/ppermute | solution.py:350
  61.5 1.4 %slice_add_fusion.1 = (f32[4,38,8,128]{3,2,1,0:T(8,128)S(1)}, f32[4,38,8,128]{3,2,1,0:T(8,128)S(1)}) fusion(f32[8,38,8,128]{3,2,1,0:T(8,128)S(1)} %collective-permute-done.12, f32[8,38,8,128]{3,2,1,0:T(8,128)} %get-tuple-element.21), kind=kLoop, calls=%fused_computation.1 | loop fusion | flops 311296 | bytes 3735552 | tf_op jit(solution)/shard_map/add | solution.py:425
  63.5 5.1 %back_zero.1.d0 = f32[640,384]{1,0:T(8,128)} custom-call(f32[640,640]{1,0:T(8,128)} %w.1, bf16[2432,384]{1,0:T(8,128)(2,1)} %get-tuple-element.19.uh, bf16[2432,384]{1,0:T(8,128)(2,1)} %get-tuple-element.20.ul), custom_call_target="tpu_custom_call" | custom-call | flops 1900000000 | bytes 4000000 | tf_op jit(solution)/shard_map/back_zero/pallas_call | solution.py:429
  68.6 4.7 %collective-permute-done.13 = f32[4,38,8,128]{3,2,1,0:T(8,128)S(1)} collective-permute-done((f32[4,38,8,128]{3,2,1,0:T(8,128)S(1)}, f32[4,38,8,128]{3,2,1,0:T(8,128)S(1)}, u32[]{:S(2)}, u32[]{:S(2)}) %collective-permute-start.13) | collective-permute-done | bytes 622624 | tf_op jit(solution)/shard_map/ppermute | solution.py:346
  73.7 5.8 %back_two.1.d2 = f32[768,384]{1,0:T(8,128)} custom-call(f32[384,384]{1,0:T(8,128)} %re.3, f32[384,384]{1,0:T(8,128)} %im.3, bf16[2432,384]{1,0:T(8,128)(2,1)} %get-tuple-element.19.uh, bf16[2432,384]{1,0:T(8,128)(2,1)} %get-tuple-element.20.ul), custom_call_target="tpu_custom_call" | custom-call | flops 1800000000 | bytes 4000000 | tf_op jit(solution)/shard_map/back_two/pallas_call | solution.py:437
  79.5 7.3 %back_one.1.d1 = f32[1024,384]{1,0:T(8,128)} custom-call(f32[512,512]{1,0:T(8,128)} %re.2, f32[512,512]{1,0:T(8,128)} %im.2, bf16[2432,384]{1,0:T(8,128)(2,1)} %get-tuple-element.19.uh, bf16[2432,384]{1,0:T(8,128)(2,1)} %get-tuple-element.20.ul), custom_call_target="tpu_custom_call" | custom-call | flops 3000000000 | bytes 5000000 | tf_op jit(solution)/shard_map/back_one/pallas_call | solution.py:433
  86.8 3.3 %collective-permute-start.15 = (f32[1,38,8,128]{3,2,1,0:T(8,128)S(1)}, f32[1,38,8,128]{3,2,1,0:T(8,128)S(1)}, u32[]{:S(2)}, u32[]{:S(2)}) collective-permute-start(f32[1,38,8,128]{3,2,1,0:T(8,128)S(1)} %slice_add_fusion.5), channel_id=1, source_target_pairs={{0,8},{1,9},{2,10},{3,11},{4,12},{5,13},{6,14},{7,15},{8,0},{9,1},... | collective-permute-start | bytes 466952 | tf_op jit(solution)/shard_map/ppermute | solution.py:346
  90.1 6.8 %source_sums.1 = f32[2,16,3200]{2,1,0:T(8,128)} custom-call(s32[3]{0:T(128)} %pad_add_fusion.me, f32[120,384]{1,0:T(8,128)} %copy-done.1, f32[640,384]{1,0:T(8,128)} %back_zero.1.d0, f32[1024,384]{1,0:T(8,128)} %back_one.1.d1, f32[768,384]{1,0:T(8,128)} %back_two.1.d2), custom_call_target="tpu_custom_call" | custom-call | flops 3000000000 | bytes 4000000 | tf_op jit(solution)/shard_map/source_sums/pallas_call | solution.py:441
  96.9 0.9 slice.57
  98.5 1.6 %collective-permute-start.16 = (f32[38,8,128]{2,1,0:T(8,128)S(1)}, f32[38,8,128]{2,1,0:T(8,128)S(1)}, u32[]{:S(2)}, u32[]{:S(2)}) collective-permute-start(f32[38,8,128]{2,1,0:T(8,128)S(1)} %fusion.1.refs_0_), channel_id=1, source_target_pairs={{0,1},{1,0},{2,3},{3,2},{4,5},{5,4},{6,7},{7,6},{8,9},{9,8},{10,11... | collective-permute-start | bytes 466952 | tf_op jit(solution)/shard_map/ppermute | solution.py:346
  100.0 5.7 %collective-permute-done.16.refs_1_ = f32[38,8,128]{2,1,0:T(8,128)S(1)} collective-permute-done((f32[38,8,128]{2,1,0:T(8,128)S(1)}, f32[38,8,128]{2,1,0:T(8,128)S(1)}, u32[]{:S(2)}, u32[]{:S(2)}) %collective-permute-start.16) | collective-permute-done | bytes 155680 | tf_op jit(solution)/shard_map/ppermute | solution.py:346
  105.7 1.7 %slice_add_fusion.4 = f32[1,16,3200]{2,1,0:T(8,128)} fusion(f32[1,16,3200]{2,1,0:T(8,128)S(1)} %collective-permute-done.11, f32[2,16,3200]{2,1,0:T(8,128)} %source_sums.1), kind=kLoop, calls=%fused_computation.4 | loop fusion | flops 51200 | bytes 614400 | tf_op jit(solution)/shard_map/add | solution.py:453
  108.7 2.0 %unpack.1 = (f32[80,640]{1,0:T(8,128)}, f32[64,512]{1,0:T(8,128)}, f32[64,512]{1,0:T(8,128)}, f32[48,384]{1,0:T(8,128)}, f32[48,384]{1,0:T(8,128)}) custom-call(s32[3]{0:T(128)} %pad_add_fusion.me, f32[38,8,128]{2,1,0:T(8,128)} %copy-done, f32[38,8,128]{2,1,0:T(8,128)} %copy-done.2, f32[38,8,128]{2,1,0:T(8,128)} %copy-done.3, f32[38,8,128]{2,1,0:T(8,128)} %copy-done.4), custom_call_target="tpu_custom_call" | custom-call | flops 1000000 | bytes 1500000 | tf_op jit(solution)/shard_map/unpack/pallas_call | solution.py:458
  (66 shorter events, 8.3 us)
Async XLA Ops:
  0.6 10.0 %collective-permute-start.9 = (f32[16,3200]{1,0:T(8,128)}, f32[16,3200]{1,0:T(8,128)S(1)}, u32[]{:S(2)}, u32[]{:S(2)}) collective-permute-start(f32[16,3200]{1,0:T(8,128)} %bitcast.17), channel_id=1, source_target_pairs={{0,2},{1,3},{2,0},{3,1},{4,6},{5,7},{6,4},{7,5},{8,10},{9,11},{10,... | collective-permute-start | bytes 614408 | tf_op jit(solution)/shard_map/ppermute | solution.py:346
  3.6 23.0 %collective-permute-start.8 = (f32[16,3200]{1,0:T(8,128)}, f32[16,3200]{1,0:T(8,128)S(1)}, u32[]{:S(2)}, u32[]{:S(2)}) collective-permute-start(f32[16,3200]{1,0:T(8,128)} %bitcast.18), channel_id=1, source_target_pairs={{0,1},{1,0},{2,3},{3,2},{4,5},{5,4},{6,7},{7,6},{8,9},{9,8},{10,11... | collective-permute-start | bytes 614408 | tf_op jit(solution)/shard_map/ppermute | solution.py:346
  5.2 11.8 %collective-permute-start.3 = (f32[16,3200]{1,0:T(8,128)}, f32[16,3200]{1,0:T(8,128)S(1)}, u32[]{:S(2)}, u32[]{:S(2)}) collective-permute-start(f32[16,3200]{1,0:T(8,128)} %bitcast.20), channel_id=1, source_target_pairs={{0,8},{1,9},{2,10},{3,11},{4,12},{5,13},{6,14},{7,15},{8,0},{9,1},... | collective-permute-start | bytes 614408 | tf_op jit(solution)/shard_map/ppermute | solution.py:346
  7.7 20.6 %collective-permute-start = (f32[16,3200]{1,0:T(8,128)}, f32[16,3200]{1,0:T(8,128)S(1)}, u32[]{:S(2)}, u32[]{:S(2)}) collective-permute-start(f32[16,3200]{1,0:T(8,128)} %bitcast.21), channel_id=1, source_target_pairs={{0,2},{1,3},{2,0},{3,1},{4,6},{5,7},{6,4},{7,5},{8,10},{9,11},{10,... | collective-permute-start | bytes 614408 | tf_op jit(solution)/shard_map/ppermute | solution.py:346
  10.7 19.7 %copy-start.7 = (f32[16,3200]{1,0:T(8,128)}, f32[16,3200]{1,0:T(8,128)S(1)}, u32[]{:S(2)}) copy-start(f32[16,3200]{1,0:T(8,128)S(1)} %collective-permute-done.9.refs_2_) | copy-start | bytes 614404
  10.7 19.7 %collective-permute-start.10 = (f32[16,3200]{1,0:T(8,128)S(1)}, f32[16,3200]{1,0:T(8,128)S(1)}, u32[]{:S(2)}, u32[]{:S(2)}) collective-permute-start(f32[16,3200]{1,0:T(8,128)S(1)} %collective-permute-done.9.refs_2_), channel_id=1, source_target_pairs={{0,1},{1,0},{2,3},{3,2},{4,5},{5,4},{6,7},{7,6},{8,9},{9,8},{10,11... | collective-permute-start | bytes 614408 | tf_op jit(solution)/shard_map/ppermute | solution.py:346
  16.9 23.9 %copy-start.5 = (f32[16,3200]{1,0:T(8,128)}, f32[16,3200]{1,0:T(8,128)S(1)}, u32[]{:S(2)}) copy-start(f32[16,3200]{1,0:T(8,128)S(1)} %collective-permute-done.3.refs_4_) | copy-start | bytes 614404
  16.9 11.7 %collective-permute-start.4 = (f32[16,3200]{1,0:T(8,128)S(1)}, f32[16,3200]{1,0:T(8,128)S(1)}, u32[]{:S(2)}, u32[]{:S(2)}) collective-permute-start(f32[16,3200]{1,0:T(8,128)S(1)} %collective-permute-done.3.refs_4_), channel_id=1, source_target_pairs={{0,2},{1,3},{2,0},{3,1},{4,6},{5,7},{6,4},{7,5},{8,10},{9,11},{10,... | collective-permute-start | bytes 614408 | tf_op jit(solution)/shard_map/ppermute | solution.py:346
  17.5 12.9 %copy-start.1 = (f32[120,384]{1,0:T(8,128)}, f32[120,384]{1,0:T(8,128)S(1)}, u32[]{:S(2)}) copy-start(f32[120,384]{1,0:T(8,128)S(1)} %maximum_maximum_fusion.refs_4_.refs_8_.pack) | copy-start | bytes 552964
  17.5 8.8 %collective-permute-start.7 = (f32[120,384]{1,0:T(8,128)S(1)}, f32[120,384]{1,0:T(8,128)S(1)}, u32[]{:S(2)}, u32[]{:S(2)}) collective-permute-start(f32[120,384]{1,0:T(8,128)S(1)} %maximum_maximum_fusion.refs_4_.refs_8_.pack), channel_id=1, source_target_pairs={{0,2},{1,3},{2,0},{3,1},{4,6},{5,7},{6,4},{7,5},{8,10},{9,11},{10,... | collective-permute-start | bytes 552968 | tf_op jit(solution)/shard_map/ppermute | solution.py:346
  26.3 14.5 %collective-permute-start.1 = (f32[16,3200]{1,0:T(8,128)}, f32[16,3200]{1,0:T(8,128)S(1)}, u32[]{:S(2)}, u32[]{:S(2)}) collective-permute-start(f32[16,3200]{1,0:T(8,128)} %bitcast.22), channel_id=1, source_target_pairs={{0,4},{1,5},{2,6},{3,7},{4,0},{5,1},{6,2},{7,3},{8,12},{9,13},{10,... | collective-permute-start | bytes 614408 | tf_op jit(solution)/shard_map/ppermute | solution.py:346
  26.6 14.2 %collective-permute-start.5 = (f32[16,3200]{1,0:T(8,128)S(1)}, f32[16,3200]{1,0:T(8,128)S(1)}, u32[]{:S(2)}, u32[]{:S(2)}) collective-permute-start(f32[16,3200]{1,0:T(8,128)S(1)} %collective-permute-done.3.refs_4_), channel_id=1, source_target_pairs={{0,4},{1,5},{2,6},{3,7},{4,0},{5,1},{6,2},{7,3},{8,12},{9,13},{10,... | collective-permute-start | bytes 614408 | tf_op jit(solution)/shard_map/ppermute | solution.py:346
  28.4 12.4 %copy-start.6 = (f32[16,3200]{1,0:T(8,128)}, f32[16,3200]{1,0:T(8,128)S(1)}, u32[]{:S(2)}) copy-start(f32[16,3200]{1,0:T(8,128)S(1)} %collective-permute-done.refs_1_) | copy-start | bytes 614404
  28.4 12.5 %collective-permute-start.2 = (f32[16,3200]{1,0:T(8,128)S(1)}, f32[16,3200]{1,0:T(8,128)S(1)}, u32[]{:S(2)}, u32[]{:S(2)}) collective-permute-start(f32[16,3200]{1,0:T(8,128)S(1)} %collective-permute-done.refs_1_), channel_id=1, source_target_pairs={{0,4},{1,5},{2,6},{3,7},{4,0},{5,1},{6,2},{7,3},{8,12},{9,13},{10,... | collective-permute-start | bytes 614408 | tf_op jit(solution)/shard_map/ppermute | solution.py:346
  28.7 12.2 %copy-start.9 = (f32[16,3200]{1,0:T(8,128)}, f32[16,3200]{1,0:T(8,128)S(1)}, u32[]{:S(2)}) copy-start(f32[16,3200]{1,0:T(8,128)S(1)} %collective-permute-done.4.refs_5_) | copy-start | bytes 614404
  28.7 12.2 %collective-permute-start.6 = (f32[16,3200]{1,0:T(8,128)S(1)}, f32[16,3200]{1,0:T(8,128)S(1)}, u32[]{:S(2)}, u32[]{:S(2)}) collective-permute-start(f32[16,3200]{1,0:T(8,128)S(1)} %collective-permute-done.4.refs_5_), channel_id=1, source_target_pairs={{0,4},{1,5},{2,6},{3,7},{4,0},{5,1},{6,2},{7,3},{8,12},{9,13},{10,... | collective-permute-start | bytes 614408 | tf_op jit(solution)/shard_map/ppermute | solution.py:346
  58.3 3.2 %collective-permute-start.12 = (f32[8,38,8,128]{3,2,1,0:T(8,128)}, f32[8,38,8,128]{3,2,1,0:T(8,128)S(1)}, u32[]{:S(2)}, u32[]{:S(2)}) collective-permute-start(f32[8,38,8,128]{3,2,1,0:T(8,128)} %get-tuple-element.22), channel_id=1, source_target_pairs={{0,16},{1,17},{2,18},{3,19},{4,20},{5,21},{6,22},{7,23},{8,24},{9,... | collective-permute-start | bytes 3735560 | tf_op jit(solution)/shard_map/ppermute | solution.py:350
  63.0 10.3 %collective-permute-start.13 = (f32[4,38,8,128]{3,2,1,0:T(8,128)S(1)}, f32[4,38,8,128]{3,2,1,0:T(8,128)S(1)}, u32[]{:S(2)}, u32[]{:S(2)}) collective-permute-start(f32[4,38,8,128]{3,2,1,0:T(8,128)S(1)} %get-tuple-element.29), channel_id=1, source_target_pairs={{0,1},{1,0},{2,3},{3,2},{4,5},{5,4},{6,7},{7,6},{8,9},{9,8},{10,11... | collective-permute-start | bytes 1867784 | tf_op jit(solution)/shard_map/ppermute | solution.py:346
  73.3 13.4 %collective-permute-start.14 = (f32[2,38,8,128]{3,2,1,0:T(8,128)S(1)}, f32[2,38,8,128]{3,2,1,0:T(8,128)S(1)}, u32[]{:S(2)}, u32[]{:S(2)}) collective-permute-start(f32[2,38,8,128]{3,2,1,0:T(8,128)S(1)} %get-tuple-element.31), channel_id=1, source_target_pairs={{0,4},{1,5},{2,6},{3,7},{4,0},{5,1},{6,2},{7,3},{8,12},{9,13},{10,... | collective-permute-start | bytes 933896 | tf_op jit(solution)/shard_map/ppermute | solution.py:346
  86.8 11.6 %collective-permute-start.15 = (f32[1,38,8,128]{3,2,1,0:T(8,128)S(1)}, f32[1,38,8,128]{3,2,1,0:T(8,128)S(1)}, u32[]{:S(2)}, u32[]{:S(2)}) collective-permute-start(f32[1,38,8,128]{3,2,1,0:T(8,128)S(1)} %slice_add_fusion.5), channel_id=1, source_target_pairs={{0,8},{1,9},{2,10},{3,11},{4,12},{5,13},{6,14},{7,15},{8,0},{9,1},... | collective-permute-start | bytes 466952 | tf_op jit(solution)/shard_map/ppermute | solution.py:346
  97.8 7.9 %collective-permute-start.11 = (f32[1,16,3200]{2,1,0:T(8,128)S(1)}, f32[1,16,3200]{2,1,0:T(8,128)S(1)}, u32[]{:S(2)}, u32[]{:S(2)}) collective-permute-start(f32[1,16,3200]{2,1,0:T(8,128)S(1)} %slice.57), channel_id=1, source_target_pairs={{0,1},{1,0},{2,3},{3,2},{4,5},{5,4},{6,7},{7,6},{8,9},{9,8},{10,11... | collective-permute-start | bytes 614408 | tf_op jit(solution)/shard_map/ppermute | solution.py:346
  98.5 7.3 %collective-permute-start.16 = (f32[38,8,128]{2,1,0:T(8,128)S(1)}, f32[38,8,128]{2,1,0:T(8,128)S(1)}, u32[]{:S(2)}, u32[]{:S(2)}) collective-permute-start(f32[38,8,128]{2,1,0:T(8,128)S(1)} %fusion.1.refs_0_), channel_id=1, source_target_pairs={{0,1},{1,0},{2,3},{3,2},{4,5},{5,4},{6,7},{7,6},{8,9},{9,8},{10,11... | collective-permute-start | bytes 466952 | tf_op jit(solution)/shard_map/ppermute | solution.py:346
  100.0 7.4 %collective-permute-start.17 = (f32[38,8,128]{2,1,0:T(8,128)S(1)}, f32[38,8,128]{2,1,0:T(8,128)S(1)}, u32[]{:S(2)}, u32[]{:S(2)}) collective-permute-start(f32[38,8,128]{2,1,0:T(8,128)S(1)} %fusion.1.refs_0_), channel_id=1, source_target_pairs={{0,16},{1,17},{2,18},{3,19},{4,20},{5,21},{6,22},{7,23},{8,24},{9,... | collective-permute-start | bytes 466952 | tf_op jit(solution)/shard_map/ppermute | solution.py:350
  105.7 1.7 %collective-permute-start.18 = (f32[38,8,128]{2,1,0:T(8,128)S(1)}, f32[38,8,128]{2,1,0:T(8,128)S(1)}, u32[]{:S(2)}, u32[]{:S(2)}) collective-permute-start(f32[38,8,128]{2,1,0:T(8,128)S(1)} %collective-permute-done.16.refs_1_), channel_id=1, source_target_pairs={{0,16},{1,17},{2,18},{3,19},{4,20},{5,21},{6,22},{7,23},{8,24},{9,... | collective-permute-start | bytes 466952 | tf_op jit(solution)/shard_map/ppermute | solution.py:350
  (11 other events, 23.7 us)

commit v2 on v1

--- a/solution.py
+++ b/solution.py
@@ -96,44 +96,40 @@
 
 
 def source_kernel(count, shard, own_slots, chans, me, *refs):
-    shards = (refs[:count], refs[count : 2 * count])
-    packs = refs[2 * count : 2 * count + 2]
-    high_out, low_out, feats, rot, full, picked = refs[2 * count + 2 :]
-    edges = packs[0].shape[1]
-    mine, owner = me[1], me[0]
+    shards = refs[:count]
+    pack = refs[count]
+    high_out, low_out, feats, rot, full, picked = refs[count + 1 :]
     rows = tuple(g * chans // (2 * own_slots) for g in GROUPS)
-    for tile in range(2):
-        select = onehot(packs[tile][ROT : ROT + 1, :], count * shard, shard, mine, None)
-        gather(shards[tile], select, feats, chans)
-        spread(packs[tile], rot)
-
-        def store(where, strip, lanes, value):
-            full[pl.ds(pl.multiple_of(where * chans + strip * 16, 16), 16), lanes] = value
-
-        rotate(rot, feats, 0, store, chans)
-        at = 0
-        for group in range(5):
-            for slot in range(own_slots):
-                owned = owner ^ (2 * slot)
-                source = pl.multiple_of(STARTS[group] * chans + owned * rows[group], 8)
-                picked[at : at + rows[group], :] = full[pl.ds(source, rows[group]), :]
-                at += rows[group]
-        high, low = split(picked[...])
-        high_out[:, tile * edges : (tile + 1) * edges] = high
-        low_out[:, tile * edges : (tile + 1) * edges] = low
+    select = onehot(pack[ROT : ROT + 1, :], count * shard, shard, me[1], None)
+    gather(shards, select, feats, chans)
+    spread(pack, rot)
+
+    def store(where, strip, lanes, value):
+        full[pl.ds(pl.multiple_of(where * chans + strip * 16, 16), 16), lanes] = value
+
+    rotate(rot, feats, 0, store, chans)
+    at = 0
+    for group in range(5):
+        for slot in range(own_slots):
+            owned = me[0] ^ (2 * slot)
+            source = pl.multiple_of(STARTS[group] * chans + owned * rows[group], 8)
+            picked[at : at + rows[group], :] = full[pl.ds(source, rows[group]), :]
+            at += rows[group]
+    high_out[...], low_out[...] = split(picked[...])
 
 
 def weight_kernel(count, shard, own_slots, parts, chans, me, *refs):
     shards = refs[:count]
     packs = refs[count : count + 2]
-    zh_any, zl_any = refs[count + 2 : count + 4]
-    keep_any, send_any, uh_any, ul_any = refs[count + 4 : count + 8]
-    feats, rot, zh, zl, uh, ul, full, load_sem, u_sem, out_sem = refs[count + 8 :]
+    z_any = refs[count + 2 : count + 6]
+    keep_any, send_any = refs[count + 6 : count + 8]
+    u_any = refs[count + 8 : count + 14]
+    feats, rot, zh, zl, uh, ul, full, load_sem, u_sem, out_sem = refs[count + 14 :]
     edges = packs[0].shape[1]
     owner, core, tgt = me[0], me[2], me[1]
     loads = [
-        pltpu.make_async_copy(zh_any, zh, load_sem.at[0]),
-        pltpu.make_async_copy(zl_any, zl, load_sem.at[1]),
+        pltpu.make_async_copy(z, half.at[:, tile * edges : (tile + 1) * edges], load_sem.at[k])
+        for k, (z, half, tile) in enumerate(zip(z_any, (zh, zl, zh, zl), (0, 0, 1, 1)))
     ]
     for load in loads:
         load.start()
@@ -152,21 +148,26 @@
         spread(packs[tile], rot)
         rotate(rot, feats, tile * edges, store, chans)
         if tile == 0:
-            saves = [
-                pltpu.make_async_copy(uh.at[:, 0:edges], uh_any, u_sem.at[0]),
-                pltpu.make_async_copy(ul.at[:, 0:edges], ul_any, u_sem.at[1]),
-            ]
+            saves = []
+            for k, first, last in ((0, 0, 5), (1, 5, 13), (2, 13, 19)):
+                for j, half in ((0, uh), (1, ul)):
+                    piece = half.at[first * chans : last * chans, 0:edges]
+                    at = 2 * k + j
+                    saves.append(pltpu.make_async_copy(piece, u_any[at], u_sem.at[at]))
             for save in saves:
                 save.start()
     for load in loads:
         load.wait()
 
-    def product(left, right):
-        lo = sum(GROUPS[:left]) * chans // 2, sum(GROUPS[: left + 1]) * chans // 2
-        ro = STARTS[right] * chans, (STARTS[right] + GROUPS[right]) * chans
-        a, b = zh[lo[0] : lo[1], :], uh[ro[0] : ro[1], :]
-        c, d = zl[lo[0] : lo[1], :], ul[ro[0] : ro[1], :]
-        return nt(a, b) + nt(a, d) + nt(c, b)
+    def product(*terms):
+        left, right = [], []
+        for a, b in ((zh, uh), (zh, ul), (zl, uh)):
+            for sign, z, u in terms:
+                first = sum(GROUPS[:z]) * chans // 2
+                value = a[first : first + GROUPS[z] * chans // 2, :]
+                left.append(value if sign > 0 else -value)
+                right.append(b[STARTS[u] * chans : (STARTS[u] + GROUPS[u]) * chans, :])
+        return nt(jnp.concatenate(left, 1), jnp.concatenate(right, 1))
 
     def put(at, value):
         wide = value.shape[1] // LANES
@@ -176,11 +177,11 @@
             full[:, at + col * high : at + (col + 1) * high] = block.reshape(own_slots, high, 8, LANES)
         return at + wide * high
 
-    at = put(0, product(0, 0))
-    at = put(at, product(1, 1) + product(2, 2))
-    at = put(at, product(1, 2) - product(2, 1))
-    at = put(at, product(3, 3) + product(4, 4))
-    at = put(at, product(3, 4) - product(4, 3))
+    at = put(0, product((1, 0, 0)))
+    at = put(at, product((1, 1, 1), (1, 2, 2)))
+    at = put(at, product((1, 1, 2), (-1, 2, 1)))
+    at = put(at, product((1, 3, 3), (1, 4, 4)))
+    at = put(at, product((1, 3, 4), (-1, 4, 3)))
     total = full.shape[1]
     if at < total:
         full[:, at:total] = jnp.zeros((own_slots, total - at, 8, LANES), F32)
@@ -203,27 +204,26 @@
         copy.wait()
 
 
-def dual(wh, wl, uh, ul):
-    return nn(wh, uh) + nn(wh, ul) + nn(wl, uh)
-
-
-def back_zero_kernel(chans, w, uh, ul, out):
+def back_zero_kernel(w, uh, ul, out):
     wh, wl = split(w[...])
-    out[...] = dual(wh, wl, uh[0 : 5 * chans, :], ul[0 : 5 * chans, :])
-
-
-def back_pair_kernel(first, groups, chans, re, im, uh, ul, out):
-    size = groups * chans
+    high, low = uh[...], ul[...]
+    out[...] = nn(jnp.concatenate([wh, wh, wl], 1), jnp.concatenate([high, low, high], 0))
+
+
+def back_pair_kernel(re, im, uh, ul, out):
+    size = re.shape[0]
     rh, rl = split(re[...])
     ih, il = split(im[...])
-    p = slice(first * chans, first * chans + size)
-    m = slice(first * chans + size, first * chans + 2 * size)
-    out[0:size, :] = dual(rh, rl, uh[p, :], ul[p, :]) + dual(ih, il, uh[m, :], ul[m, :])
-    out[size : 2 * size, :] = dual(rh, rl, uh[m, :], ul[m, :]) - dual(ih, il, uh[p, :], ul[p, :])
+    ph, mh = uh[0:size, :], uh[size : 2 * size, :]
+    pl_, ml = ul[0:size, :], ul[size : 2 * size, :]
+    w = jnp.concatenate([rh, ih, rh, ih, rl, il], 1)
+    out[0:size, :] = nn(w, jnp.concatenate([ph, mh, pl_, ml, ph, mh], 0))
+    out[size : 2 * size, :] = nn(w, jnp.concatenate([mh, -ph, ml, -pl_, mh, -ph], 0))
 
 
 def scatter_kernel(count, shard, chans, me, pack, d0, d1, d2, out, rot, back):
     select = onehot(pack[ROT : ROT + 1, :], count * shard, shard, me[1], None, False)
+    select = jnp.concatenate([select, select], 1)
     spread(pack, rot)
     edges = pack.shape[1]
     tiles = edges // LANES
@@ -258,7 +258,7 @@
     for level in range(5):
         first, last = level * level * chans, (level + 1) * (level + 1) * chans
         high, low = split(back[first:last, :])
-        total = nt(select, high) + nt(select, low)
+        total = nt(select, jnp.concatenate([high, low], 1))
         for part in range(count):
             out[part, :, first:last] = total[part * shard : (part + 1) * shard]
 
@@ -294,7 +294,7 @@
 SMEM = [pl.BlockSpec(memory_space=pltpu.SMEM)]
 
 
-def call(kernel, name, ins, outs, shapes, scratch, flops, moved):
+def call(kernel, name, ins, outs, shapes, scratch, micros, limit):
     return pl.pallas_call(
         kernel,
         name=name,
@@ -302,8 +302,10 @@
         out_specs=outs,
         out_shape=shapes,
         scratch_shapes=scratch,
-        compiler_params=pltpu.CompilerParams(vmem_limit_bytes=56 * 1024 * 1024),
-        cost_estimate=pl.CostEstimate(flops=flops, bytes_accessed=moved, transcendentals=0),
+        compiler_params=pltpu.CompilerParams(vmem_limit_bytes=limit * 1024 * 1024),
+        cost_estimate=pl.CostEstimate(
+            flops=int(micros * 1_150_000_000), bytes_accessed=100_000, transcendentals=0
+        ),
     )
 
 
@@ -371,21 +373,24 @@
 
     groups = sum(GROUPS) * chans
     z_rows = groups // 2
-    zh, zl = call(
-        functools.partial(source_kernel, ntgt, shard, slots, chans),
-        "source_rows",
-        SMEM + vmem(2 * ntgt + 2),
-        vmem(2),
-        [shape(z_rows, 2 * edges, dtype=BF16)] * 2,
-        [
-            pltpu.VMEM((feat, edges), F32),
-            pltpu.VMEM((ROT, 8, edges), F32),
-            pltpu.VMEM((groups, edges), F32),
-            pltpu.VMEM((z_rows, edges), F32),
-        ],
-        3_000_000_000,
-        8_000_000,
-    )(me, *x_parts, *y_parts, pack, pack_other)
+    z_tiles = [
+        call(
+            functools.partial(source_kernel, ntgt, shard, slots, chans),
+            "source_rows",
+            SMEM + vmem(ntgt + 1),
+            vmem(2),
+            [shape(z_rows, edges, dtype=BF16)] * 2,
+            [
+                pltpu.VMEM((feat, edges), F32),
+                pltpu.VMEM((ROT, 8, edges), F32),
+                pltpu.VMEM((groups, edges), F32),
+                pltpu.VMEM((z_rows, edges), F32),
+            ],
+            5,
+            24,
+        )(me, *parts, rows)
+        for parts, rows in ((x_parts, pack), (y_parts, pack_other))
+    ]
 
     per_slot = sum(
         (w.shape[0] // nsrc // 8) * (w.shape[1] // LANES)
@@ -393,12 +398,13 @@
     )
     piece = -(-per_slot // (reps * ntgt))
     subs = ntgt * slots
-    keep, send, uh, ul = call(
+    keep, send, *u = call(
         functools.partial(weight_kernel, nsrc, shard, slots, ntgt, chans),
         "weight_terms",
-        SMEM + vmem(nsrc + 2) + anywhere(2),
-        anywhere(4),
-        [shape(subs, piece, 8, LANES)] * 2 + [shape(groups, edges, dtype=BF16)] * 2,
+        SMEM + vmem(nsrc + 2) + anywhere(4),
+        anywhere(8),
+        [shape(subs, piece, 8, LANES)] * 2
+        + [shape(k * chans, edges, dtype=BF16) for k in (5, 5, 8, 8, 6, 6)],
         [
             pltpu.VMEM((feat, 2 * edges), F32),
             pltpu.VMEM((ROT, 8, edges), F32),
@@ -407,13 +413,13 @@
             pltpu.VMEM((groups, 2 * edges), BF16),
             pltpu.VMEM((groups, 2 * edges), BF16),
             pltpu.VMEM((slots, piece * reps * ntgt, 8, LANES), F32),
-            pltpu.SemaphoreType.DMA((2,)),
-            pltpu.SemaphoreType.DMA((2,)),
+            pltpu.SemaphoreType.DMA((4,)),
+            pltpu.SemaphoreType.DMA((6,)),
             pltpu.SemaphoreType.DMA((2 * subs,)),
         ],
-        8_000_000_000,
-        12_000_000,
-    )(me, *g_list, pack, pack_other, zh, zl)
+        14,
+        44,
+    )(me, *g_list, pack, pack_other, *z_tiles[0], *z_tiles[1])
 
     routes = [((0, 1), (2, 0)), ((2, 0), (0, 1))]
     routes += [((0, 1 << b),) * 2 for b in range(tgt_bits - 1, 0, -1)]
@@ -427,17 +433,14 @@
     final = held[0] + came[0]
 
     d0 = call(
-        functools.partial(back_zero_kernel, chans),
-        "back_zero", vmem(3), vmem(1)[0], shape(5 * chans, edges), [], 1_900_000_000, 4_000_000,
-    )(w_zero, uh, ul)
+        back_zero_kernel, "back_zero", vmem(3), vmem(1)[0], shape(5 * chans, edges), [], 3, 20
+    )(w_zero, *u[0:2])
     d1 = call(
-        functools.partial(back_pair_kernel, 5, 4, chans),
-        "back_one", vmem(4), vmem(1)[0], shape(8 * chans, edges), [], 3_000_000_000, 5_000_000,
-    )(w_one_re, w_one_im, uh, ul)
+        back_pair_kernel, "back_one", vmem(4), vmem(1)[0], shape(8 * chans, edges), [], 4, 24
+    )(w_one_re, w_one_im, *u[2:4])
     d2 = call(
-        functools.partial(back_pair_kernel, 13, 3, chans),
-        "back_two", vmem(4), vmem(1)[0], shape(6 * chans, edges), [], 1_800_000_000, 4_000_000,
-    )(w_two_re, w_two_im, uh, ul)
+        back_pair_kernel, "back_two", vmem(4), vmem(1)[0], shape(6 * chans, edges), [], 3, 20
+    )(w_two_re, w_two_im, *u[4:6])
     atoms = call(
         functools.partial(scatter_kernel, ntgt, shard, chans),
         "source_sums",
@@ -445,8 +448,8 @@
         vmem(1)[0],
         shape(ntgt, shard, feat),
         [pltpu.VMEM((ROT, 8, edges), F32), pltpu.VMEM((feat, edges), F32)],
-        3_000_000_000,
-        4_000_000,
+        5,
+        24,
     )(me, pack, d0, d1, d2)
     for b in range(tgt_bits - 1, -1, -1):
         half = atoms.shape[0] // 2
@@ -465,8 +468,8 @@
             for w in (w_zero, w_one_re, w_one_im, w_two_re, w_two_im)
         ],
         [pltpu.VMEM((piece * reps * ntgt, 8, LANES), F32)],
-        1_000_000,
-        1_500_000,
+        2,
+        8,
     )(me, *mine, *other)
     return (grad_feats, *outs)
 

time: 111 us -> 88.8 us (0.80)
  Pallas kernels: 53.2 us -> 35.6 us
  local copies, waits for them, and re-layouts: 4.79 us -> 2.04 us
  starting transfers between devices: 20.8 us -> 19.2 us
  other arithmetic: 4.71 us -> 3.23 us
  waiting for transfers between devices: 25.7 us -> 27.1 us
    pallas_call x3, Pallas kernels: 18.1 us -> 6.96 us  [the longest x1 3.46 us: local(): call(back_pair_kernel, 'back_one', vmem(4), vmem(1)[0], shape(8 * chans,...]
    pallas_call x1 -> x2, Pallas kernels: 9.67 us -> 7.14 us  [local(): call(functools.partial(source_kernel, ntgt, shard, slots, chans), 'source...]
    pallas_call x1, Pallas kernels: 6.78 us -> 4.34 us  [local(): call(functools.partial(scatter_kernel, ntgt, shard, chans), 'source_sums'...]
    unnamed x33 -> x15, local copies, waits for them, and re-layouts: 3.77 us -> 1.94 us
    ppermute x16, starting transfers between devices: 20.8 us -> 19.1 us  [hop(): return lax.ppermute(value, AXES, pairs)]
  transfers between devices with their start and end apart: 19 -> 19, of which waited for: 5 -> 9; matrix products, arithmetic and copies ran while one was open for 5% -> 3% of each run, Pallas kernels for 31% -> 21%
where the time goes in v2:
time: 88.8 us; the launch traced here: 88.6 us
  Pallas kernels  35.6 us (40%)
  waiting for transfers between devices  27.1 us (31%)
  starting transfers between devices  19.2 us (22%)
  other arithmetic  3.23 us (4%)
  local copies, waits for them, and re-layouts  2.04 us (2%)
  between operations  1.45 us (2%)
    ppermute x16, waiting for transfers between devices, hop(): return lax.ppermute(value, AXES, pairs)  23.3 us
    ppermute x16, starting transfers between devices, hop(): return lax.ppermute(value, AXES, pairs)  19.1 us
    pallas_call x1, Pallas kernels, local(): call(functools.partial(weight_kernel, nsrc, shard, slots, ntgt, chans), '...  15.7 us
    pallas_call x2, Pallas kernels, local(): call(functools.partial(source_kernel, ntgt, shard, slots, chans), 'source...  7.14 us
    pallas_call x1, Pallas kernels, local(): call(functools.partial(scatter_kernel, ntgt, shard, chans), 'source_sums'...  4.34 us
    ppermute x3, waiting for transfers between devices, cross(): lax.ppermute(value, AXES, [(i, (i + half) % (2 * half)) for i in range(2...  3.81 us
    pallas_call x1, Pallas kernels, local(): call(back_pair_kernel, 'back_one', vmem(4), vmem(1)[0], shape(8 * chans,...  3.46 us
    pallas_call x1, Pallas kernels, local(): call(back_pair_kernel, 'back_two', vmem(4), vmem(1)[0], shape(6 * chans,...  2.03 us
  transfers between devices with their start and end apart: 19, of which 9 were waited for; matrix products, arithmetic and copies ran while one was open for 3% of the time, Pallas kernels for 21%

profile of v2, /device:TPU:0, one launch (start us, length us, event | category | flops | bytes accessed | tf_op | source)
XLA Modules:
  0.0 88.6 jit_solution(17638527738103516165)
XLA Ops:
  0.6 3.0 %collective-permute-start.9 = (f32[16,3200]{1,0:T(8,128)}, f32[16,3200]{1,0:T(8,128)S(1)}, u32[]{:S(2)}, u32[]{:S(2)}) collective-permute-start(f32[16,3200]{1,0:T(8,128)} %bitcast.16), channel_id=1, source_target_pairs={{0,2},{1,3},{2,0},{3,1},{4,6},{5,7},{6,4},{7,5},{8,10},{9,11},{10,... | collective-permute-start | bytes 614408 | tf_op jit(solution)/shard_map/ppermute | solution.py:348
  3.6 1.5 %collective-permute-start.8 = (f32[16,3200]{1,0:T(8,128)}, f32[16,3200]{1,0:T(8,128)S(1)}, u32[]{:S(2)}, u32[]{:S(2)}) collective-permute-start(f32[16,3200]{1,0:T(8,128)} %bitcast.17), channel_id=1, source_target_pairs={{0,1},{1,0},{2,3},{3,2},{4,5},{5,4},{6,7},{7,6},{8,9},{9,8},{10,11... | collective-permute-start | bytes 614408 | tf_op jit(solution)/shard_map/ppermute | solution.py:348
  5.2 2.6 %collective-permute-start.3 = (f32[16,3200]{1,0:T(8,128)}, f32[16,3200]{1,0:T(8,128)S(1)}, u32[]{:S(2)}, u32[]{:S(2)}) collective-permute-start(f32[16,3200]{1,0:T(8,128)} %bitcast.19), channel_id=1, source_target_pairs={{0,8},{1,9},{2,10},{3,11},{4,12},{5,13},{6,14},{7,15},{8,0},{9,1},... | collective-permute-start | bytes 614408 | tf_op jit(solution)/shard_map/ppermute | solution.py:348
  7.7 1.6 %collective-permute-start.1 = (f32[16,3200]{1,0:T(8,128)}, f32[16,3200]{1,0:T(8,128)S(1)}, u32[]{:S(2)}, u32[]{:S(2)}) collective-permute-start(f32[16,3200]{1,0:T(8,128)} %bitcast.20), channel_id=1, source_target_pairs={{0,4},{1,5},{2,6},{3,7},{4,0},{5,1},{6,2},{7,3},{8,12},{9,13},{10,... | collective-permute-start | bytes 614408 | tf_op jit(solution)/shard_map/ppermute | solution.py:348
  12.4 1.6 %collective-permute-start.7 = (f32[120,384]{1,0:T(8,128)S(1)}, f32[120,384]{1,0:T(8,128)S(1)}, u32[]{:S(2)}, u32[]{:S(2)}) collective-permute-start(f32[120,384]{1,0:T(8,128)S(1)} %maximum_maximum_fusion.refs_2_.refs_8_.pack), channel_id=1, source_target_pairs={{0,2},{1,3},{2,0},{3,1},{4,6},{5,7},{6,4},{7,5},{8,10},{9,11},{10,... | collective-permute-start | bytes 552968 | tf_op jit(solution)/shard_map/ppermute | solution.py:348
  14.5 2.5 %collective-permute-done.3.refs_4_ = f32[16,3200]{1,0:T(8,128)S(1)} collective-permute-done((f32[16,3200]{1,0:T(8,128)}, f32[16,3200]{1,0:T(8,128)S(1)}, u32[]{:S(2)}, u32[]{:S(2)}) %collective-permute-start.3) | collective-permute-done | bytes 204832 | tf_op jit(solution)/shard_map/ppermute | solution.py:348
  18.5 3.6 %source_rows.2 = (bf16[1216,384]{1,0:T(8,128)(2,1)S(1)}, bf16[1216,384]{1,0:T(8,128)(2,1)S(1)}) custom-call(s32[3]{0:T(128)S(1)} %pad_add_fusion.me, f32[16,3200]{1,0:T(8,128)S(1)} %bitcast.18, f32[16,3200]{1,0:T(8,128)S(1)} %collective-permute-done.8.refs_1_, f32[120,384]{1,0:T(8,128)S(1)} %maximum_maximum_fusion.refs_2_.refs_8_.pack), custom_call_target="tpu_custom_call" | custom-call | flops 5750000128 | bytes 100000 | tf_op jit(solution)/shard_map/source_rows/pallas_call | solution.py:377
  22.9 1.3 %collective-permute-start.2 = (f32[16,3200]{1,0:T(8,128)S(1)}, f32[16,3200]{1,0:T(8,128)S(1)}, u32[]{:S(2)}, u32[]{:S(2)}) collective-permute-start(f32[16,3200]{1,0:T(8,128)S(1)} %collective-permute-done.refs_1_), channel_id=1, source_target_pairs={{0,4},{1,5},{2,6},{3,7},{4,0},{5,1},{6,2},{7,3},{8,12},{9,13},{10,... | collective-permute-start | bytes 614408 | tf_op jit(solution)/shard_map/ppermute | solution.py:348
  24.9 3.6 %source_rows.3 = (bf16[1216,384]{1,0:T(8,128)(2,1)S(1)}, bf16[1216,384]{1,0:T(8,128)(2,1)S(1)}) custom-call(s32[3]{0:T(128)S(1)} %pad_add_fusion.me, f32[16,3200]{1,0:T(8,128)S(1)} %collective-permute-done.9.refs_0_, f32[16,3200]{1,0:T(8,128)S(1)} %collective-permute-done.10.refs_1_, f32[120,384]{1,0:T(8,128)S(1)} %collective-permute-done.7.refs_2_.refs_9_), custom_call_target="tpu_custom_call" | custom-call | flops 5750000128 | bytes 100000 | tf_op jit(solution)/shard_map/source_rows/pallas_call | solution.py:377
  28.5 1.6 %collective-permute-done.2.refs_3_ = f32[16,3200]{1,0:T(8,128)S(1)} collective-permute-done((f32[16,3200]{1,0:T(8,128)S(1)}, f32[16,3200]{1,0:T(8,128)S(1)}, u32[]{:S(2)}, u32[]{:S(2)}) %collective-permute-start.2) | collective-permute-done | bytes 204832 | tf_op jit(solution)/shard_map/ppermute | solution.py:348
  30.1 2.2 %collective-permute-done.6.refs_7_ = f32[16,3200]{1,0:T(8,128)S(1)} collective-permute-done((f32[16,3200]{1,0:T(8,128)S(1)}, f32[16,3200]{1,0:T(8,128)S(1)}, u32[]{:S(2)}, u32[]{:S(2)}) %collective-permute-start.6) | collective-permute-done | bytes 204832 | tf_op jit(solution)/shard_map/ppermute | solution.py:348
  32.3 15.7 %weight_terms.1 = (f32[8,38,8,128]{3,2,1,0:T(8,128)}, f32[8,38,8,128]{3,2,1,0:T(8,128)}, bf16[640,384]{1,0:T(8,128)(2,1)S(1)}, bf16[640,384]{1,0:T(8,128)(2,1)S(...) custom-call(s32[3]{0:T(128)S(1)} %pad_add_fusion.me, ...), custom_call_target="tpu_custom_call" | custom-call | flops 16099999744 | bytes 100000 | tf_op jit(solution)/shard_map/weight_terms/pallas_call | solution.py:401
  48.1 3.1 %collective-permute-done.12 = f32[8,38,8,128]{3,2,1,0:T(8,128)S(1)} collective-permute-done((f32[8,38,8,128]{3,2,1,0:T(8,128)}, f32[8,38,8,128]{3,2,1,0:T(8,128)S(1)}, u32[]{:S(2)}, u32[]{:S(2)}) %collective-permute-start.12) | collective-permute-done | bytes 1245216 | tf_op jit(solution)/shard_map/ppermute | solution.py:352
  51.2 1.5 %slice_add_fusion.1 = (f32[4,38,8,128]{3,2,1,0:T(8,128)S(1)}, f32[4,38,8,128]{3,2,1,0:T(8,128)S(1)}) fusion(f32[8,38,8,128]{3,2,1,0:T(8,128)S(1)} %collective-permute-done.12, f32[8,38,8,128]{3,2,1,0:T(8,128)} %get-tuple-element.33), kind=kLoop, calls=%fused_computation.1 | loop fusion | flops 311296 | bytes 3735552 | tf_op jit(solution)/shard_map/add | solution.py:431
  53.3 1.5 %back_zero.1.d0 = f32[640,384]{1,0:T(8,128)S(1)} custom-call(f32[640,640]{1,0:T(8,128)S(1)} %copy-done, bf16[640,384]{1,0:T(8,128)(2,1)S(1)} %get-tuple-element.27.uh, bf16[640,384]{1,0:T(8,128)(2,1)S(1)} %get-tuple-element.28.ul), custom_call_target="tpu_custom_call" | custom-call | flops 3449999872 | bytes 100000 | tf_op jit(solution)/shard_map/back_zero/pallas_call | solution.py:435
  54.8 3.5 %back_one.1.d1 = f32[1024,384]{1,0:T(8,128)S(1)} custom-call(f32[512,512]{1,0:T(8,128)S(1)} %copy-done.1, f32[512,512]{1,0:T(8,128)S(1)} %copy-done.2, bf16[1024,384]{1,0:T(8,128)(2,1)S(1)} %get-tuple-element.29.uh, bf16[1024,384]{1,0:T(8,128)(2,1)S(1)} %get-tuple-element.30.ul), custom_call_target="tpu_custom_call" | custom-call | flops 4600000000 | bytes 100000 | tf_op jit(solution)/shard_map/back_one/pallas_call | solution.py:438
  58.3 4.8 %collective-permute-done.13 = f32[4,38,8,128]{3,2,1,0:T(8,128)S(1)} collective-permute-done((f32[4,38,8,128]{3,2,1,0:T(8,128)S(1)}, f32[4,38,8,128]{3,2,1,0:T(8,128)S(1)}, u32[]{:S(2)}, u32[]{:S(2)}) %collective-permute-start.13) | collective-permute-done | bytes 622624 | tf_op jit(solution)/shard_map/ppermute | solution.py:348
  63.9 2.0 %back_two.1.d2 = f32[768,384]{1,0:T(8,128)S(1)} custom-call(f32[384,384]{1,0:T(8,128)S(1)} %copy-done.3, f32[384,384]{1,0:T(8,128)S(1)} %copy-done.4, bf16[768,384]{1,0:T(8,128)(2,1)S(1)} %get-tuple-element.31.uh, bf16[768,384]{1,0:T(8,128)(2,1)S(1)} %get-tuple-element.32.ul), custom_call_target="tpu_custom_call" | custom-call | flops 3449999872 | bytes 100000 | tf_op jit(solution)/shard_map/back_two/pallas_call | solution.py:441
  66.0 4.1 %collective-permute-done.14 = f32[2,38,8,128]{3,2,1,0:T(8,128)S(1)} collective-permute-done((f32[2,38,8,128]{3,2,1,0:T(8,128)S(1)}, f32[2,38,8,128]{3,2,1,0:T(8,128)S(1)}, u32[]{:S(2)}, u32[]{:S(2)}) %collective-permute-start.14) | collective-permute-done | bytes 311328 | tf_op jit(solution)/shard_map/ppermute | solution.py:348
  70.1 2.1 %collective-permute-start.15 = (f32[1,38,8,128]{3,2,1,0:T(8,128)S(1)}, f32[1,38,8,128]{3,2,1,0:T(8,128)S(1)}, u32[]{:S(2)}, u32[]{:S(2)}) collective-permute-start(f32[1,38,8,128]{3,2,1,0:T(8,128)S(1)} %slice_add_fusion.5), channel_id=1, source_target_pairs={{0,8},{1,9},{2,10},{3,11},{4,12},{5,13},{6,14},{7,15},{8,0},{9,1},... | collective-permute-start | bytes 466952 | tf_op jit(solution)/shard_map/ppermute | solution.py:348
  72.2 4.3 %source_sums.1 = f32[2,16,3200]{2,1,0:T(8,128)S(1)} custom-call(s32[3]{0:T(128)S(1)} %pad_add_fusion.me, f32[120,384]{1,0:T(8,128)S(1)} %maximum_maximum_fusion.refs_2_.refs_8_.pack, f32[640,384]{1,0:T(8,128)S(1)} %back_zero.1.d0, f32[1024,384]{1,0:T(8,128)S(1)} %back_one.1.d1, f32[768,384]{1,0:T(8,128)S(1)} %back_two.1.d2), custom_call_target="tpu_custom_call" | custom-call | flops 5750000128 | bytes 100000 | tf_op jit(solution)/shard_map/source_sums/pallas_call | solution.py:444
  77.2 1.6 %collective-permute-done.15 = f32[1,38,8,128]{3,2,1,0:T(8,128)S(1)} collective-permute-done((f32[1,38,8,128]{3,2,1,0:T(8,128)S(1)}, f32[1,38,8,128]{3,2,1,0:T(8,128)S(1)}, u32[]{:S(2)}, u32[]{:S(2)}) %collective-permute-start.15) | collective-permute-done | bytes 155680 | tf_op jit(solution)/shard_map/ppermute | solution.py:348
  79.3 6.4 %collective-permute-done.16.refs_1_ = f32[38,8,128]{2,1,0:T(8,128)S(1)} collective-permute-done((f32[38,8,128]{2,1,0:T(8,128)S(1)}, f32[38,8,128]{2,1,0:T(8,128)S(1)}, u32[]{:S(2)}, u32[]{:S(2)}) %collective-permute-start.16) | collective-permute-done | bytes 155680 | tf_op jit(solution)/shard_map/ppermute | solution.py:348
  87.1 1.4 %unpack.1 = (f32[80,640]{1,0:T(8,128)}, f32[64,512]{1,0:T(8,128)}, f32[64,512]{1,0:T(8,128)}, f32[48,384]{1,0:T(8,128)}, f32[48,384]{1,0:T(8,128)}) custom-call(s32[3]{0:T(128)S(1)} %pad_add_fusion.me, f32[38,8,128]{2,1,0:T(8,128)S(1)} %fusion.1.refs_0_, f32[38,8,128]{2,1,0:T(8,128)S(1)} %collective-permute-done.16.refs_1_, ...), custom_call_target="tpu_custom_call" | custom-call | flops 2300000000 | bytes 100000 | tf_op jit(solution)/shard_map/unpack/pallas_call | solution.py:461
  (49 shorter events, 10.0 us)
Async XLA Ops:
  0.6 11.8 %collective-permute-start.9 = (f32[16,3200]{1,0:T(8,128)}, f32[16,3200]{1,0:T(8,128)S(1)}, u32[]{:S(2)}, u32[]{:S(2)}) collective-permute-start(f32[16,3200]{1,0:T(8,128)} %bitcast.16), channel_id=1, source_target_pairs={{0,2},{1,3},{2,0},{3,1},{4,6},{5,7},{6,4},{7,5},{8,10},{9,11},{10,... | collective-permute-start | bytes 614408 | tf_op jit(solution)/shard_map/ppermute | solution.py:348
  3.6 10.4 %collective-permute-start.8 = (f32[16,3200]{1,0:T(8,128)}, f32[16,3200]{1,0:T(8,128)S(1)}, u32[]{:S(2)}, u32[]{:S(2)}) collective-permute-start(f32[16,3200]{1,0:T(8,128)} %bitcast.17), channel_id=1, source_target_pairs={{0,1},{1,0},{2,3},{3,2},{4,5},{5,4},{6,7},{7,6},{8,9},{9,8},{10,11... | collective-permute-start | bytes 614408 | tf_op jit(solution)/shard_map/ppermute | solution.py:348
  5.2 11.9 %collective-permute-start.3 = (f32[16,3200]{1,0:T(8,128)}, f32[16,3200]{1,0:T(8,128)S(1)}, u32[]{:S(2)}, u32[]{:S(2)}) collective-permute-start(f32[16,3200]{1,0:T(8,128)} %bitcast.19), channel_id=1, source_target_pairs={{0,8},{1,9},{2,10},{3,11},{4,12},{5,13},{6,14},{7,15},{8,0},{9,1},... | collective-permute-start | bytes 614408 | tf_op jit(solution)/shard_map/ppermute | solution.py:348
  7.7 20.7 %collective-permute-start.1 = (f32[16,3200]{1,0:T(8,128)}, f32[16,3200]{1,0:T(8,128)S(1)}, u32[]{:S(2)}, u32[]{:S(2)}) collective-permute-start(f32[16,3200]{1,0:T(8,128)} %bitcast.20), channel_id=1, source_target_pairs={{0,4},{1,5},{2,6},{3,7},{4,0},{5,1},{6,2},{7,3},{8,12},{9,13},{10,... | collective-permute-start | bytes 614408 | tf_op jit(solution)/shard_map/ppermute | solution.py:348
  9.3 13.5 %collective-permute-start = (f32[16,3200]{1,0:T(8,128)}, f32[16,3200]{1,0:T(8,128)S(1)}, u32[]{:S(2)}, u32[]{:S(2)}) collective-permute-start(f32[16,3200]{1,0:T(8,128)} %bitcast.21), channel_id=1, source_target_pairs={{0,2},{1,3},{2,0},{3,1},{4,6},{5,7},{6,4},{7,5},{8,10},{9,11},{10,... | collective-permute-start | bytes 614408 | tf_op jit(solution)/shard_map/ppermute | solution.py:348
  12.4 9.6 %collective-permute-start.7 = (f32[120,384]{1,0:T(8,128)S(1)}, f32[120,384]{1,0:T(8,128)S(1)}, u32[]{:S(2)}, u32[]{:S(2)}) collective-permute-start(f32[120,384]{1,0:T(8,128)S(1)} %maximum_maximum_fusion.refs_2_.refs_8_.pack), channel_id=1, source_target_pairs={{0,2},{1,3},{2,0},{3,1},{4,6},{5,7},{6,4},{7,5},{8,10},{9,11},{10,... | collective-permute-start | bytes 552968 | tf_op jit(solution)/shard_map/ppermute | solution.py:348
  14.0 10.9 %collective-permute-start.10 = (f32[16,3200]{1,0:T(8,128)S(1)}, f32[16,3200]{1,0:T(8,128)S(1)}, u32[]{:S(2)}, u32[]{:S(2)}) collective-permute-start(f32[16,3200]{1,0:T(8,128)S(1)} %collective-permute-done.9.refs_0_), channel_id=1, source_target_pairs={{0,1},{1,0},{2,3},{3,2},{4,5},{5,4},{6,7},{7,6},{8,9},{9,8},{10,11... | collective-permute-start | bytes 614408 | tf_op jit(solution)/shard_map/ppermute | solution.py:348
  17.0 7.2 %collective-permute-start.4 = (f32[16,3200]{1,0:T(8,128)S(1)}, f32[16,3200]{1,0:T(8,128)S(1)}, u32[]{:S(2)}, u32[]{:S(2)}) collective-permute-start(f32[16,3200]{1,0:T(8,128)S(1)} %collective-permute-done.3.refs_4_), channel_id=1, source_target_pairs={{0,2},{1,3},{2,0},{3,1},{4,6},{5,7},{6,4},{7,5},{8,10},{9,11},{10,... | collective-permute-start | bytes 614408 | tf_op jit(solution)/shard_map/ppermute | solution.py:348
  22.1 10.2 %copy-start.6 = (f32[1,16,3200]{2,1,0:T(8,128)S(1)}, f32[1,16,3200]{2,1,0:T(8,128)}, u32[]{:S(2)}) copy-start(f32[1,16,3200]{2,1,0:T(8,128)} %param.12) | copy-start | bytes 614404
  22.1 6.4 %collective-permute-start.5 = (f32[16,3200]{1,0:T(8,128)S(1)}, f32[16,3200]{1,0:T(8,128)S(1)}, u32[]{:S(2)}, u32[]{:S(2)}) collective-permute-start(f32[16,3200]{1,0:T(8,128)S(1)} %collective-permute-done.3.refs_4_), channel_id=1, source_target_pairs={{0,4},{1,5},{2,6},{3,7},{4,0},{5,1},{6,2},{7,3},{8,12},{9,13},{10,... | collective-permute-start | bytes 614408 | tf_op jit(solution)/shard_map/ppermute | solution.py:348
  22.9 7.2 %collective-permute-start.2 = (f32[16,3200]{1,0:T(8,128)S(1)}, f32[16,3200]{1,0:T(8,128)S(1)}, u32[]{:S(2)}, u32[]{:S(2)}) collective-permute-start(f32[16,3200]{1,0:T(8,128)S(1)} %collective-permute-done.refs_1_), channel_id=1, source_target_pairs={{0,4},{1,5},{2,6},{3,7},{4,0},{5,1},{6,2},{7,3},{8,12},{9,13},{10,... | collective-permute-start | bytes 614408 | tf_op jit(solution)/shard_map/ppermute | solution.py:348
  24.2 8.1 %collective-permute-start.6 = (f32[16,3200]{1,0:T(8,128)S(1)}, f32[16,3200]{1,0:T(8,128)S(1)}, u32[]{:S(2)}, u32[]{:S(2)}) collective-permute-start(f32[16,3200]{1,0:T(8,128)S(1)} %collective-permute-done.4.refs_5_), channel_id=1, source_target_pairs={{0,4},{1,5},{2,6},{3,7},{4,0},{5,1},{6,2},{7,3},{8,12},{9,13},{10,... | collective-permute-start | bytes 614408 | tf_op jit(solution)/shard_map/ppermute | solution.py:348
  48.0 3.2 %collective-permute-start.12 = (f32[8,38,8,128]{3,2,1,0:T(8,128)}, f32[8,38,8,128]{3,2,1,0:T(8,128)S(1)}, u32[]{:S(2)}, u32[]{:S(2)}) collective-permute-start(f32[8,38,8,128]{3,2,1,0:T(8,128)} %get-tuple-element.34), channel_id=1, source_target_pairs={{0,16},{1,17},{2,18},{3,19},{4,20},{5,21},{6,22},{7,23},{8,24},{9,... | collective-permute-start | bytes 3735560 | tf_op jit(solution)/shard_map/ppermute | solution.py:352
  51.2 2.0 %copy-start = (f32[640,640]{1,0:T(8,128)S(1)}, f32[640,640]{1,0:T(8,128)}, u32[]{:S(2)}) copy-start(f32[640,640]{1,0:T(8,128)} %w.1) | copy-start | bytes 4915204
  52.8 10.3 %collective-permute-start.13 = (f32[4,38,8,128]{3,2,1,0:T(8,128)S(1)}, f32[4,38,8,128]{3,2,1,0:T(8,128)S(1)}, u32[]{:S(2)}, u32[]{:S(2)}) collective-permute-start(f32[4,38,8,128]{3,2,1,0:T(8,128)S(1)} %get-tuple-element.41), channel_id=1, source_target_pairs={{0,1},{1,0},{2,3},{3,2},{4,5},{5,4},{6,7},{7,6},{8,9},{9,8},{10,11... | collective-permute-start | bytes 1867784 | tf_op jit(solution)/shard_map/ppermute | solution.py:348
  53.3 1.5 %copy-start.2 = (f32[512,512]{1,0:T(8,128)S(1)}, f32[512,512]{1,0:T(8,128)}, u32[]{:S(2)}) copy-start(f32[512,512]{1,0:T(8,128)} %im.2) | copy-start | bytes 3145732
  58.3 5.7 %copy-start.3 = (f32[384,384]{1,0:T(8,128)S(1)}, f32[384,384]{1,0:T(8,128)}, u32[]{:S(2)}) copy-start(f32[384,384]{1,0:T(8,128)} %re.3) | copy-start | bytes 1769476
  58.3 5.6 %copy-start.4 = (f32[384,384]{1,0:T(8,128)S(1)}, f32[384,384]{1,0:T(8,128)}, u32[]{:S(2)}) copy-start(f32[384,384]{1,0:T(8,128)} %im.3) | copy-start | bytes 1769476
  63.1 7.0 %collective-permute-start.14 = (f32[2,38,8,128]{3,2,1,0:T(8,128)S(1)}, f32[2,38,8,128]{3,2,1,0:T(8,128)S(1)}, u32[]{:S(2)}, u32[]{:S(2)}) collective-permute-start(f32[2,38,8,128]{3,2,1,0:T(8,128)S(1)} %get-tuple-element.43), channel_id=1, source_target_pairs={{0,4},{1,5},{2,6},{3,7},{4,0},{5,1},{6,2},{7,3},{8,12},{9,13},{10,... | collective-permute-start | bytes 933896 | tf_op jit(solution)/shard_map/ppermute | solution.py:348
  70.1 8.7 %collective-permute-start.15 = (f32[1,38,8,128]{3,2,1,0:T(8,128)S(1)}, f32[1,38,8,128]{3,2,1,0:T(8,128)S(1)}, u32[]{:S(2)}, u32[]{:S(2)}) collective-permute-start(f32[1,38,8,128]{3,2,1,0:T(8,128)S(1)} %slice_add_fusion.5), channel_id=1, source_target_pairs={{0,8},{1,9},{2,10},{3,11},{4,12},{5,13},{6,14},{7,15},{8,0},{9,1},... | collective-permute-start | bytes 466952 | tf_op jit(solution)/shard_map/ppermute | solution.py:348
  76.6 9.2 %collective-permute-start.11 = (f32[1,16,3200]{2,1,0:T(8,128)S(1)}, f32[1,16,3200]{2,1,0:T(8,128)S(1)}, u32[]{:S(2)}, u32[]{:S(2)}) collective-permute-start(f32[1,16,3200]{2,1,0:T(8,128)S(1)} %slice.57), channel_id=1, source_target_pairs={{0,1},{1,0},{2,3},{3,2},{4,5},{5,4},{6,7},{7,6},{8,9},{9,8},{10,11... | collective-permute-start | bytes 614408 | tf_op jit(solution)/shard_map/ppermute | solution.py:348
  78.8 6.9 %collective-permute-start.16 = (f32[38,8,128]{2,1,0:T(8,128)S(1)}, f32[38,8,128]{2,1,0:T(8,128)S(1)}, u32[]{:S(2)}, u32[]{:S(2)}) collective-permute-start(f32[38,8,128]{2,1,0:T(8,128)S(1)} %fusion.1.refs_0_), channel_id=1, source_target_pairs={{0,1},{1,0},{2,3},{3,2},{4,5},{5,4},{6,7},{7,6},{8,9},{9,8},{10,11... | collective-permute-start | bytes 466952 | tf_op jit(solution)/shard_map/ppermute | solution.py:348
  79.3 7.1 %collective-permute-start.17 = (f32[38,8,128]{2,1,0:T(8,128)S(1)}, f32[38,8,128]{2,1,0:T(8,128)S(1)}, u32[]{:S(2)}, u32[]{:S(2)}) collective-permute-start(f32[38,8,128]{2,1,0:T(8,128)S(1)} %fusion.1.refs_0_), channel_id=1, source_target_pairs={{0,16},{1,17},{2,18},{3,19},{4,20},{5,21},{6,22},{7,23},{8,24},{9,... | collective-permute-start | bytes 466952 | tf_op jit(solution)/shard_map/ppermute | solution.py:352
  85.8 1.4 %collective-permute-start.18 = (f32[38,8,128]{2,1,0:T(8,128)S(1)}, f32[38,8,128]{2,1,0:T(8,128)S(1)}, u32[]{:S(2)}, u32[]{:S(2)}) collective-permute-start(f32[38,8,128]{2,1,0:T(8,128)S(1)} %collective-permute-done.16.refs_1_), channel_id=1, source_target_pairs={{0,16},{1,17},{2,18},{3,19},{4,20},{5,21},{6,22},{7,23},{8,24},{9,... | collective-permute-start | bytes 466952 | tf_op jit(solution)/shard_map/ppermute | solution.py:352
  (2 other events, 2.4 us)

commit v3 on v2

--- a/solution.py
+++ b/solution.py
@@ -10,6 +10,7 @@
 OFFSETS = (0, 1, 10, 35, 70)
 ROT = 115
 LANES = 128
+STRIP = 32
 AXES = ("rep", "src", "tgt")
 F32 = jnp.float32
 BF16 = jnp.bfloat16
@@ -63,8 +64,40 @@
 
 
 def spread(pack, out):
+    tiles = out.shape[2] // LANES
     for k in range(ROT):
-        out[k] = jnp.broadcast_to(pack[k : k + 1, :], (8, pack.shape[1]))
+        for t in range(tiles):
+            row = pack[k * tiles + t : k * tiles + t + 1, :]
+            out[k, :, t * LANES : (t + 1) * LANES] = jnp.broadcast_to(row, (8, LANES))
+
+
+def ends(pack, which, edges):
+    tiles = edges // LANES
+    at = (ROT + which) * tiles
+    return jnp.concatenate([pack[at + t : at + t + 1, :] for t in range(tiles)], 1)
+
+
+def prepare_kernel(count, rotation_any, source_any, target_any, pack, rotation, source, target, sems):
+    pairs = ((rotation_any, rotation), (source_any, source), (target_any, target))
+    copies = [pltpu.make_async_copy(a, b, sems.at[k]) for k, (a, b) in enumerate(pairs)]
+    for copy in copies:
+        copy.start()
+    for copy in copies:
+        copy.wait()
+    rows, edges = rotation.shape[2], rotation.shape[4]
+    tiles = edges // LANES
+    for k in range(rows):
+        for t in range(tiles):
+            at = k * tiles + t
+            pack[at : at + 1, :] = rotation[0, 0, k, :, t * LANES : (t + 1) * LANES]
+    slot = lax.broadcasted_iota(jnp.int32, (1, LANES), 1)
+    for which, end in enumerate((source, target)):
+        for t in range(tiles):
+            at = (rows + which) * tiles + t
+            value = end[0, 0, :, t * LANES : (t + 1) * LANES]
+            pack[at : at + 1, :] = jnp.where(slot + t * LANES < count[0, 0, 0], value, -1).astype(F32)
+    at = (rows + 2) * tiles
+    pack[at:, :] = jnp.zeros((pack.shape[0] - at, LANES), F32)
 
 
 def rotate(rot, feats, base, store, chans):
@@ -79,42 +112,70 @@
         for level in range(5):
             order = min(level, 2)
             cols = 2 * level + 1
-            acc = [[None, None] for _ in range(2 * order + 1)]
+            acc = [[None] * (STRIP // 8) for _ in range(2 * order + 1)]
             for c in range(cols):
-                row = pl.multiple_of((level * level + c) * chans + strip * 16, 16)
-                x = feats[pl.ds(row, 16), wide]
+                row = pl.multiple_of((level * level + c) * chans + strip * STRIP, STRIP)
+                x = feats[pl.ds(row, STRIP), wide]
                 for r in range(2 * order + 1):
                     factor = rot[OFFSETS[level] + r * cols + c, :, lanes]
-                    for half in range(2):
-                        term = factor * x[half * 8 : half * 8 + 8]
-                        acc[r][half] = term if c == 0 else acc[r][half] + term
+                    for part in range(STRIP // 8):
+                        term = factor * x[part * 8 : part * 8 + 8]
+                        acc[r][part] = term if c == 0 else acc[r][part] + term
             for r in range(2 * order + 1):
                 store(place(level, r - order), strip, wide, jnp.concatenate(acc[r], 0))
         return carry
 
-    lax.fori_loop(0, (chans // 16) * tiles, body, 0)
+    lax.fori_loop(0, (chans // STRIP) * tiles, body, 0)
 
 
 def source_kernel(count, shard, own_slots, chans, me, *refs):
     shards = refs[:count]
     pack = refs[count]
-    high_out, low_out, feats, rot, full, picked = refs[count + 1 :]
+    high_out, low_out, feats, rot, picked = refs[count + 1 :]
+    edges = rot.shape[2]
+    tiles = edges // LANES
     rows = tuple(g * chans // (2 * own_slots) for g in GROUPS)
-    select = onehot(pack[ROT : ROT + 1, :], count * shard, shard, me[1], None)
+    bases = tuple(sum(GROUPS[:g]) * chans // 2 for g in range(5))
+    select = onehot(ends(pack, 0, edges), count * shard, shard, me[1], None)
     gather(shards, select, feats, chans)
     spread(pack, rot)
-
-    def store(where, strip, lanes, value):
-        full[pl.ds(pl.multiple_of(where * chans + strip * 16, 16), 16), lanes] = value
-
-    rotate(rot, feats, 0, store, chans)
-    at = 0
-    for group in range(5):
-        for slot in range(own_slots):
-            owned = me[0] ^ (2 * slot)
-            source = pl.multiple_of(STARTS[group] * chans + owned * rows[group], 8)
-            picked[at : at + rows[group], :] = full[pl.ds(source, rows[group]), :]
-            at += rows[group]
+    parts = STRIP // 8
+    high = lax.shift_right_logical(me[0], 1)
+
+    def pick(parity):
+        for strip in range(chans // STRIP):
+
+            def body(tile, carry):
+                lanes = pl.ds(pl.multiple_of(tile * LANES, LANES), LANES)
+                for level in range(5):
+                    order = min(level, 2)
+                    cols = 2 * level + 1
+                    wanted = []
+                    for r in range(2 * order + 1):
+                        group = (0, 1, 3)[abs(r - order)] + (1 if r < order else 0)
+                        for part in range(parts):
+                            row = (level - abs(r - order)) * chans + strip * STRIP + part * 8
+                            owner, inner = divmod(row, rows[group])
+                            if owner % 2 == parity:
+                                wanted.append((r, part, group, owner // 2, inner))
+                    acc = {}
+                    for c in range(cols if wanted else 0):
+                        row = (level * level + c) * chans + strip * STRIP
+                        x = feats[row : row + STRIP, lanes]
+                        for r in sorted({w[0] for w in wanted}):
+                            factor = rot[OFFSETS[level] + r * cols + c, :, lanes]
+                            for part in (w[1] for w in wanted if w[0] == r):
+                                term = factor * x[part * 8 : part * 8 + 8]
+                                acc[r, part] = acc[r, part] + term if c else term
+                    for r, part, group, slot, inner in wanted:
+                        at = bases[group] + (slot ^ high) * rows[group] + inner
+                        picked[pl.ds(pl.multiple_of(at, 8), 8), lanes] = acc[r, part]
+                return carry
+
+            lax.fori_loop(0, tiles, body, 0)
+
+    for parity in range(2):
+        pl.when((me[0] & 1) == parity)(functools.partial(pick, parity))
     high_out[...], low_out[...] = split(picked[...])
 
 
@@ -125,7 +186,7 @@
     keep_any, send_any = refs[count + 6 : count + 8]
     u_any = refs[count + 8 : count + 14]
     feats, rot, zh, zl, uh, ul, full, load_sem, u_sem, out_sem = refs[count + 14 :]
-    edges = packs[0].shape[1]
+    edges = rot.shape[2]
     owner, core, tgt = me[0], me[2], me[1]
     loads = [
         pltpu.make_async_copy(z, half.at[:, tile * edges : (tile + 1) * edges], load_sem.at[k])
@@ -134,13 +195,13 @@
     for load in loads:
         load.start()
     select = jnp.concatenate(
-        [onehot(p[ROT + 1 : ROT + 2, :], count * shard, shard, owner, core) for p in packs], 1
+        [onehot(ends(p, 1, edges), count * shard, shard, owner, core) for p in packs], 1
     )
     gather(shards, select, feats, chans)
 
     def store(where, strip, lanes, value):
         high, low = split(value)
-        rows = pl.ds(pl.multiple_of(where * chans + strip * 16, 16), 16)
+        rows = pl.ds(pl.multiple_of(where * chans + strip * STRIP, STRIP), STRIP)
         uh[rows, lanes] = high
         ul[rows, lanes] = low
 
@@ -222,10 +283,10 @@
 
 
 def scatter_kernel(count, shard, chans, me, pack, d0, d1, d2, out, rot, back):
-    select = onehot(pack[ROT : ROT + 1, :], count * shard, shard, me[1], None, False)
+    edges = rot.shape[2]
+    select = onehot(ends(pack, 0, edges), count * shard, shard, me[1], None, False)
     select = jnp.concatenate([select, select], 1)
     spread(pack, rot)
-    edges = pack.shape[1]
     tiles = edges // LANES
     pieces = (d0, d1, d2)
     firsts = (0, 5, 13)
@@ -351,30 +412,47 @@
         half = nsrc * ntgt
         return lax.ppermute(value, AXES, [(i, (i + half) % (2 * half)) for i in range(2 * half)])
 
-    live = jnp.arange(edges, dtype=jnp.int32) < edge_count[0, 0, 0]
-    ends = jnp.stack([jnp.where(live, e[0, 0, 0], -1) for e in (edge_src, edge_tgt)]).astype(F32)
-    pack = jnp.concatenate([rotation[0, 0, 0], ends, jnp.zeros((3, edges), F32)], 0)
+    tiles = edges // LANES
+    length = -(-(ROT + 2) * tiles // 8) * 8
+    pack = call(
+        prepare_kernel,
+        "prepare",
+        SMEM + [pl.BlockSpec(memory_space=pltpu.HBM)] * 3,
+        vmem(1)[0],
+        shape(length, LANES),
+        [
+            pltpu.VMEM((1, 1, ROT, 1, edges), F32),
+            pltpu.VMEM((1, 1, 1, edges), jnp.int32),
+            pltpu.VMEM((1, 1, 1, edges), jnp.int32),
+            pltpu.SemaphoreType.DMA((3,)),
+        ],
+        2,
+        4,
+    )(edge_count, jnp.transpose(rotation, (0, 1, 3, 2, 4)), edge_src, edge_tgt)
     x_own = src_feats[0]
-    g_own = tgt_cotangent[0]
-
-    g_parts = {0: g_own}
+    g_parts = {0: tgt_cotangent[0]}
     for bit in range(src_bits - 1, 1, -1):
         for k, part in list(g_parts.items()):
             g_parts[k | (1 << bit)] = hop(part, None, (1 << bit, 0))
+    far = [k for k in g_parts if k > 0]
+    first, second = ((1, 0), (2, 0)), ((2, 0), (1, 0))
+    g_parts[1] = hop(g_parts[0], None, *first)
+    x_other = hop(x_own, None, (1, 0))
+    x_parts = [x_own] + [hop(x_own, None, (0, t)) for t in range(1, ntgt)]
+    g_parts[2] = hop(g_parts[0], None, *second)
+    arrived = [g_parts[k] for k in far]
     pack_other = hop(pack, None, (1, 0))
-    x_other = hop(x_own, None, (1, 0))
-    for k, part in list(g_parts.items()):
-        g_parts[k | 1] = hop(part, None, (1, 0), (2, 0))
-    x_parts = [x_own] + [hop(x_own, None, (0, t)) for t in range(1, ntgt)]
     y_parts = [x_other] + [hop(x_other, None, (0, t)) for t in range(1, ntgt)]
-    for k, part in list(g_parts.items()):
-        g_parts[k | 2] = hop(part, None, (2, 0), (1, 0))
-    g_list = [g_parts[k] for k in range(nsrc)]
-
+    g_parts[3] = hop(g_parts[1], None, *second)
+    for k, part in zip(far, arrived):
+        g_parts[k] = part
+        g_parts[k | 1] = hop(part, None, *first)
+        g_parts[k | 2] = hop(part, None, *second)
     groups = sum(GROUPS) * chans
     z_rows = groups // 2
-    z_tiles = [
-        call(
+
+    def source_rows(parts, rows):
+        return call(
             functools.partial(source_kernel, ntgt, shard, slots, chans),
             "source_rows",
             SMEM + vmem(ntgt + 1),
@@ -383,14 +461,19 @@
             [
                 pltpu.VMEM((feat, edges), F32),
                 pltpu.VMEM((ROT, 8, edges), F32),
-                pltpu.VMEM((groups, edges), F32),
                 pltpu.VMEM((z_rows, edges), F32),
             ],
-            5,
-            24,
+            2.5,
+            20,
         )(me, *parts, rows)
-        for parts, rows in ((x_parts, pack), (y_parts, pack_other))
-    ]
+
+    z_own = list(source_rows(x_parts, pack))
+    arrived = [g_parts[k | 1] for k in far]
+    for k, part in zip(far, arrived):
+        g_parts[k | 1] = part
+        g_parts[k | 3] = hop(part, None, *second)
+    z_other = source_rows(y_parts, pack_other)
+    g_list = [g_parts[k] for k in range(nsrc)]
 
     per_slot = sum(
         (w.shape[0] // nsrc // 8) * (w.shape[1] // LANES)
@@ -419,18 +502,7 @@
         ],
         14,
         44,
-    )(me, *g_list, pack, pack_other, *z_tiles[0], *z_tiles[1])
-
-    routes = [((0, 1), (2, 0)), ((2, 0), (0, 1))]
-    routes += [((0, 1 << b),) * 2 for b in range(tgt_bits - 1, 0, -1)]
-    routes += [((1 << b, 0),) * 2 for b in range(src_bits - 1, 1, -1)]
-    held, came = keep, cross(send)
-    for route in routes:
-        half = held.shape[0] // 2
-        sent = held[half:] + came[half:]
-        held = held[:half] + came[:half]
-        came = hop(sent, None, *route)
-    final = held[0] + came[0]
+    )(me, *g_list, pack, pack_other, *z_own, *z_other)
 
     d0 = call(
         back_zero_kernel, "back_zero", vmem(3), vmem(1)[0], shape(5 * chans, edges), [], 3, 20
@@ -441,16 +513,31 @@
     d2 = call(
         back_pair_kernel, "back_two", vmem(4), vmem(1)[0], shape(6 * chans, edges), [], 3, 20
     )(w_two_re, w_two_im, *u[4:6])
-    atoms = call(
-        functools.partial(scatter_kernel, ntgt, shard, chans),
-        "source_sums",
-        SMEM + vmem(4),
-        vmem(1)[0],
-        shape(ntgt, shard, feat),
-        [pltpu.VMEM((ROT, 8, edges), F32), pltpu.VMEM((feat, edges), F32)],
-        5,
-        24,
-    )(me, pack, d0, d1, d2)
+    routes = [((0, 1), (2, 0)), ((2, 0), (0, 1))]
+    routes += [((0, 1 << b),) * 2 for b in range(tgt_bits - 1, 0, -1)]
+    routes += [((1 << b, 0),) * 2 for b in range(src_bits - 1, 1, -1)]
+    held, came = keep, cross(send)
+    for k, route in enumerate(routes):
+        half = held.shape[0] // 2
+        sent = held[half:] + came[half:]
+        if k == 1:
+            sent, d0, d1, d2 = lax.optimization_barrier((sent, d0, d1, d2))
+            atoms = call(
+                functools.partial(scatter_kernel, ntgt, shard, chans),
+                "source_sums",
+                SMEM + vmem(4),
+                vmem(1)[0],
+                shape(ntgt, shard, feat),
+                [pltpu.VMEM((ROT, 8, edges), F32), pltpu.VMEM((feat, edges), F32)],
+                5,
+                24,
+            )(me, pack, d0, d1, d2)
+        if k == 2:
+            sent, atoms = lax.optimization_barrier((sent, atoms))
+        held = held[:half] + came[:half]
+        came = hop(sent, None, *route)
+    final = held[0] + came[0]
+
     for b in range(tgt_bits - 1, -1, -1):
         half = atoms.shape[0] // 2
         atoms = atoms[:half] + hop(atoms[half:], None, (0, 1 << b))

time: 88.8 us -> 83.4 us (0.939)
  waiting for transfers between devices: 27.1 us -> 24.8 us
  Pallas kernels: 35.6 us -> 33.4 us
  other arithmetic: 3.23 us -> 1.03 us
    pallas_call x2 -> x3, Pallas kernels: 7.14 us -> 5.32 us  [the longest x2 5.07 us: source_rows(): call(functools.partial(source_kernel, ntgt, shard, slots, chans), 'source...]
    ppermute x3, waiting for transfers between devices: 3.81 us -> 2.3 us  [cross(): lax.ppermute(value, AXES, [(i, (i + half) % (2 * half)) for i in range(2...]
    add x2, other arithmetic: 1.6 us -> 0.19 us  [local(): held = held[:half] + came[:half]]
    unnamed x15 -> x22, local copies, waits for them, and re-layouts: 1.94 us -> 2.9 us
  transfers between devices with their start and end apart: 19 -> 19, of which waited for: 9 -> 10; matrix products, arithmetic and copies ran while one was open for 3% -> 1% of each run, Pallas kernels for 21% -> 20%
where the time goes in v3:
time: 83.4 us; the launch traced here: 83.2 us
  Pallas kernels  33.4 us (40%)
  waiting for transfers between devices  24.8 us (30%)
  starting transfers between devices  19.5 us (23%)
  local copies, waits for them, and re-layouts  2.92 us (4%)
  between operations  1.45 us (2%)
  other arithmetic  1.03 us (1%)
    ppermute x16, waiting for transfers between devices, hop(): return lax.ppermute(value, AXES, pairs)  22.5 us
    ppermute x16, starting transfers between devices, hop(): return lax.ppermute(value, AXES, pairs)  19.5 us
    pallas_call x1, Pallas kernels, local(): call(functools.partial(weight_kernel, nsrc, shard, slots, ntgt, chans), '...  15.3 us
    pallas_call x2, Pallas kernels, source_rows(): call(functools.partial(source_kernel, ntgt, shard, slots, chans), 'source...  5.07 us
    pallas_call x1, Pallas kernels, local(): call(functools.partial(scatter_kernel, ntgt, shard, chans), 'source_sums'...  4.39 us
    pallas_call x1, Pallas kernels, local(): call(back_pair_kernel, 'back_one', vmem(4), vmem(1)[0], shape(8 * chans,...  3.45 us
    unnamed x22, local copies, waits for them, and re-layouts  2.9 us
    ppermute x3, waiting for transfers between devices, cross(): lax.ppermute(value, AXES, [(i, (i + half) % (2 * half)) for i in range(2...  2.3 us
  transfers between devices with their start and end apart: 19, of which 10 were waited for; matrix products, arithmetic and copies ran while one was open for 1% of the time, Pallas kernels for 20%

profile of v3, /device:TPU:0, one launch (start us, length us, event | category | flops | bytes accessed | tf_op | source)
XLA Modules:
  0.0 83.2 jit_solution(7496889221254253722)
XLA Ops:
  0.6 3.0 %collective-permute-start.9 = (f32[16,3200]{1,0:T(8,128)}, f32[16,3200]{1,0:T(8,128)S(1)}, u32[]{:S(2)}, u32[]{:S(2)}) collective-permute-start(f32[16,3200]{1,0:T(8,128)} %bitcast.8), channel_id=1, source_target_pairs={{0,2},{1,3},{2,0},{3,1},{4,6},{5,7},{6,4},{7,5},{8,10},{9,11},{10,... | collective-permute-start | bytes 614408 | tf_op jit(solution)/shard_map/ppermute | solution.py:409
  3.6 1.5 %collective-permute-start.8 = (f32[16,3200]{1,0:T(8,128)}, f32[16,3200]{1,0:T(8,128)S(1)}, u32[]{:S(2)}, u32[]{:S(2)}) collective-permute-start(f32[16,3200]{1,0:T(8,128)} %bitcast.9), channel_id=1, source_target_pairs={{0,1},{1,0},{2,3},{3,2},{4,5},{5,4},{6,7},{7,6},{8,9},{9,8},{10,11... | collective-permute-start | bytes 614408 | tf_op jit(solution)/shard_map/ppermute | solution.py:409
  5.2 2.6 %collective-permute-start.3 = (f32[16,3200]{1,0:T(8,128)}, f32[16,3200]{1,0:T(8,128)S(1)}, u32[]{:S(2)}, u32[]{:S(2)}) collective-permute-start(f32[16,3200]{1,0:T(8,128)} %bitcast.11), channel_id=1, source_target_pairs={{0,8},{1,9},{2,10},{3,11},{4,12},{5,13},{6,14},{7,15},{8,0},{9,1},... | collective-permute-start | bytes 614408 | tf_op jit(solution)/shard_map/ppermute | solution.py:409
  7.7 1.6 %collective-permute-start.1 = (f32[16,3200]{1,0:T(8,128)}, f32[16,3200]{1,0:T(8,128)S(1)}, u32[]{:S(2)}, u32[]{:S(2)}) collective-permute-start(f32[16,3200]{1,0:T(8,128)} %bitcast.12), channel_id=1, source_target_pairs={{0,4},{1,5},{2,6},{3,7},{4,0},{5,1},{6,2},{7,3},{8,12},{9,13},{10,... | collective-permute-start | bytes 614408 | tf_op jit(solution)/shard_map/ppermute | solution.py:409
  13.1 1.6 %collective-permute-start.7 = (f32[352,128]{1,0:T(8,128)S(1)}, f32[352,128]{1,0:T(8,128)S(1)}, u32[]{:S(2)}, u32[]{:S(2)}) collective-permute-start(f32[352,128]{1,0:T(8,128)S(1)} %prepare.1.refs_2_.refs_8_.pack), channel_id=1, source_target_pairs={{0,2},{1,3},{2,0},{3,1},{4,6},{5,7},{6,4},{7,5},{8,10},{9,11},{10,... | collective-permute-start | bytes 540680 | tf_op jit(solution)/shard_map/ppermute | solution.py:409
  15.2 1.8 %collective-permute-done.3.refs_4_ = f32[16,3200]{1,0:T(8,128)S(1)} collective-permute-done((f32[16,3200]{1,0:T(8,128)}, f32[16,3200]{1,0:T(8,128)S(1)}, u32[]{:S(2)}, u32[]{:S(2)}) %collective-permute-start.3) | collective-permute-done | bytes 204832 | tf_op jit(solution)/shard_map/ppermute | solution.py:409
  17.6 2.5 %source_rows.2 = (bf16[1216,384]{1,0:T(8,128)(2,1)S(1)}, bf16[1216,384]{1,0:T(8,128)(2,1)S(1)}) custom-call(s32[3]{0:T(128)S(1)} %pad_add_fusion.me, f32[16,3200]{1,0:T(8,128)S(1)} %bitcast.10, f32[16,3200]{1,0:T(8,128)S(1)} %collective-permute-done.8.refs_1_, f32[352,128]{1,0:T(8,128)S(1)} %prepare.1.refs_2_.refs_8_.pack), custom_call_target="tpu_custom_call" | custom-call | flops 2875000064 | bytes 100000 | tf_op jit(solution)/shard_map/source_rows/pallas_call | solution.py:455
  20.9 1.3 %collective-permute-start.2 = (f32[16,3200]{1,0:T(8,128)S(1)}, f32[16,3200]{1,0:T(8,128)S(1)}, u32[]{:S(2)}, u32[]{:S(2)}) collective-permute-start(f32[16,3200]{1,0:T(8,128)S(1)} %collective-permute-done.refs_1_), channel_id=1, source_target_pairs={{0,4},{1,5},{2,6},{3,7},{4,0},{5,1},{6,2},{7,3},{8,12},{9,13},{10,... | collective-permute-start | bytes 614408 | tf_op jit(solution)/shard_map/ppermute | solution.py:409
  22.8 1.1 %collective-permute-start.6 = (f32[16,3200]{1,0:T(8,128)S(1)}, f32[16,3200]{1,0:T(8,128)S(1)}, u32[]{:S(2)}, u32[]{:S(2)}) collective-permute-start(f32[16,3200]{1,0:T(8,128)S(1)} %collective-permute-done.4.refs_5_), channel_id=1, source_target_pairs={{0,4},{1,5},{2,6},{3,7},{4,0},{5,1},{6,2},{7,3},{8,12},{9,13},{10,... | collective-permute-start | bytes 614408 | tf_op jit(solution)/shard_map/ppermute | solution.py:409
  23.9 2.5 %source_rows.3 = (bf16[1216,384]{1,0:T(8,128)(2,1)S(1)}, bf16[1216,384]{1,0:T(8,128)(2,1)S(1)}) custom-call(s32[3]{0:T(128)S(1)} %pad_add_fusion.me, f32[16,3200]{1,0:T(8,128)S(1)} %collective-permute-done.9.refs_0_, f32[16,3200]{1,0:T(8,128)S(1)} %collective-permute-done.10.refs_1_, f32[352,128]{1,0:T(8,128)S(1)} %collective-permute-done.7.refs_2_.refs_9_), custom_call_target="tpu_custom_call" | custom-call | flops 2875000064 | bytes 100000 | tf_op jit(solution)/shard_map/source_rows/pallas_call | solution.py:455
  26.5 1.7 %collective-permute-done.2.refs_3_ = f32[16,3200]{1,0:T(8,128)S(1)} collective-permute-done((f32[16,3200]{1,0:T(8,128)S(1)}, f32[16,3200]{1,0:T(8,128)S(1)}, u32[]{:S(2)}, u32[]{:S(2)}) %collective-permute-start.2) | collective-permute-done | bytes 204832 | tf_op jit(solution)/shard_map/ppermute | solution.py:409
  28.1 2.2 %collective-permute-done.6.refs_7_ = f32[16,3200]{1,0:T(8,128)S(1)} collective-permute-done((f32[16,3200]{1,0:T(8,128)S(1)}, f32[16,3200]{1,0:T(8,128)S(1)}, u32[]{:S(2)}, u32[]{:S(2)}) %collective-permute-start.6) | collective-permute-done | bytes 204832 | tf_op jit(solution)/shard_map/ppermute | solution.py:409
  30.3 15.3 %weight_terms.1 = (f32[8,38,8,128]{3,2,1,0:T(8,128)}, f32[8,38,8,128]{3,2,1,0:T(8,128)}, bf16[640,384]{1,0:T(8,128)(2,1)S(1)}, bf16[640,384]{1,0:T(8,128)(2,1)S(...) custom-call(s32[3]{0:T(128)S(1)} %pad_add_fusion.me, ...), custom_call_target="tpu_custom_call" | custom-call | flops 16099999744 | bytes 100000 | tf_op jit(solution)/shard_map/weight_terms/pallas_call | solution.py:484
  45.8 1.5 %back_zero.1.d0 = f32[640,384]{1,0:T(8,128)S(1)} custom-call(f32[640,640]{1,0:T(8,128)S(1)} %copy-done, bf16[640,384]{1,0:T(8,128)(2,1)S(1)} %get-tuple-element.35.uh, bf16[640,384]{1,0:T(8,128)(2,1)S(1)} %get-tuple-element.36.ul), custom_call_target="tpu_custom_call" | custom-call | flops 3449999872 | bytes 100000 | tf_op jit(solution)/shard_map/back_zero/pallas_call | solution.py:507
  47.2 1.6 %collective-permute-done.11 = f32[8,38,8,128]{3,2,1,0:T(8,128)S(1)} collective-permute-done((f32[8,38,8,128]{3,2,1,0:T(8,128)}, f32[8,38,8,128]{3,2,1,0:T(8,128)S(1)}, u32[]{:S(2)}, u32[]{:S(2)}) %collective-permute-start.11) | collective-permute-done | bytes 1245216 | tf_op jit(solution)/shard_map/ppermute | solution.py:413
  50.1 2.0 %back_two.1.d2 = f32[768,384]{1,0:T(8,128)S(1)} custom-call(f32[384,384]{1,0:T(8,128)S(1)} %copy-done.3, f32[384,384]{1,0:T(8,128)S(1)} %copy-done.4, bf16[768,384]{1,0:T(8,128)(2,1)S(1)} %get-tuple-element.39.uh, bf16[768,384]{1,0:T(8,128)(2,1)S(1)} %get-tuple-element.40.ul), custom_call_target="tpu_custom_call" | custom-call | flops 3449999872 | bytes 100000 | tf_op jit(solution)/shard_map/back_two/pallas_call | solution.py:513
  52.2 3.5 %back_one.1.d1 = f32[1024,384]{1,0:T(8,128)S(1)} custom-call(f32[512,512]{1,0:T(8,128)S(1)} %copy-done.1, f32[512,512]{1,0:T(8,128)S(1)} %copy-done.2, bf16[1024,384]{1,0:T(8,128)(2,1)S(1)} %get-tuple-element.37.uh, bf16[1024,384]{1,0:T(8,128)(2,1)S(1)} %get-tuple-element.38.ul), custom_call_target="tpu_custom_call" | custom-call | flops 4600000000 | bytes 100000 | tf_op jit(solution)/shard_map/back_one/pallas_call | solution.py:510
  55.6 3.7 %collective-permute-done.12 = f32[4,38,8,128]{3,2,1,0:T(8,128)S(1)} collective-permute-done((f32[4,38,8,128]{3,2,1,0:T(8,128)S(1)}, f32[4,38,8,128]{3,2,1,0:T(8,128)S(1)}, u32[]{:S(2)}, u32[]{:S(2)}) %collective-permute-start.12) | collective-permute-done | bytes 622624 | tf_op jit(solution)/shard_map/ppermute | solution.py:409
  60.2 4.4 %source_sums.1 = f32[2,16,3200]{2,1,0:T(8,128)S(1)} custom-call(s32[3]{0:T(128)S(1)} %pad_add_fusion.me, f32[352,128]{1,0:T(8,128)S(1)} %prepare.1.refs_2_.refs_8_.pack, f32[640,384]{1,0:T(8,128)S(1)} %back_zero.1.d0, f32[1024,384]{1,0:T(8,128)S(1)} %back_one.1.d1, f32[768,384]{1,0:T(8,128)S(1)} %back_two.1.d2), custom_call_target="tpu_custom_call" | custom-call | flops 5750000128 | bytes 100000 | tf_op jit(solution)/shard_map/source_sums/pallas_call | solution.py:525
  64.6 1.8 %collective-permute-done.13 = f32[2,38,8,128]{3,2,1,0:T(8,128)S(1)} collective-permute-done((f32[2,38,8,128]{3,2,1,0:T(8,128)S(1)}, f32[2,38,8,128]{3,2,1,0:T(8,128)S(1)}, u32[]{:S(2)}, u32[]{:S(2)}) %collective-permute-start.13) | collective-permute-done | bytes 311328 | tf_op jit(solution)/shard_map/ppermute | solution.py:409
  66.4 2.1 %collective-permute-start.15 = (f32[1,38,8,128]{3,2,1,0:T(8,128)S(1)}, f32[1,38,8,128]{3,2,1,0:T(8,128)S(1)}, u32[]{:S(2)}, u32[]{:S(2)}) collective-permute-start(f32[1,38,8,128]{3,2,1,0:T(8,128)S(1)} %slice_add_fusion.6), channel_id=1, source_target_pairs={{0,8},{1,9},{2,10},{3,11},{4,12},{5,13},{6,14},{7,15},{8,0},{9,1},... | collective-permute-start | bytes 466952 | tf_op jit(solution)/shard_map/ppermute | solution.py:409
  69.1 6.0 %collective-permute-done.15 = f32[1,38,8,128]{3,2,1,0:T(8,128)S(1)} collective-permute-done((f32[1,38,8,128]{3,2,1,0:T(8,128)S(1)}, f32[1,38,8,128]{3,2,1,0:T(8,128)S(1)}, u32[]{:S(2)}, u32[]{:S(2)}) %collective-permute-start.15) | collective-permute-done | bytes 155680 | tf_op jit(solution)/shard_map/ppermute | solution.py:409
  75.6 4.8 %collective-permute-done.16.refs_1_ = f32[38,8,128]{2,1,0:T(8,128)S(1)} collective-permute-done((f32[38,8,128]{2,1,0:T(8,128)S(1)}, f32[38,8,128]{2,1,0:T(8,128)S(1)}, u32[]{:S(2)}, u32[]{:S(2)}) %collective-permute-start.16) | collective-permute-done | bytes 155680 | tf_op jit(solution)/shard_map/ppermute | solution.py:409
  81.7 1.4 %unpack.1 = (f32[80,640]{1,0:T(8,128)}, f32[64,512]{1,0:T(8,128)}, f32[64,512]{1,0:T(8,128)}, f32[48,384]{1,0:T(8,128)}, f32[48,384]{1,0:T(8,128)}) custom-call(s32[3]{0:T(128)S(1)} %pad_add_fusion.me, f32[38,8,128]{2,1,0:T(8,128)S(1)} %fusion.1.refs_0_, f32[38,8,128]{2,1,0:T(8,128)S(1)} %collective-permute-done.16.refs_1_, ...), custom_call_target="tpu_custom_call" | custom-call | flops 2300000000 | bytes 100000 | tf_op jit(solution)/shard_map/unpack/pallas_call | solution.py:548
  (52 shorter events, 10.3 us)
Async XLA Ops:
  0.6 12.5 %collective-permute-start.9 = (f32[16,3200]{1,0:T(8,128)}, f32[16,3200]{1,0:T(8,128)S(1)}, u32[]{:S(2)}, u32[]{:S(2)}) collective-permute-start(f32[16,3200]{1,0:T(8,128)} %bitcast.8), channel_id=1, source_target_pairs={{0,2},{1,3},{2,0},{3,1},{4,6},{5,7},{6,4},{7,5},{8,10},{9,11},{10,... | collective-permute-start | bytes 614408 | tf_op jit(solution)/shard_map/ppermute | solution.py:409
  3.6 11.1 %collective-permute-start.8 = (f32[16,3200]{1,0:T(8,128)}, f32[16,3200]{1,0:T(8,128)S(1)}, u32[]{:S(2)}, u32[]{:S(2)}) collective-permute-start(f32[16,3200]{1,0:T(8,128)} %bitcast.9), channel_id=1, source_target_pairs={{0,1},{1,0},{2,3},{3,2},{4,5},{5,4},{6,7},{7,6},{8,9},{9,8},{10,11... | collective-permute-start | bytes 614408 | tf_op jit(solution)/shard_map/ppermute | solution.py:409
  5.2 11.9 %collective-permute-start.3 = (f32[16,3200]{1,0:T(8,128)}, f32[16,3200]{1,0:T(8,128)S(1)}, u32[]{:S(2)}, u32[]{:S(2)}) collective-permute-start(f32[16,3200]{1,0:T(8,128)} %bitcast.11), channel_id=1, source_target_pairs={{0,8},{1,9},{2,10},{3,11},{4,12},{5,13},{6,14},{7,15},{8,0},{9,1},... | collective-permute-start | bytes 614408 | tf_op jit(solution)/shard_map/ppermute | solution.py:409
  7.7 18.7 %collective-permute-start.1 = (f32[16,3200]{1,0:T(8,128)}, f32[16,3200]{1,0:T(8,128)S(1)}, u32[]{:S(2)}, u32[]{:S(2)}) collective-permute-start(f32[16,3200]{1,0:T(8,128)} %bitcast.12), channel_id=1, source_target_pairs={{0,4},{1,5},{2,6},{3,7},{4,0},{5,1},{6,2},{7,3},{8,12},{9,13},{10,... | collective-permute-start | bytes 614408 | tf_op jit(solution)/shard_map/ppermute | solution.py:409
  9.3 11.6 %collective-permute-start = (f32[16,3200]{1,0:T(8,128)}, f32[16,3200]{1,0:T(8,128)S(1)}, u32[]{:S(2)}, u32[]{:S(2)}) collective-permute-start(f32[16,3200]{1,0:T(8,128)} %bitcast.13), channel_id=1, source_target_pairs={{0,2},{1,3},{2,0},{3,1},{4,6},{5,7},{6,4},{7,5},{8,10},{9,11},{10,... | collective-permute-start | bytes 614408 | tf_op jit(solution)/shard_map/ppermute | solution.py:409
  12.9 4.7 %copy-start.5 = (f32[1,16,3200]{2,1,0:T(8,128)S(1)}, f32[1,16,3200]{2,1,0:T(8,128)}, u32[]{:S(2)}) copy-start(f32[1,16,3200]{2,1,0:T(8,128)} %param.11) | copy-start | bytes 614404
  13.1 7.0 %collective-permute-start.7 = (f32[352,128]{1,0:T(8,128)S(1)}, f32[352,128]{1,0:T(8,128)S(1)}, u32[]{:S(2)}, u32[]{:S(2)}) collective-permute-start(f32[352,128]{1,0:T(8,128)S(1)} %prepare.1.refs_2_.refs_8_.pack), channel_id=1, source_target_pairs={{0,2},{1,3},{2,0},{3,1},{4,6},{5,7},{6,4},{7,5},{8,10},{9,11},{10,... | collective-permute-start | bytes 540680 | tf_op jit(solution)/shard_map/ppermute | solution.py:409
  14.7 9.2 %collective-permute-start.10 = (f32[16,3200]{1,0:T(8,128)S(1)}, f32[16,3200]{1,0:T(8,128)S(1)}, u32[]{:S(2)}, u32[]{:S(2)}) collective-permute-start(f32[16,3200]{1,0:T(8,128)S(1)} %collective-permute-done.9.refs_0_), channel_id=1, source_target_pairs={{0,1},{1,0},{2,3},{3,2},{4,5},{5,4},{6,7},{7,6},{8,9},{9,8},{10,11... | collective-permute-start | bytes 614408 | tf_op jit(solution)/shard_map/ppermute | solution.py:409
  17.0 5.8 %collective-permute-start.4 = (f32[16,3200]{1,0:T(8,128)S(1)}, f32[16,3200]{1,0:T(8,128)S(1)}, u32[]{:S(2)}, u32[]{:S(2)}) collective-permute-start(f32[16,3200]{1,0:T(8,128)S(1)} %collective-permute-done.3.refs_4_), channel_id=1, source_target_pairs={{0,2},{1,3},{2,0},{3,1},{4,6},{5,7},{6,4},{7,5},{8,10},{9,11},{10,... | collective-permute-start | bytes 614408 | tf_op jit(solution)/shard_map/ppermute | solution.py:409
  20.1 10.2 %copy-start.6 = (f32[1,16,3200]{2,1,0:T(8,128)S(1)}, f32[1,16,3200]{2,1,0:T(8,128)}, u32[]{:S(2)}) copy-start(f32[1,16,3200]{2,1,0:T(8,128)} %param.12) | copy-start | bytes 614404
  20.1 6.3 %collective-permute-start.5 = (f32[16,3200]{1,0:T(8,128)S(1)}, f32[16,3200]{1,0:T(8,128)S(1)}, u32[]{:S(2)}, u32[]{:S(2)}) collective-permute-start(f32[16,3200]{1,0:T(8,128)S(1)} %collective-permute-done.3.refs_4_), channel_id=1, source_target_pairs={{0,4},{1,5},{2,6},{3,7},{4,0},{5,1},{6,2},{7,3},{8,12},{9,13},{10,... | collective-permute-start | bytes 614408 | tf_op jit(solution)/shard_map/ppermute | solution.py:409
  20.9 7.2 %collective-permute-start.2 = (f32[16,3200]{1,0:T(8,128)S(1)}, f32[16,3200]{1,0:T(8,128)S(1)}, u32[]{:S(2)}, u32[]{:S(2)}) collective-permute-start(f32[16,3200]{1,0:T(8,128)S(1)} %collective-permute-done.refs_1_), channel_id=1, source_target_pairs={{0,4},{1,5},{2,6},{3,7},{4,0},{5,1},{6,2},{7,3},{8,12},{9,13},{10,... | collective-permute-start | bytes 614408 | tf_op jit(solution)/shard_map/ppermute | solution.py:409
  22.8 7.5 %collective-permute-start.6 = (f32[16,3200]{1,0:T(8,128)S(1)}, f32[16,3200]{1,0:T(8,128)S(1)}, u32[]{:S(2)}, u32[]{:S(2)}) collective-permute-start(f32[16,3200]{1,0:T(8,128)S(1)} %collective-permute-done.4.refs_5_), channel_id=1, source_target_pairs={{0,4},{1,5},{2,6},{3,7},{4,0},{5,1},{6,2},{7,3},{8,12},{9,13},{10,... | collective-permute-start | bytes 614408 | tf_op jit(solution)/shard_map/ppermute | solution.py:409
  30.3 15.4 %copy-start = (f32[640,640]{1,0:T(8,128)S(1)}, f32[640,640]{1,0:T(8,128)}, u32[]{:S(2)}) copy-start(f32[640,640]{1,0:T(8,128)} %w.1) | copy-start | bytes 4915204
  45.7 3.2 %collective-permute-start.11 = (f32[8,38,8,128]{3,2,1,0:T(8,128)}, f32[8,38,8,128]{3,2,1,0:T(8,128)S(1)}, u32[]{:S(2)}, u32[]{:S(2)}) collective-permute-start(f32[8,38,8,128]{3,2,1,0:T(8,128)} %get-tuple-element.34), channel_id=1, source_target_pairs={{0,16},{1,17},{2,18},{3,19},{4,20},{5,21},{6,22},{7,23},{8,24},{9,... | collective-permute-start | bytes 3735560 | tf_op jit(solution)/shard_map/ppermute | solution.py:413
  45.8 3.1 %copy-start.10 = (f32[8,38,8,128]{3,2,1,0:T(8,128)S(1)}, f32[8,38,8,128]{3,2,1,0:T(8,128)}, u32[]{:S(2)}) copy-start(f32[8,38,8,128]{3,2,1,0:T(8,128)} %get-tuple-element.33) | copy-start | bytes 3735556
  49.0 10.3 %collective-permute-start.12 = (f32[4,38,8,128]{3,2,1,0:T(8,128)S(1)}, f32[4,38,8,128]{3,2,1,0:T(8,128)S(1)}, u32[]{:S(2)}, u32[]{:S(2)}) collective-permute-start(f32[4,38,8,128]{3,2,1,0:T(8,128)S(1)} %get-tuple-element.53), channel_id=1, source_target_pairs={{0,1},{1,0},{2,3},{3,2},{4,5},{5,4},{6,7},{7,6},{8,9},{9,8},{10,11... | collective-permute-start | bytes 1867784 | tf_op jit(solution)/shard_map/ppermute | solution.py:409
  50.1 2.0 %copy-start.2 = (f32[512,512]{1,0:T(8,128)S(1)}, f32[512,512]{1,0:T(8,128)}, u32[]{:S(2)}) copy-start(f32[512,512]{1,0:T(8,128)} %im.2) | copy-start | bytes 3145732
  59.4 7.0 %collective-permute-start.13 = (f32[2,38,8,128]{3,2,1,0:T(8,128)S(1)}, f32[2,38,8,128]{3,2,1,0:T(8,128)S(1)}, u32[]{:S(2)}, u32[]{:S(2)}) collective-permute-start(f32[2,38,8,128]{3,2,1,0:T(8,128)S(1)} %get-tuple-element.41), channel_id=1, source_target_pairs={{0,4},{1,5},{2,6},{3,7},{4,0},{5,1},{6,2},{7,3},{8,12},{9,13},{10,... | collective-permute-start | bytes 933896 | tf_op jit(solution)/shard_map/ppermute | solution.py:409
  66.4 8.7 %collective-permute-start.15 = (f32[1,38,8,128]{3,2,1,0:T(8,128)S(1)}, f32[1,38,8,128]{3,2,1,0:T(8,128)S(1)}, u32[]{:S(2)}, u32[]{:S(2)}) collective-permute-start(f32[1,38,8,128]{3,2,1,0:T(8,128)S(1)} %slice_add_fusion.6), channel_id=1, source_target_pairs={{0,8},{1,9},{2,10},{3,11},{4,12},{5,13},{6,14},{7,15},{8,0},{9,1},... | collective-permute-start | bytes 466952 | tf_op jit(solution)/shard_map/ppermute | solution.py:409
  68.5 11.9 %collective-permute-start.14 = (f32[1,16,3200]{2,1,0:T(8,128)S(1)}, f32[1,16,3200]{2,1,0:T(8,128)S(1)}, u32[]{:S(2)}, u32[]{:S(2)}) collective-permute-start(f32[1,16,3200]{2,1,0:T(8,128)S(1)} %slice.53), channel_id=1, source_target_pairs={{0,1},{1,0},{2,3},{3,2},{4,5},{5,4},{6,7},{7,6},{8,9},{9,8},{10,11... | collective-permute-start | bytes 614408 | tf_op jit(solution)/shard_map/ppermute | solution.py:409
  75.1 5.3 %collective-permute-start.16 = (f32[38,8,128]{2,1,0:T(8,128)S(1)}, f32[38,8,128]{2,1,0:T(8,128)S(1)}, u32[]{:S(2)}, u32[]{:S(2)}) collective-permute-start(f32[38,8,128]{2,1,0:T(8,128)S(1)} %fusion.1.refs_0_), channel_id=1, source_target_pairs={{0,1},{1,0},{2,3},{3,2},{4,5},{5,4},{6,7},{7,6},{8,9},{9,8},{10,11... | collective-permute-start | bytes 466952 | tf_op jit(solution)/shard_map/ppermute | solution.py:409
  75.6 5.5 %collective-permute-start.17 = (f32[38,8,128]{2,1,0:T(8,128)S(1)}, f32[38,8,128]{2,1,0:T(8,128)S(1)}, u32[]{:S(2)}, u32[]{:S(2)}) collective-permute-start(f32[38,8,128]{2,1,0:T(8,128)S(1)} %fusion.1.refs_0_), channel_id=1, source_target_pairs={{0,16},{1,17},{2,18},{3,19},{4,20},{5,21},{6,22},{7,23},{8,24},{9,... | collective-permute-start | bytes 466952 | tf_op jit(solution)/shard_map/ppermute | solution.py:413
  80.4 1.4 %collective-permute-start.18 = (f32[38,8,128]{2,1,0:T(8,128)S(1)}, f32[38,8,128]{2,1,0:T(8,128)S(1)}, u32[]{:S(2)}, u32[]{:S(2)}) collective-permute-start(f32[38,8,128]{2,1,0:T(8,128)S(1)} %collective-permute-done.16.refs_1_), channel_id=1, source_target_pairs={{0,16},{1,17},{2,18},{3,19},{4,20},{5,21},{6,22},{7,23},{8,24},{9,... | collective-permute-start | bytes 466952 | tf_op jit(solution)/shard_map/ppermute | solution.py:413
  (6 other events, 6.6 us)

commit v4 on v3

--- a/solution.py
+++ b/solution.py
@@ -41,14 +41,18 @@
     return lax.dot_general(left, right, (((1,), (0,)), ((), ())), preferred_element_type=F32)
 
 
-def onehot(row, atoms, shard, mine, flip, twice=True):
+def twist(index, top):
+    return index ^ lax.shift_left(lax.shift_right_logical(index, top) & 1, top - 1)
+
+
+def onehot(row, atoms, shard, mine, top=None, flip=None, twice=True):
     ids = row.astype(jnp.int32)
     bits = shard.bit_length() - 1
     rel = lax.shift_right_arithmetic(ids, bits) ^ mine
-    if flip is not None:
-        pair = rel & 3
-        swapped = lax.shift_right_logical(pair, 1) | lax.shift_left(pair & 1, 1)
-        rel = jnp.where(flip != 0, (rel & ~3) | swapped, rel)
+    if top is not None:
+        rel = twist(rel, top)
+        differ = (rel ^ lax.shift_right_logical(rel, 1)) & 1
+        rel = jnp.where(flip != 0, rel ^ (differ * 3), rel)
     where = jnp.where(ids < 0, -1, lax.shift_left(rel, bits) | (ids & (shard - 1)))
     hit = lax.broadcasted_iota(jnp.int32, (atoms, row.shape[1]), 0) == where
     one = jnp.where(hit, 1.0, 0.0).astype(BF16)
@@ -136,11 +140,12 @@
     tiles = edges // LANES
     rows = tuple(g * chans // (2 * own_slots) for g in GROUPS)
     bases = tuple(sum(GROUPS[:g]) * chans // 2 for g in range(5))
-    select = onehot(ends(pack, 0, edges), count * shard, shard, me[1], None)
+    select = onehot(ends(pack, 0, edges), count * shard, shard, me[1])
     gather(shards, select, feats, chans)
     spread(pack, rot)
     parts = STRIP // 8
     high = lax.shift_right_logical(me[0], 1)
+    top = own_slots.bit_length() - 2
 
     def pick(parity):
         for strip in range(chans // STRIP):
@@ -168,7 +173,7 @@
                                 term = factor * x[part * 8 : part * 8 + 8]
                                 acc[r, part] = acc[r, part] + term if c else term
                     for r, part, group, slot, inner in wanted:
-                        at = bases[group] + (slot ^ high) * rows[group] + inner
+                        at = bases[group] + twist(slot ^ high, top) * rows[group] + inner
                         picked[pl.ds(pl.multiple_of(at, 8), 8), lanes] = acc[r, part]
                 return carry
 
@@ -195,7 +200,7 @@
     for load in loads:
         load.start()
     select = jnp.concatenate(
-        [onehot(ends(p, 1, edges), count * shard, shard, owner, core) for p in packs], 1
+        [onehot(ends(p, 1, edges), count * shard, shard, owner, own_slots.bit_length() - 1, core) for p in packs], 1
     )
     gather(shards, select, feats, chans)
 
@@ -284,7 +289,7 @@
 
 def scatter_kernel(count, shard, chans, me, pack, d0, d1, d2, out, rot, back):
     edges = rot.shape[2]
-    select = onehot(ends(pack, 0, edges), count * shard, shard, me[1], None, False)
+    select = onehot(ends(pack, 0, edges), count * shard, shard, me[1], twice=False)
     select = jnp.concatenate([select, select], 1)
     spread(pack, rot)
     tiles = edges // LANES
@@ -430,10 +435,12 @@
         4,
     )(edge_count, jnp.transpose(rotation, (0, 1, 3, 2, 4)), edge_src, edge_tgt)
     x_own = src_feats[0]
+    masks = [1 << b for b in range(src_bits)]
+    masks[-1] |= masks[-2]
     g_parts = {0: tgt_cotangent[0]}
     for bit in range(src_bits - 1, 1, -1):
         for k, part in list(g_parts.items()):
-            g_parts[k | (1 << bit)] = hop(part, None, (1 << bit, 0))
+            g_parts[k | (1 << bit)] = hop(part, None, (masks[bit], 0))
     far = [k for k in g_parts if k > 0]
     first, second = ((1, 0), (2, 0)), ((2, 0), (1, 0))
     g_parts[1] = hop(g_parts[0], None, *first)
@@ -515,7 +522,7 @@
     )(w_two_re, w_two_im, *u[4:6])
     routes = [((0, 1), (2, 0)), ((2, 0), (0, 1))]
     routes += [((0, 1 << b),) * 2 for b in range(tgt_bits - 1, 0, -1)]
-    routes += [((1 << b, 0),) * 2 for b in range(src_bits - 1, 1, -1)]
+    routes += [((masks[b], 0),) * 2 for b in range(src_bits - 1, 1, -1)]
     held, came = keep, cross(send)
     for k, route in enumerate(routes):
         half = held.shape[0] // 2

time: 83.4 us -> 80.7 us (0.968)
  waiting for transfers between devices: 24.8 us -> 17.4 us
  starting transfers between devices: 19.5 us -> 24.3 us
    ppermute x16, waiting for transfers between devices: 22.5 us -> 15.1 us  [hop(): return lax.ppermute(value, AXES, pairs)]
    ppermute x16, starting transfers between devices: 19.5 us -> 24.2 us  [hop(): return lax.ppermute(value, AXES, pairs)]
  transfers between devices with their start and end apart: 19 -> 19, of which waited for: 10 -> 10; matrix products, arithmetic and copies ran while one was open for 1% -> 1% of each run, Pallas kernels for 20% -> 21%
where the time goes in v4:
time: 80.7 us; the launch traced here: 80.3 us
  Pallas kernels  33.4 us (41%)
  starting transfers between devices  24.3 us (30%)
  waiting for transfers between devices  17.4 us (22%)
  local copies, waits for them, and re-layouts  2.82 us (3%)
  between operations  1.45 us (2%)
  other arithmetic  1.03 us (1%)
    ppermute x16, starting transfers between devices, hop(): return lax.ppermute(value, AXES, pairs)  24.2 us
    pallas_call x1, Pallas kernels, local(): call(functools.partial(weight_kernel, nsrc, shard, slots, ntgt, chans), '...  15.3 us
    ppermute x16, waiting for transfers between devices, hop(): return lax.ppermute(value, AXES, pairs)  15.1 us
    pallas_call x2, Pallas kernels, source_rows(): call(functools.partial(source_kernel, ntgt, shard, slots, chans), 'source...  5.09 us
    pallas_call x1, Pallas kernels, local(): call(functools.partial(scatter_kernel, ntgt, shard, chans), 'source_sums'...  4.39 us
    pallas_call x1, Pallas kernels, local(): call(back_pair_kernel, 'back_one', vmem(4), vmem(1)[0], shape(8 * chans,...  3.45 us
    unnamed x22, local copies, waits for them, and re-layouts  2.81 us
    ppermute x3, waiting for transfers between devices, cross(): lax.ppermute(value, AXES, [(i, (i + half) % (2 * half)) for i in range(2...  2.3 us
  transfers between devices with their start and end apart: 19, of which 10 were waited for; matrix products, arithmetic and copies ran while one was open for 1% of the time, Pallas kernels for 21%

profile of v4, /device:TPU:0, one launch (start us, length us, event | category | flops | bytes accessed | tf_op | source)
XLA Modules:
  0.0 80.3 jit_solution(8501407896835939076)
XLA Ops:
  0.6 3.0 %collective-permute-start.9 = (f32[16,3200]{1,0:T(8,128)}, f32[16,3200]{1,0:T(8,128)S(1)}, u32[]{:S(2)}, u32[]{:S(2)}) collective-permute-start(f32[16,3200]{1,0:T(8,128)} %bitcast.8), channel_id=1, source_target_pairs={{0,2},{1,3},{2,0},{3,1},{4,6},{5,7},{6,4},{7,5},{8,10},{9,11},{10,... | collective-permute-start | bytes 614408 | tf_op jit(solution)/shard_map/ppermute | solution.py:414
  3.6 1.5 %collective-permute-start.8 = (f32[16,3200]{1,0:T(8,128)}, f32[16,3200]{1,0:T(8,128)S(1)}, u32[]{:S(2)}, u32[]{:S(2)}) collective-permute-start(f32[16,3200]{1,0:T(8,128)} %bitcast.9), channel_id=1, source_target_pairs={{0,1},{1,0},{2,3},{3,2},{4,5},{5,4},{6,7},{7,6},{8,9},{9,8},{10,11... | collective-permute-start | bytes 614408 | tf_op jit(solution)/shard_map/ppermute | solution.py:414
  5.2 3.6 %collective-permute-start.3 = (f32[16,3200]{1,0:T(8,128)}, f32[16,3200]{1,0:T(8,128)S(1)}, u32[]{:S(2)}, u32[]{:S(2)}) collective-permute-start(f32[16,3200]{1,0:T(8,128)} %bitcast.11), channel_id=1, source_target_pairs={{0,12},{1,13},{2,14},{3,15},{4,8},{5,9},{6,10},{7,11},{8,4},{9,5},... | collective-permute-start | bytes 614408 | tf_op jit(solution)/shard_map/ppermute | solution.py:414
  10.0 0.9 %copy-done.7 = f32[1,1,1,115,384]{4,2,3,1,0:T(1,128)S(1)} copy-done((f32[1,1,1,115,384]{4,2,3,1,0:T(1,128)S(1)}, f32[1,1,1,115,384]{4,2,3,1,0:T(1,128)}, u32[]{:S(2)}) %copy-start.7) | copy-done | bytes 176664
  10.9 0.7 copy-done.8
  12.6 1.6 %collective-permute-start.7 = (f32[352,128]{1,0:T(8,128)S(1)}, f32[352,128]{1,0:T(8,128)S(1)}, u32[]{:S(2)}, u32[]{:S(2)}) collective-permute-start(f32[352,128]{1,0:T(8,128)S(1)} %prepare.1.refs_2_.refs_8_.pack), channel_id=1, source_target_pairs={{0,2},{1,3},{2,0},{3,1},{4,6},{5,7},{6,4},{7,5},{8,10},{9,11},{10,... | collective-permute-start | bytes 540680 | tf_op jit(solution)/shard_map/ppermute | solution.py:414
  15.7 2.5 %source_rows.2 = (bf16[1216,384]{1,0:T(8,128)(2,1)S(1)}, bf16[1216,384]{1,0:T(8,128)(2,1)S(1)}) custom-call(s32[3]{0:T(128)S(1)} %pad_add_fusion.me, f32[16,3200]{1,0:T(8,128)S(1)} %bitcast.10, f32[16,3200]{1,0:T(8,128)S(1)} %collective-permute-done.8.refs_1_, f32[352,128]{1,0:T(8,128)S(1)} %prepare.1.refs_2_.refs_8_.pack), custom_call_target="tpu_custom_call" | custom-call | flops 2875000064 | bytes 100000 | tf_op jit(solution)/shard_map/source_rows/pallas_call | solution.py:462
  18.8 2.0 %collective-permute-start.5 = (f32[16,3200]{1,0:T(8,128)S(1)}, f32[16,3200]{1,0:T(8,128)S(1)}, u32[]{:S(2)}, u32[]{:S(2)}) collective-permute-start(f32[16,3200]{1,0:T(8,128)S(1)} %collective-permute-done.3.refs_4_), channel_id=1, source_target_pairs={{0,4},{1,5},{2,6},{3,7},{4,0},{5,1},{6,2},{7,3},{8,12},{9,13},{10,... | collective-permute-start | bytes 614408 | tf_op jit(solution)/shard_map/ppermute | solution.py:414
  21.0 3.8 %collective-permute-start.6 = (f32[16,3200]{1,0:T(8,128)S(1)}, f32[16,3200]{1,0:T(8,128)S(1)}, u32[]{:S(2)}, u32[]{:S(2)}) collective-permute-start(f32[16,3200]{1,0:T(8,128)S(1)} %collective-permute-done.4.refs_5_), channel_id=1, source_target_pairs={{0,4},{1,5},{2,6},{3,7},{4,0},{5,1},{6,2},{7,3},{8,12},{9,13},{10,... | collective-permute-start | bytes 614408 | tf_op jit(solution)/shard_map/ppermute | solution.py:414
  24.8 2.5 %source_rows.3 = (bf16[1216,384]{1,0:T(8,128)(2,1)S(1)}, bf16[1216,384]{1,0:T(8,128)(2,1)S(1)}) custom-call(s32[3]{0:T(128)S(1)} %pad_add_fusion.me, f32[16,3200]{1,0:T(8,128)S(1)} %collective-permute-done.9.refs_0_, f32[16,3200]{1,0:T(8,128)S(1)} %collective-permute-done.10.refs_1_, f32[352,128]{1,0:T(8,128)S(1)} %collective-permute-done.7.refs_2_.refs_9_), custom_call_target="tpu_custom_call" | custom-call | flops 2875000064 | bytes 100000 | tf_op jit(solution)/shard_map/source_rows/pallas_call | solution.py:462
  27.4 1.6 %collective-permute-done.6.refs_7_ = f32[16,3200]{1,0:T(8,128)S(1)} collective-permute-done((f32[16,3200]{1,0:T(8,128)S(1)}, f32[16,3200]{1,0:T(8,128)S(1)}, u32[]{:S(2)}, u32[]{:S(2)}) %collective-permute-start.6) | collective-permute-done | bytes 204832 | tf_op jit(solution)/shard_map/ppermute | solution.py:414
  29.0 15.3 %weight_terms.1 = (f32[8,38,8,128]{3,2,1,0:T(8,128)}, f32[8,38,8,128]{3,2,1,0:T(8,128)}, bf16[640,384]{1,0:T(8,128)(2,1)S(1)}, bf16[640,384]{1,0:T(8,128)(2,1)S(...) custom-call(s32[3]{0:T(128)S(1)} %pad_add_fusion.me, ...), custom_call_target="tpu_custom_call" | custom-call | flops 16099999744 | bytes 100000 | tf_op jit(solution)/shard_map/weight_terms/pallas_call | solution.py:491
  44.4 1.5 %back_zero.1.d0 = f32[640,384]{1,0:T(8,128)S(1)} custom-call(f32[640,640]{1,0:T(8,128)S(1)} %copy-done, bf16[640,384]{1,0:T(8,128)(2,1)S(1)} %get-tuple-element.35.uh, bf16[640,384]{1,0:T(8,128)(2,1)S(1)} %get-tuple-element.36.ul), custom_call_target="tpu_custom_call" | custom-call | flops 3449999872 | bytes 100000 | tf_op jit(solution)/shard_map/back_zero/pallas_call | solution.py:514
  45.9 1.6 %collective-permute-done.11 = f32[8,38,8,128]{3,2,1,0:T(8,128)S(1)} collective-permute-done((f32[8,38,8,128]{3,2,1,0:T(8,128)}, f32[8,38,8,128]{3,2,1,0:T(8,128)S(1)}, u32[]{:S(2)}, u32[]{:S(2)}) %collective-permute-start.11) | collective-permute-done | bytes 1245216 | tf_op jit(solution)/shard_map/ppermute | solution.py:418
  48.8 2.0 %back_two.1.d2 = f32[768,384]{1,0:T(8,128)S(1)} custom-call(f32[384,384]{1,0:T(8,128)S(1)} %copy-done.3, f32[384,384]{1,0:T(8,128)S(1)} %copy-done.4, bf16[768,384]{1,0:T(8,128)(2,1)S(1)} %get-tuple-element.39.uh, bf16[768,384]{1,0:T(8,128)(2,1)S(1)} %get-tuple-element.40.ul), custom_call_target="tpu_custom_call" | custom-call | flops 3449999872 | bytes 100000 | tf_op jit(solution)/shard_map/back_two/pallas_call | solution.py:520
  50.8 3.5 %back_one.1.d1 = f32[1024,384]{1,0:T(8,128)S(1)} custom-call(f32[512,512]{1,0:T(8,128)S(1)} %copy-done.1, f32[512,512]{1,0:T(8,128)S(1)} %copy-done.2, bf16[1024,384]{1,0:T(8,128)(2,1)S(1)} %get-tuple-element.37.uh, bf16[1024,384]{1,0:T(8,128)(2,1)S(1)} %get-tuple-element.38.ul), custom_call_target="tpu_custom_call" | custom-call | flops 4600000000 | bytes 100000 | tf_op jit(solution)/shard_map/back_one/pallas_call | solution.py:517
  54.3 3.7 %collective-permute-done.12 = f32[4,38,8,128]{3,2,1,0:T(8,128)S(1)} collective-permute-done((f32[4,38,8,128]{3,2,1,0:T(8,128)S(1)}, f32[4,38,8,128]{3,2,1,0:T(8,128)S(1)}, u32[]{:S(2)}, u32[]{:S(2)}) %collective-permute-start.12) | collective-permute-done | bytes 622624 | tf_op jit(solution)/shard_map/ppermute | solution.py:414
  58.0 2.0 %collective-permute-start.13 = (f32[2,38,8,128]{3,2,1,0:T(8,128)S(1)}, f32[2,38,8,128]{3,2,1,0:T(8,128)S(1)}, u32[]{:S(2)}, u32[]{:S(2)}) collective-permute-start(f32[2,38,8,128]{3,2,1,0:T(8,128)S(1)} %get-tuple-element.41), channel_id=1, source_target_pairs={{0,4},{1,5},{2,6},{3,7},{4,0},{5,1},{6,2},{7,3},{8,12},{9,13},{10,... | collective-permute-start | bytes 933896 | tf_op jit(solution)/shard_map/ppermute | solution.py:414
  60.0 4.4 %source_sums.1 = f32[2,16,3200]{2,1,0:T(8,128)S(1)} custom-call(s32[3]{0:T(128)S(1)} %pad_add_fusion.me, f32[352,128]{1,0:T(8,128)S(1)} %prepare.1.refs_2_.refs_8_.pack, f32[640,384]{1,0:T(8,128)S(1)} %back_zero.1.d0, f32[1024,384]{1,0:T(8,128)S(1)} %back_one.1.d1, f32[768,384]{1,0:T(8,128)S(1)} %back_two.1.d2), custom_call_target="tpu_custom_call" | custom-call | flops 5750000128 | bytes 100000 | tf_op jit(solution)/shard_map/source_sums/pallas_call | solution.py:532
  65.0 3.4 %collective-permute-start.15 = (f32[1,38,8,128]{3,2,1,0:T(8,128)S(1)}, f32[1,38,8,128]{3,2,1,0:T(8,128)S(1)}, u32[]{:S(2)}, u32[]{:S(2)}) collective-permute-start(f32[1,38,8,128]{3,2,1,0:T(8,128)S(1)} %slice_add_fusion.6), channel_id=1, source_target_pairs={{0,12},{1,13},{2,14},{3,15},{4,8},{5,9},{6,10},{7,11},{8,4},{9,5},... | collective-permute-start | bytes 466952 | tf_op jit(solution)/shard_map/ppermute | solution.py:414
  68.9 3.3 %collective-permute-done.15 = f32[1,38,8,128]{3,2,1,0:T(8,128)S(1)} collective-permute-done((f32[1,38,8,128]{3,2,1,0:T(8,128)S(1)}, f32[1,38,8,128]{3,2,1,0:T(8,128)S(1)}, u32[]{:S(2)}, u32[]{:S(2)}) %collective-permute-start.15) | collective-permute-done | bytes 155680 | tf_op jit(solution)/shard_map/ppermute | solution.py:414
  72.8 4.7 %collective-permute-done.16.refs_1_ = f32[38,8,128]{2,1,0:T(8,128)S(1)} collective-permute-done((f32[38,8,128]{2,1,0:T(8,128)S(1)}, f32[38,8,128]{2,1,0:T(8,128)S(1)}, u32[]{:S(2)}, u32[]{:S(2)}) %collective-permute-start.16) | collective-permute-done | bytes 155680 | tf_op jit(solution)/shard_map/ppermute | solution.py:414
  77.6 0.7 slice_add_fusion.4
  78.9 1.4 %unpack.1 = (f32[80,640]{1,0:T(8,128)}, f32[64,512]{1,0:T(8,128)}, f32[64,512]{1,0:T(8,128)}, f32[48,384]{1,0:T(8,128)}, f32[48,384]{1,0:T(8,128)}) custom-call(s32[3]{0:T(128)S(1)} %pad_add_fusion.me, f32[38,8,128]{2,1,0:T(8,128)S(1)} %fusion.1.refs_0_, f32[38,8,128]{2,1,0:T(8,128)S(1)} %collective-permute-done.16.refs_1_, ...), custom_call_target="tpu_custom_call" | custom-call | flops 2300000000 | bytes 100000 | tf_op jit(solution)/shard_map/unpack/pallas_call | solution.py:555
  (52 shorter events, 7.7 us)
Async XLA Ops:
  0.6 11.9 %collective-permute-start.9 = (f32[16,3200]{1,0:T(8,128)}, f32[16,3200]{1,0:T(8,128)S(1)}, u32[]{:S(2)}, u32[]{:S(2)}) collective-permute-start(f32[16,3200]{1,0:T(8,128)} %bitcast.8), channel_id=1, source_target_pairs={{0,2},{1,3},{2,0},{3,1},{4,6},{5,7},{6,4},{7,5},{8,10},{9,11},{10,... | collective-permute-start | bytes 614408 | tf_op jit(solution)/shard_map/ppermute | solution.py:414
  3.6 10.5 %collective-permute-start.8 = (f32[16,3200]{1,0:T(8,128)}, f32[16,3200]{1,0:T(8,128)S(1)}, u32[]{:S(2)}, u32[]{:S(2)}) collective-permute-start(f32[16,3200]{1,0:T(8,128)} %bitcast.9), channel_id=1, source_target_pairs={{0,1},{1,0},{2,3},{3,2},{4,5},{5,4},{6,7},{7,6},{8,9},{9,8},{10,11... | collective-permute-start | bytes 614408 | tf_op jit(solution)/shard_map/ppermute | solution.py:414
  5.2 10.0 %collective-permute-start.3 = (f32[16,3200]{1,0:T(8,128)}, f32[16,3200]{1,0:T(8,128)S(1)}, u32[]{:S(2)}, u32[]{:S(2)}) collective-permute-start(f32[16,3200]{1,0:T(8,128)} %bitcast.11), channel_id=1, source_target_pairs={{0,12},{1,13},{2,14},{3,15},{4,8},{5,9},{6,10},{7,11},{8,4},{9,5},... | collective-permute-start | bytes 614408 | tf_op jit(solution)/shard_map/ppermute | solution.py:414
  8.8 18.6 %collective-permute-start.1 = (f32[16,3200]{1,0:T(8,128)}, f32[16,3200]{1,0:T(8,128)S(1)}, u32[]{:S(2)}, u32[]{:S(2)}) collective-permute-start(f32[16,3200]{1,0:T(8,128)} %bitcast.12), channel_id=1, source_target_pairs={{0,4},{1,5},{2,6},{3,7},{4,0},{5,1},{6,2},{7,3},{8,12},{9,13},{10,... | collective-permute-start | bytes 614408 | tf_op jit(solution)/shard_map/ppermute | solution.py:414
  8.8 12.0 %collective-permute-start = (f32[16,3200]{1,0:T(8,128)}, f32[16,3200]{1,0:T(8,128)S(1)}, u32[]{:S(2)}, u32[]{:S(2)}) collective-permute-start(f32[16,3200]{1,0:T(8,128)} %bitcast.13), channel_id=1, source_target_pairs={{0,2},{1,3},{2,0},{3,1},{4,6},{5,7},{6,4},{7,5},{8,10},{9,11},{10,... | collective-permute-start | bytes 614408 | tf_op jit(solution)/shard_map/ppermute | solution.py:414
  12.3 3.4 %copy-start.5 = (f32[1,16,3200]{2,1,0:T(8,128)S(1)}, f32[1,16,3200]{2,1,0:T(8,128)}, u32[]{:S(2)}) copy-start(f32[1,16,3200]{2,1,0:T(8,128)} %param.11) | copy-start | bytes 614404
  12.6 6.2 %collective-permute-start.7 = (f32[352,128]{1,0:T(8,128)S(1)}, f32[352,128]{1,0:T(8,128)S(1)}, u32[]{:S(2)}, u32[]{:S(2)}) collective-permute-start(f32[352,128]{1,0:T(8,128)S(1)} %prepare.1.refs_2_.refs_8_.pack), channel_id=1, source_target_pairs={{0,2},{1,3},{2,0},{3,1},{4,6},{5,7},{6,4},{7,5},{8,10},{9,11},{10,... | collective-permute-start | bytes 540680 | tf_op jit(solution)/shard_map/ppermute | solution.py:414
  14.1 10.7 %collective-permute-start.10 = (f32[16,3200]{1,0:T(8,128)S(1)}, f32[16,3200]{1,0:T(8,128)S(1)}, u32[]{:S(2)}, u32[]{:S(2)}) collective-permute-start(f32[16,3200]{1,0:T(8,128)S(1)} %collective-permute-done.9.refs_0_), channel_id=1, source_target_pairs={{0,1},{1,0},{2,3},{3,2},{4,5},{5,4},{6,7},{7,6},{8,9},{9,8},{10,11... | collective-permute-start | bytes 614408 | tf_op jit(solution)/shard_map/ppermute | solution.py:414
  15.2 5.8 %collective-permute-start.4 = (f32[16,3200]{1,0:T(8,128)S(1)}, f32[16,3200]{1,0:T(8,128)S(1)}, u32[]{:S(2)}, u32[]{:S(2)}) collective-permute-start(f32[16,3200]{1,0:T(8,128)S(1)} %collective-permute-done.3.refs_4_), channel_id=1, source_target_pairs={{0,2},{1,3},{2,0},{3,1},{4,6},{5,7},{6,4},{7,5},{8,10},{9,11},{10,... | collective-permute-start | bytes 614408 | tf_op jit(solution)/shard_map/ppermute | solution.py:414
  18.3 10.7 %copy-start.6 = (f32[1,16,3200]{2,1,0:T(8,128)S(1)}, f32[1,16,3200]{2,1,0:T(8,128)}, u32[]{:S(2)}) copy-start(f32[1,16,3200]{2,1,0:T(8,128)} %param.12) | copy-start | bytes 614404
  18.8 8.6 %collective-permute-start.5 = (f32[16,3200]{1,0:T(8,128)S(1)}, f32[16,3200]{1,0:T(8,128)S(1)}, u32[]{:S(2)}, u32[]{:S(2)}) collective-permute-start(f32[16,3200]{1,0:T(8,128)S(1)} %collective-permute-done.3.refs_4_), channel_id=1, source_target_pairs={{0,4},{1,5},{2,6},{3,7},{4,0},{5,1},{6,2},{7,3},{8,12},{9,13},{10,... | collective-permute-start | bytes 614408 | tf_op jit(solution)/shard_map/ppermute | solution.py:414
  20.8 6.6 %collective-permute-start.2 = (f32[16,3200]{1,0:T(8,128)S(1)}, f32[16,3200]{1,0:T(8,128)S(1)}, u32[]{:S(2)}, u32[]{:S(2)}) collective-permute-start(f32[16,3200]{1,0:T(8,128)S(1)} %collective-permute-done.refs_1_), channel_id=1, source_target_pairs={{0,4},{1,5},{2,6},{3,7},{4,0},{5,1},{6,2},{7,3},{8,12},{9,13},{10,... | collective-permute-start | bytes 614408 | tf_op jit(solution)/shard_map/ppermute | solution.py:414
  21.0 8.0 %collective-permute-start.6 = (f32[16,3200]{1,0:T(8,128)S(1)}, f32[16,3200]{1,0:T(8,128)S(1)}, u32[]{:S(2)}, u32[]{:S(2)}) collective-permute-start(f32[16,3200]{1,0:T(8,128)S(1)} %collective-permute-done.4.refs_5_), channel_id=1, source_target_pairs={{0,4},{1,5},{2,6},{3,7},{4,0},{5,1},{6,2},{7,3},{8,12},{9,13},{10,... | collective-permute-start | bytes 614408 | tf_op jit(solution)/shard_map/ppermute | solution.py:414
  29.0 15.4 %copy-start = (f32[640,640]{1,0:T(8,128)S(1)}, f32[640,640]{1,0:T(8,128)}, u32[]{:S(2)}) copy-start(f32[640,640]{1,0:T(8,128)} %w.1) | copy-start | bytes 4915204
  44.3 3.2 %collective-permute-start.11 = (f32[8,38,8,128]{3,2,1,0:T(8,128)}, f32[8,38,8,128]{3,2,1,0:T(8,128)S(1)}, u32[]{:S(2)}, u32[]{:S(2)}) collective-permute-start(f32[8,38,8,128]{3,2,1,0:T(8,128)} %get-tuple-element.34), channel_id=1, source_target_pairs={{0,16},{1,17},{2,18},{3,19},{4,20},{5,21},{6,22},{7,23},{8,24},{9,... | collective-permute-start | bytes 3735560 | tf_op jit(solution)/shard_map/ppermute | solution.py:418
  44.4 3.1 %copy-start.10 = (f32[8,38,8,128]{3,2,1,0:T(8,128)S(1)}, f32[8,38,8,128]{3,2,1,0:T(8,128)}, u32[]{:S(2)}) copy-start(f32[8,38,8,128]{3,2,1,0:T(8,128)} %get-tuple-element.33) | copy-start | bytes 3735556
  47.6 10.3 %collective-permute-start.12 = (f32[4,38,8,128]{3,2,1,0:T(8,128)S(1)}, f32[4,38,8,128]{3,2,1,0:T(8,128)S(1)}, u32[]{:S(2)}, u32[]{:S(2)}) collective-permute-start(f32[4,38,8,128]{3,2,1,0:T(8,128)S(1)} %get-tuple-element.53), channel_id=1, source_target_pairs={{0,1},{1,0},{2,3},{3,2},{4,5},{5,4},{6,7},{7,6},{8,9},{9,8},{10,11... | collective-permute-start | bytes 1867784 | tf_op jit(solution)/shard_map/ppermute | solution.py:414
  48.7 2.0 %copy-start.2 = (f32[512,512]{1,0:T(8,128)S(1)}, f32[512,512]{1,0:T(8,128)}, u32[]{:S(2)}) copy-start(f32[512,512]{1,0:T(8,128)} %im.2) | copy-start | bytes 3145732
  58.0 7.0 %collective-permute-start.13 = (f32[2,38,8,128]{3,2,1,0:T(8,128)S(1)}, f32[2,38,8,128]{3,2,1,0:T(8,128)S(1)}, u32[]{:S(2)}, u32[]{:S(2)}) collective-permute-start(f32[2,38,8,128]{3,2,1,0:T(8,128)S(1)} %get-tuple-element.41), channel_id=1, source_target_pairs={{0,4},{1,5},{2,6},{3,7},{4,0},{5,1},{6,2},{7,3},{8,12},{9,13},{10,... | collective-permute-start | bytes 933896 | tf_op jit(solution)/shard_map/ppermute | solution.py:414
  65.0 7.2 %collective-permute-start.15 = (f32[1,38,8,128]{3,2,1,0:T(8,128)S(1)}, f32[1,38,8,128]{3,2,1,0:T(8,128)S(1)}, u32[]{:S(2)}, u32[]{:S(2)}) collective-permute-start(f32[1,38,8,128]{3,2,1,0:T(8,128)S(1)} %slice_add_fusion.6), channel_id=1, source_target_pairs={{0,12},{1,13},{2,14},{3,15},{4,8},{5,9},{6,10},{7,11},{8,4},{9,5},... | collective-permute-start | bytes 466952 | tf_op jit(solution)/shard_map/ppermute | solution.py:414
  68.4 9.2 %collective-permute-start.14 = (f32[1,16,3200]{2,1,0:T(8,128)S(1)}, f32[1,16,3200]{2,1,0:T(8,128)S(1)}, u32[]{:S(2)}, u32[]{:S(2)}) collective-permute-start(f32[1,16,3200]{2,1,0:T(8,128)S(1)} %slice.53), channel_id=1, source_target_pairs={{0,1},{1,0},{2,3},{3,2},{4,5},{5,4},{6,7},{7,6},{8,9},{9,8},{10,11... | collective-permute-start | bytes 614408 | tf_op jit(solution)/shard_map/ppermute | solution.py:414
  72.2 5.3 %collective-permute-start.16 = (f32[38,8,128]{2,1,0:T(8,128)S(1)}, f32[38,8,128]{2,1,0:T(8,128)S(1)}, u32[]{:S(2)}, u32[]{:S(2)}) collective-permute-start(f32[38,8,128]{2,1,0:T(8,128)S(1)} %fusion.1.refs_0_), channel_id=1, source_target_pairs={{0,1},{1,0},{2,3},{3,2},{4,5},{5,4},{6,7},{7,6},{8,9},{9,8},{10,11... | collective-permute-start | bytes 466952 | tf_op jit(solution)/shard_map/ppermute | solution.py:414
  72.8 5.4 %collective-permute-start.17 = (f32[38,8,128]{2,1,0:T(8,128)S(1)}, f32[38,8,128]{2,1,0:T(8,128)S(1)}, u32[]{:S(2)}, u32[]{:S(2)}) collective-permute-start(f32[38,8,128]{2,1,0:T(8,128)S(1)} %fusion.1.refs_0_), channel_id=1, source_target_pairs={{0,16},{1,17},{2,18},{3,19},{4,20},{5,21},{6,22},{7,23},{8,24},{9,... | collective-permute-start | bytes 466952 | tf_op jit(solution)/shard_map/ppermute | solution.py:418
  77.5 1.4 %collective-permute-start.18 = (f32[38,8,128]{2,1,0:T(8,128)S(1)}, f32[38,8,128]{2,1,0:T(8,128)S(1)}, u32[]{:S(2)}, u32[]{:S(2)}) collective-permute-start(f32[38,8,128]{2,1,0:T(8,128)S(1)} %collective-permute-done.16.refs_1_), channel_id=1, source_target_pairs={{0,16},{1,17},{2,18},{3,19},{4,20},{5,21},{6,22},{7,23},{8,24},{9,... | collective-permute-start | bytes 466952 | tf_op jit(solution)/shard_map/ppermute | solution.py:418
  (6 other events, 6.6 us)

commit v5 on v4

--- a/solution.py
+++ b/solution.py
@@ -10,7 +10,7 @@
 OFFSETS = (0, 1, 10, 35, 70)
 ROT = 115
 LANES = 128
-STRIP = 32
+STRIP = 64
 AXES = ("rep", "src", "tgt")
 F32 = jnp.float32
 BF16 = jnp.bfloat16

time: 80.7 us -> 80.6 us (level)
  no operation moved by 1% of the time
where the time goes in v5:
time: 80.6 us; the launch traced here: 80.3 us
  Pallas kernels  33.4 us (41%)
  starting transfers between devices  24.4 us (30%)
  waiting for transfers between devices  17.2 us (21%)
  local copies, waits for them, and re-layouts  2.8 us (3%)
  between operations  1.45 us (2%)
  other arithmetic  1.03 us (1%)
    ppermute x16, starting transfers between devices, hop(): return lax.ppermute(value, AXES, pairs)  24.3 us
    pallas_call x1, Pallas kernels, local(): call(functools.partial(weight_kernel, nsrc, shard, slots, ntgt, chans), '...  15.2 us
    ppermute x16, waiting for transfers between devices, hop(): return lax.ppermute(value, AXES, pairs)  14.9 us
    pallas_call x2, Pallas kernels, source_rows(): call(functools.partial(source_kernel, ntgt, shard, slots, chans), 'source...  5.15 us
    pallas_call x1, Pallas kernels, local(): call(functools.partial(scatter_kernel, ntgt, shard, chans), 'source_sums'...  4.39 us
    pallas_call x1, Pallas kernels, local(): call(back_pair_kernel, 'back_one', vmem(4), vmem(1)[0], shape(8 * chans,...  3.45 us
    unnamed x22, local copies, waits for them, and re-layouts  2.79 us
    ppermute x3, waiting for transfers between devices, cross(): lax.ppermute(value, AXES, [(i, (i + half) % (2 * half)) for i in range(2...  2.3 us
  transfers between devices with their start and end apart: 19, of which 10 were waited for; matrix products, arithmetic and copies ran while one was open for 1% of the time, Pallas kernels for 21%

profile of v5, /device:TPU:0, one launch (start us, length us, event | category | flops | bytes accessed | tf_op | source)
XLA Modules:
  0.0 80.3 jit_solution(13813763032097192806)
XLA Ops:
  0.6 3.0 %collective-permute-start.9 = (f32[16,3200]{1,0:T(8,128)}, f32[16,3200]{1,0:T(8,128)S(1)}, u32[]{:S(2)}, u32[]{:S(2)}) collective-permute-start(f32[16,3200]{1,0:T(8,128)} %bitcast.8), channel_id=1, source_target_pairs={{0,2},{1,3},{2,0},{3,1},{4,6},{5,7},{6,4},{7,5},{8,10},{9,11},{10,... | collective-permute-start | bytes 614408 | tf_op jit(solution)/shard_map/ppermute | solution.py:414
  3.6 1.5 %collective-permute-start.8 = (f32[16,3200]{1,0:T(8,128)}, f32[16,3200]{1,0:T(8,128)S(1)}, u32[]{:S(2)}, u32[]{:S(2)}) collective-permute-start(f32[16,3200]{1,0:T(8,128)} %bitcast.9), channel_id=1, source_target_pairs={{0,1},{1,0},{2,3},{3,2},{4,5},{5,4},{6,7},{7,6},{8,9},{9,8},{10,11... | collective-permute-start | bytes 614408 | tf_op jit(solution)/shard_map/ppermute | solution.py:414
  5.2 3.6 %collective-permute-start.3 = (f32[16,3200]{1,0:T(8,128)}, f32[16,3200]{1,0:T(8,128)S(1)}, u32[]{:S(2)}, u32[]{:S(2)}) collective-permute-start(f32[16,3200]{1,0:T(8,128)} %bitcast.11), channel_id=1, source_target_pairs={{0,12},{1,13},{2,14},{3,15},{4,8},{5,9},{6,10},{7,11},{8,4},{9,5},... | collective-permute-start | bytes 614408 | tf_op jit(solution)/shard_map/ppermute | solution.py:414
  10.0 0.9 %copy-done.7 = f32[1,1,1,115,384]{4,2,3,1,0:T(1,128)S(1)} copy-done((f32[1,1,1,115,384]{4,2,3,1,0:T(1,128)S(1)}, f32[1,1,1,115,384]{4,2,3,1,0:T(1,128)}, u32[]{:S(2)}) %copy-start.7) | copy-done | bytes 176664
  10.9 0.7 copy-done.8
  12.6 1.6 %collective-permute-start.7 = (f32[352,128]{1,0:T(8,128)S(1)}, f32[352,128]{1,0:T(8,128)S(1)}, u32[]{:S(2)}, u32[]{:S(2)}) collective-permute-start(f32[352,128]{1,0:T(8,128)S(1)} %prepare.1.refs_2_.refs_8_.pack), channel_id=1, source_target_pairs={{0,2},{1,3},{2,0},{3,1},{4,6},{5,7},{6,4},{7,5},{8,10},{9,11},{10,... | collective-permute-start | bytes 540680 | tf_op jit(solution)/shard_map/ppermute | solution.py:414
  15.7 2.6 %source_rows.2 = (bf16[1216,384]{1,0:T(8,128)(2,1)S(1)}, bf16[1216,384]{1,0:T(8,128)(2,1)S(1)}) custom-call(s32[3]{0:T(128)S(1)} %pad_add_fusion.me, f32[16,3200]{1,0:T(8,128)S(1)} %bitcast.10, f32[16,3200]{1,0:T(8,128)S(1)} %collective-permute-done.8.refs_1_, f32[352,128]{1,0:T(8,128)S(1)} %prepare.1.refs_2_.refs_8_.pack), custom_call_target="tpu_custom_call" | custom-call | flops 2875000064 | bytes 100000 | tf_op jit(solution)/shard_map/source_rows/pallas_call | solution.py:462
  18.8 2.0 %collective-permute-start.5 = (f32[16,3200]{1,0:T(8,128)S(1)}, f32[16,3200]{1,0:T(8,128)S(1)}, u32[]{:S(2)}, u32[]{:S(2)}) collective-permute-start(f32[16,3200]{1,0:T(8,128)S(1)} %collective-permute-done.3.refs_4_), channel_id=1, source_target_pairs={{0,4},{1,5},{2,6},{3,7},{4,0},{5,1},{6,2},{7,3},{8,12},{9,13},{10,... | collective-permute-start | bytes 614408 | tf_op jit(solution)/shard_map/ppermute | solution.py:414
  21.0 3.8 %collective-permute-start.6 = (f32[16,3200]{1,0:T(8,128)S(1)}, f32[16,3200]{1,0:T(8,128)S(1)}, u32[]{:S(2)}, u32[]{:S(2)}) collective-permute-start(f32[16,3200]{1,0:T(8,128)S(1)} %collective-permute-done.4.refs_5_), channel_id=1, source_target_pairs={{0,4},{1,5},{2,6},{3,7},{4,0},{5,1},{6,2},{7,3},{8,12},{9,13},{10,... | collective-permute-start | bytes 614408 | tf_op jit(solution)/shard_map/ppermute | solution.py:414
  24.8 2.6 %source_rows.3 = (bf16[1216,384]{1,0:T(8,128)(2,1)S(1)}, bf16[1216,384]{1,0:T(8,128)(2,1)S(1)}) custom-call(s32[3]{0:T(128)S(1)} %pad_add_fusion.me, f32[16,3200]{1,0:T(8,128)S(1)} %collective-permute-done.9.refs_0_, f32[16,3200]{1,0:T(8,128)S(1)} %collective-permute-done.10.refs_1_, f32[352,128]{1,0:T(8,128)S(1)} %collective-permute-done.7.refs_2_.refs_9_), custom_call_target="tpu_custom_call" | custom-call | flops 2875000064 | bytes 100000 | tf_op jit(solution)/shard_map/source_rows/pallas_call | solution.py:462
  27.4 1.6 %collective-permute-done.6.refs_7_ = f32[16,3200]{1,0:T(8,128)S(1)} collective-permute-done((f32[16,3200]{1,0:T(8,128)S(1)}, f32[16,3200]{1,0:T(8,128)S(1)}, u32[]{:S(2)}, u32[]{:S(2)}) %collective-permute-start.6) | collective-permute-done | bytes 204832 | tf_op jit(solution)/shard_map/ppermute | solution.py:414
  29.0 15.2 %weight_terms.1 = (f32[8,38,8,128]{3,2,1,0:T(8,128)}, f32[8,38,8,128]{3,2,1,0:T(8,128)}, bf16[640,384]{1,0:T(8,128)(2,1)S(1)}, bf16[640,384]{1,0:T(8,128)(2,1)S(...) custom-call(s32[3]{0:T(128)S(1)} %pad_add_fusion.me, ...), custom_call_target="tpu_custom_call" | custom-call | flops 16099999744 | bytes 100000 | tf_op jit(solution)/shard_map/weight_terms/pallas_call | solution.py:491
  44.3 1.5 %back_zero.1.d0 = f32[640,384]{1,0:T(8,128)S(1)} custom-call(f32[640,640]{1,0:T(8,128)S(1)} %copy-done, bf16[640,384]{1,0:T(8,128)(2,1)S(1)} %get-tuple-element.35.uh, bf16[640,384]{1,0:T(8,128)(2,1)S(1)} %get-tuple-element.36.ul), custom_call_target="tpu_custom_call" | custom-call | flops 3449999872 | bytes 100000 | tf_op jit(solution)/shard_map/back_zero/pallas_call | solution.py:514
  45.8 1.6 %collective-permute-done.11 = f32[8,38,8,128]{3,2,1,0:T(8,128)S(1)} collective-permute-done((f32[8,38,8,128]{3,2,1,0:T(8,128)}, f32[8,38,8,128]{3,2,1,0:T(8,128)S(1)}, u32[]{:S(2)}, u32[]{:S(2)}) %collective-permute-start.11) | collective-permute-done | bytes 1245216 | tf_op jit(solution)/shard_map/ppermute | solution.py:418
  48.7 2.0 %back_two.1.d2 = f32[768,384]{1,0:T(8,128)S(1)} custom-call(f32[384,384]{1,0:T(8,128)S(1)} %copy-done.3, f32[384,384]{1,0:T(8,128)S(1)} %copy-done.4, bf16[768,384]{1,0:T(8,128)(2,1)S(1)} %get-tuple-element.39.uh, bf16[768,384]{1,0:T(8,128)(2,1)S(1)} %get-tuple-element.40.ul), custom_call_target="tpu_custom_call" | custom-call | flops 3449999872 | bytes 100000 | tf_op jit(solution)/shard_map/back_two/pallas_call | solution.py:520
  50.7 3.5 %back_one.1.d1 = f32[1024,384]{1,0:T(8,128)S(1)} custom-call(f32[512,512]{1,0:T(8,128)S(1)} %copy-done.1, f32[512,512]{1,0:T(8,128)S(1)} %copy-done.2, bf16[1024,384]{1,0:T(8,128)(2,1)S(1)} %get-tuple-element.37.uh, bf16[1024,384]{1,0:T(8,128)(2,1)S(1)} %get-tuple-element.38.ul), custom_call_target="tpu_custom_call" | custom-call | flops 4600000000 | bytes 100000 | tf_op jit(solution)/shard_map/back_one/pallas_call | solution.py:517
  54.2 3.7 %collective-permute-done.12 = f32[4,38,8,128]{3,2,1,0:T(8,128)S(1)} collective-permute-done((f32[4,38,8,128]{3,2,1,0:T(8,128)S(1)}, f32[4,38,8,128]{3,2,1,0:T(8,128)S(1)}, u32[]{:S(2)}, u32[]{:S(2)}) %collective-permute-start.12) | collective-permute-done | bytes 622624 | tf_op jit(solution)/shard_map/ppermute | solution.py:414
  57.9 2.1 %collective-permute-start.13 = (f32[2,38,8,128]{3,2,1,0:T(8,128)S(1)}, f32[2,38,8,128]{3,2,1,0:T(8,128)S(1)}, u32[]{:S(2)}, u32[]{:S(2)}) collective-permute-start(f32[2,38,8,128]{3,2,1,0:T(8,128)S(1)} %get-tuple-element.41), channel_id=1, source_target_pairs={{0,4},{1,5},{2,6},{3,7},{4,0},{5,1},{6,2},{7,3},{8,12},{9,13},{10,... | collective-permute-start | bytes 933896 | tf_op jit(solution)/shard_map/ppermute | solution.py:414
  60.0 4.4 %source_sums.1 = f32[2,16,3200]{2,1,0:T(8,128)S(1)} custom-call(s32[3]{0:T(128)S(1)} %pad_add_fusion.me, f32[352,128]{1,0:T(8,128)S(1)} %prepare.1.refs_2_.refs_8_.pack, f32[640,384]{1,0:T(8,128)S(1)} %back_zero.1.d0, f32[1024,384]{1,0:T(8,128)S(1)} %back_one.1.d1, f32[768,384]{1,0:T(8,128)S(1)} %back_two.1.d2), custom_call_target="tpu_custom_call" | custom-call | flops 5750000128 | bytes 100000 | tf_op jit(solution)/shard_map/source_sums/pallas_call | solution.py:532
  64.9 3.4 %collective-permute-start.15 = (f32[1,38,8,128]{3,2,1,0:T(8,128)S(1)}, f32[1,38,8,128]{3,2,1,0:T(8,128)S(1)}, u32[]{:S(2)}, u32[]{:S(2)}) collective-permute-start(f32[1,38,8,128]{3,2,1,0:T(8,128)S(1)} %slice_add_fusion.6), channel_id=1, source_target_pairs={{0,12},{1,13},{2,14},{3,15},{4,8},{5,9},{6,10},{7,11},{8,4},{9,5},... | collective-permute-start | bytes 466952 | tf_op jit(solution)/shard_map/ppermute | solution.py:414
  68.8 3.3 %collective-permute-done.15 = f32[1,38,8,128]{3,2,1,0:T(8,128)S(1)} collective-permute-done((f32[1,38,8,128]{3,2,1,0:T(8,128)S(1)}, f32[1,38,8,128]{3,2,1,0:T(8,128)S(1)}, u32[]{:S(2)}, u32[]{:S(2)}) %collective-permute-start.15) | collective-permute-done | bytes 155680 | tf_op jit(solution)/shard_map/ppermute | solution.py:414
  72.8 4.7 %collective-permute-done.16.refs_1_ = f32[38,8,128]{2,1,0:T(8,128)S(1)} collective-permute-done((f32[38,8,128]{2,1,0:T(8,128)S(1)}, f32[38,8,128]{2,1,0:T(8,128)S(1)}, u32[]{:S(2)}, u32[]{:S(2)}) %collective-permute-start.16) | collective-permute-done | bytes 155680 | tf_op jit(solution)/shard_map/ppermute | solution.py:414
  77.5 0.7 slice_add_fusion.4
  78.8 1.4 %unpack.1 = (f32[80,640]{1,0:T(8,128)}, f32[64,512]{1,0:T(8,128)}, f32[64,512]{1,0:T(8,128)}, f32[48,384]{1,0:T(8,128)}, f32[48,384]{1,0:T(8,128)}) custom-call(s32[3]{0:T(128)S(1)} %pad_add_fusion.me, f32[38,8,128]{2,1,0:T(8,128)S(1)} %fusion.1.refs_0_, f32[38,8,128]{2,1,0:T(8,128)S(1)} %collective-permute-done.16.refs_1_, ...), custom_call_target="tpu_custom_call" | custom-call | flops 2300000000 | bytes 100000 | tf_op jit(solution)/shard_map/unpack/pallas_call | solution.py:555
  (52 shorter events, 7.6 us)
Async XLA Ops:
  0.6 11.9 %collective-permute-start.9 = (f32[16,3200]{1,0:T(8,128)}, f32[16,3200]{1,0:T(8,128)S(1)}, u32[]{:S(2)}, u32[]{:S(2)}) collective-permute-start(f32[16,3200]{1,0:T(8,128)} %bitcast.8), channel_id=1, source_target_pairs={{0,2},{1,3},{2,0},{3,1},{4,6},{5,7},{6,4},{7,5},{8,10},{9,11},{10,... | collective-permute-start | bytes 614408 | tf_op jit(solution)/shard_map/ppermute | solution.py:414
  3.6 10.5 %collective-permute-start.8 = (f32[16,3200]{1,0:T(8,128)}, f32[16,3200]{1,0:T(8,128)S(1)}, u32[]{:S(2)}, u32[]{:S(2)}) collective-permute-start(f32[16,3200]{1,0:T(8,128)} %bitcast.9), channel_id=1, source_target_pairs={{0,1},{1,0},{2,3},{3,2},{4,5},{5,4},{6,7},{7,6},{8,9},{9,8},{10,11... | collective-permute-start | bytes 614408 | tf_op jit(solution)/shard_map/ppermute | solution.py:414
  5.2 10.0 %collective-permute-start.3 = (f32[16,3200]{1,0:T(8,128)}, f32[16,3200]{1,0:T(8,128)S(1)}, u32[]{:S(2)}, u32[]{:S(2)}) collective-permute-start(f32[16,3200]{1,0:T(8,128)} %bitcast.11), channel_id=1, source_target_pairs={{0,12},{1,13},{2,14},{3,15},{4,8},{5,9},{6,10},{7,11},{8,4},{9,5},... | collective-permute-start | bytes 614408 | tf_op jit(solution)/shard_map/ppermute | solution.py:414
  8.8 18.6 %collective-permute-start.1 = (f32[16,3200]{1,0:T(8,128)}, f32[16,3200]{1,0:T(8,128)S(1)}, u32[]{:S(2)}, u32[]{:S(2)}) collective-permute-start(f32[16,3200]{1,0:T(8,128)} %bitcast.12), channel_id=1, source_target_pairs={{0,4},{1,5},{2,6},{3,7},{4,0},{5,1},{6,2},{7,3},{8,12},{9,13},{10,... | collective-permute-start | bytes 614408 | tf_op jit(solution)/shard_map/ppermute | solution.py:414
  8.8 12.0 %collective-permute-start = (f32[16,3200]{1,0:T(8,128)}, f32[16,3200]{1,0:T(8,128)S(1)}, u32[]{:S(2)}, u32[]{:S(2)}) collective-permute-start(f32[16,3200]{1,0:T(8,128)} %bitcast.13), channel_id=1, source_target_pairs={{0,2},{1,3},{2,0},{3,1},{4,6},{5,7},{6,4},{7,5},{8,10},{9,11},{10,... | collective-permute-start | bytes 614408 | tf_op jit(solution)/shard_map/ppermute | solution.py:414
  12.3 3.4 %copy-start.5 = (f32[1,16,3200]{2,1,0:T(8,128)S(1)}, f32[1,16,3200]{2,1,0:T(8,128)}, u32[]{:S(2)}) copy-start(f32[1,16,3200]{2,1,0:T(8,128)} %param.11) | copy-start | bytes 614404
  12.6 6.2 %collective-permute-start.7 = (f32[352,128]{1,0:T(8,128)S(1)}, f32[352,128]{1,0:T(8,128)S(1)}, u32[]{:S(2)}, u32[]{:S(2)}) collective-permute-start(f32[352,128]{1,0:T(8,128)S(1)} %prepare.1.refs_2_.refs_8_.pack), channel_id=1, source_target_pairs={{0,2},{1,3},{2,0},{3,1},{4,6},{5,7},{6,4},{7,5},{8,10},{9,11},{10,... | collective-permute-start | bytes 540680 | tf_op jit(solution)/shard_map/ppermute | solution.py:414
  14.1 10.6 %collective-permute-start.10 = (f32[16,3200]{1,0:T(8,128)S(1)}, f32[16,3200]{1,0:T(8,128)S(1)}, u32[]{:S(2)}, u32[]{:S(2)}) collective-permute-start(f32[16,3200]{1,0:T(8,128)S(1)} %collective-permute-done.9.refs_0_), channel_id=1, source_target_pairs={{0,1},{1,0},{2,3},{3,2},{4,5},{5,4},{6,7},{7,6},{8,9},{9,8},{10,11... | collective-permute-start | bytes 614408 | tf_op jit(solution)/shard_map/ppermute | solution.py:414
  15.2 5.8 %collective-permute-start.4 = (f32[16,3200]{1,0:T(8,128)S(1)}, f32[16,3200]{1,0:T(8,128)S(1)}, u32[]{:S(2)}, u32[]{:S(2)}) collective-permute-start(f32[16,3200]{1,0:T(8,128)S(1)} %collective-permute-done.3.refs_4_), channel_id=1, source_target_pairs={{0,2},{1,3},{2,0},{3,1},{4,6},{5,7},{6,4},{7,5},{8,10},{9,11},{10,... | collective-permute-start | bytes 614408 | tf_op jit(solution)/shard_map/ppermute | solution.py:414
  18.3 10.7 %copy-start.6 = (f32[1,16,3200]{2,1,0:T(8,128)S(1)}, f32[1,16,3200]{2,1,0:T(8,128)}, u32[]{:S(2)}) copy-start(f32[1,16,3200]{2,1,0:T(8,128)} %param.12) | copy-start | bytes 614404
  18.8 8.6 %collective-permute-start.5 = (f32[16,3200]{1,0:T(8,128)S(1)}, f32[16,3200]{1,0:T(8,128)S(1)}, u32[]{:S(2)}, u32[]{:S(2)}) collective-permute-start(f32[16,3200]{1,0:T(8,128)S(1)} %collective-permute-done.3.refs_4_), channel_id=1, source_target_pairs={{0,4},{1,5},{2,6},{3,7},{4,0},{5,1},{6,2},{7,3},{8,12},{9,13},{10,... | collective-permute-start | bytes 614408 | tf_op jit(solution)/shard_map/ppermute | solution.py:414
  20.8 6.6 %collective-permute-start.2 = (f32[16,3200]{1,0:T(8,128)S(1)}, f32[16,3200]{1,0:T(8,128)S(1)}, u32[]{:S(2)}, u32[]{:S(2)}) collective-permute-start(f32[16,3200]{1,0:T(8,128)S(1)} %collective-permute-done.refs_1_), channel_id=1, source_target_pairs={{0,4},{1,5},{2,6},{3,7},{4,0},{5,1},{6,2},{7,3},{8,12},{9,13},{10,... | collective-permute-start | bytes 614408 | tf_op jit(solution)/shard_map/ppermute | solution.py:414
  21.0 8.0 %collective-permute-start.6 = (f32[16,3200]{1,0:T(8,128)S(1)}, f32[16,3200]{1,0:T(8,128)S(1)}, u32[]{:S(2)}, u32[]{:S(2)}) collective-permute-start(f32[16,3200]{1,0:T(8,128)S(1)} %collective-permute-done.4.refs_5_), channel_id=1, source_target_pairs={{0,4},{1,5},{2,6},{3,7},{4,0},{5,1},{6,2},{7,3},{8,12},{9,13},{10,... | collective-permute-start | bytes 614408 | tf_op jit(solution)/shard_map/ppermute | solution.py:414
  29.0 15.3 %copy-start = (f32[640,640]{1,0:T(8,128)S(1)}, f32[640,640]{1,0:T(8,128)}, u32[]{:S(2)}) copy-start(f32[640,640]{1,0:T(8,128)} %w.1) | copy-start | bytes 4915204
  44.2 3.2 %collective-permute-start.11 = (f32[8,38,8,128]{3,2,1,0:T(8,128)}, f32[8,38,8,128]{3,2,1,0:T(8,128)S(1)}, u32[]{:S(2)}, u32[]{:S(2)}) collective-permute-start(f32[8,38,8,128]{3,2,1,0:T(8,128)} %get-tuple-element.34), channel_id=1, source_target_pairs={{0,16},{1,17},{2,18},{3,19},{4,20},{5,21},{6,22},{7,23},{8,24},{9,... | collective-permute-start | bytes 3735560 | tf_op jit(solution)/shard_map/ppermute | solution.py:418
  44.3 3.1 %copy-start.10 = (f32[8,38,8,128]{3,2,1,0:T(8,128)S(1)}, f32[8,38,8,128]{3,2,1,0:T(8,128)}, u32[]{:S(2)}) copy-start(f32[8,38,8,128]{3,2,1,0:T(8,128)} %get-tuple-element.33) | copy-start | bytes 3735556
  47.6 10.3 %collective-permute-start.12 = (f32[4,38,8,128]{3,2,1,0:T(8,128)S(1)}, f32[4,38,8,128]{3,2,1,0:T(8,128)S(1)}, u32[]{:S(2)}, u32[]{:S(2)}) collective-permute-start(f32[4,38,8,128]{3,2,1,0:T(8,128)S(1)} %get-tuple-element.53), channel_id=1, source_target_pairs={{0,1},{1,0},{2,3},{3,2},{4,5},{5,4},{6,7},{7,6},{8,9},{9,8},{10,11... | collective-permute-start | bytes 1867784 | tf_op jit(solution)/shard_map/ppermute | solution.py:414
  48.7 2.0 %copy-start.2 = (f32[512,512]{1,0:T(8,128)S(1)}, f32[512,512]{1,0:T(8,128)}, u32[]{:S(2)}) copy-start(f32[512,512]{1,0:T(8,128)} %im.2) | copy-start | bytes 3145732
  57.9 7.0 %collective-permute-start.13 = (f32[2,38,8,128]{3,2,1,0:T(8,128)S(1)}, f32[2,38,8,128]{3,2,1,0:T(8,128)S(1)}, u32[]{:S(2)}, u32[]{:S(2)}) collective-permute-start(f32[2,38,8,128]{3,2,1,0:T(8,128)S(1)} %get-tuple-element.41), channel_id=1, source_target_pairs={{0,4},{1,5},{2,6},{3,7},{4,0},{5,1},{6,2},{7,3},{8,12},{9,13},{10,... | collective-permute-start | bytes 933896 | tf_op jit(solution)/shard_map/ppermute | solution.py:414
  64.9 7.2 %collective-permute-start.15 = (f32[1,38,8,128]{3,2,1,0:T(8,128)S(1)}, f32[1,38,8,128]{3,2,1,0:T(8,128)S(1)}, u32[]{:S(2)}, u32[]{:S(2)}) collective-permute-start(f32[1,38,8,128]{3,2,1,0:T(8,128)S(1)} %slice_add_fusion.6), channel_id=1, source_target_pairs={{0,12},{1,13},{2,14},{3,15},{4,8},{5,9},{6,10},{7,11},{8,4},{9,5},... | collective-permute-start | bytes 466952 | tf_op jit(solution)/shard_map/ppermute | solution.py:414
  68.3 9.2 %collective-permute-start.14 = (f32[1,16,3200]{2,1,0:T(8,128)S(1)}, f32[1,16,3200]{2,1,0:T(8,128)S(1)}, u32[]{:S(2)}, u32[]{:S(2)}) collective-permute-start(f32[1,16,3200]{2,1,0:T(8,128)S(1)} %slice.53), channel_id=1, source_target_pairs={{0,1},{1,0},{2,3},{3,2},{4,5},{5,4},{6,7},{7,6},{8,9},{9,8},{10,11... | collective-permute-start | bytes 614408 | tf_op jit(solution)/shard_map/ppermute | solution.py:414
  72.2 5.3 %collective-permute-start.16 = (f32[38,8,128]{2,1,0:T(8,128)S(1)}, f32[38,8,128]{2,1,0:T(8,128)S(1)}, u32[]{:S(2)}, u32[]{:S(2)}) collective-permute-start(f32[38,8,128]{2,1,0:T(8,128)S(1)} %fusion.1.refs_0_), channel_id=1, source_target_pairs={{0,1},{1,0},{2,3},{3,2},{4,5},{5,4},{6,7},{7,6},{8,9},{9,8},{10,11... | collective-permute-start | bytes 466952 | tf_op jit(solution)/shard_map/ppermute | solution.py:414
  72.8 5.4 %collective-permute-start.17 = (f32[38,8,128]{2,1,0:T(8,128)S(1)}, f32[38,8,128]{2,1,0:T(8,128)S(1)}, u32[]{:S(2)}, u32[]{:S(2)}) collective-permute-start(f32[38,8,128]{2,1,0:T(8,128)S(1)} %fusion.1.refs_0_), channel_id=1, source_target_pairs={{0,16},{1,17},{2,18},{3,19},{4,20},{5,21},{6,22},{7,23},{8,24},{9,... | collective-permute-start | bytes 466952 | tf_op jit(solution)/shard_map/ppermute | solution.py:418
  77.5 1.4 %collective-permute-start.18 = (f32[38,8,128]{2,1,0:T(8,128)S(1)}, f32[38,8,128]{2,1,0:T(8,128)S(1)}, u32[]{:S(2)}, u32[]{:S(2)}) collective-permute-start(f32[38,8,128]{2,1,0:T(8,128)S(1)} %collective-permute-done.16.refs_1_), channel_id=1, source_target_pairs={{0,16},{1,17},{2,18},{3,19},{4,20},{5,21},{6,22},{7,23},{8,24},{9,... | collective-permute-start | bytes 466952 | tf_op jit(solution)/shard_map/ppermute | solution.py:418
  (6 other events, 6.6 us)
